TPU v7x, 32 devices: a whole 2x2x4 slice. The times are simulated.
32 devices in a mesh: groups: 2 (over y), section: 4 (over z), tensor: 4 (over x, core).
Axes of the slice: x: 2, y: 2, z: 4, core: 2. Of those that a mesh axis runs over, the one named last changes fastest.
Arguments:
- prefill_q: bfloat16 [4096, 8192], P(('groups', 'section'), 'tensor'), parts along dimension 0, may hold values from -48 to 48
- kv_pool: bfloat16 [2, 4096, 1024], P(None, ('groups', 'section'), 'tensor'), parts along dimension 1, may hold values from -48 to 48
- decode_q: bfloat16 [64, 4, 8192], P(('groups', 'section'), None, 'tensor'), parts along dimension 0, may hold values from -48 to 48
- decode_kv: bfloat16 [2, 64, 4, 1024], P(None, ('groups', 'section'), None, 'tensor'), parts along dimension 1, may hold values from -48 to 48
- wo_weight: bfloat16 [8192, 8192], P('tensor', 'section'), may hold values from -0.0625 to 0.0625
- page_pair: int32 [8, 32], P('groups'), parts along dimension 0, may hold values from 0 to 3, never falling along the last dimension, each value on 1 to 16 neighbouring positions
- slot_owner: int32 [32, 1], P('groups'), parts along dimension 0, may hold values from 0 to 3, as said below
Outputs:
- prefill_ctx: bfloat16 [4096, 8192], P(('groups', 'section'), 'tensor'), parts along dimension 0
- decode_out: bfloat16 [64, 4, 8192], P('groups', None, 'section'), parts along dimension 0
There are 2 independent parts, one for each index of `groups`. A program takes and returns all parts, laid end to end along the dimension named above; an argument that names none is the same for every part. Nothing has to cross between parts.
Inputs may be any that keep to these rules, and one draw needn't show every extreme that they name: `page_pair`: in each row, pair numbers never fall, every pair has 1 to 16 pages, and some pair has exactly 16. `slot_owner`: every section index decodes at least one pair and at most 8; some index decodes exactly 8. Of the 4 pairs prefilled on one section index (pairs s * 4 to s * 4 + 3), at most 2 go to one decoding index, and some section index gives exactly 2 to one.
All inputs are finite; a program needn't handle non-finite values.
Results may differ from a plain program's by a relative error of at most 0.012.
Values may be sent and summed in bfloat16 or wider, within the bound.
No kernel may reach another device: no remote copies, remote signals or barrier semaphores. Data moves between devices by JAX's collectives and lax.ppermute only.
A program may use at most 128 MiB of HBM per device.

v0:
```python
import jax
import jax.numpy as jnp
from jax import lax
from jax.sharding import PartitionSpec as P

HEADS = 64
KV_HEADS = 8
HEAD_DIM = 128
PAGE = 16
PAGES_DEV = 32
PAIRS_DEV = 4
STEPS = 4
DSLOT = 8
TOK_DEV = 512


def pair_tables(page_pair, slot_owner, section_count):
    page_ids = jnp.arange(section_count * PAGES_DEV, dtype=jnp.int32)
    page_owner_pair = page_ids // PAGES_DEV * PAIRS_DEV + page_pair.reshape(-1)
    token_pair = jnp.repeat(page_owner_pair, PAGE)
    pair_count = slot_owner.shape[0]
    owner_device = slot_owner[:, 0]
    pair_ids = jnp.arange(pair_count, dtype=jnp.int32)
    same_owner = (owner_device[:, None] == owner_device[None, :]) & (
        pair_ids[None, :] < pair_ids[:, None]
    )
    slot_rank = jnp.sum(same_owner.astype(jnp.int32), axis=1)
    slot_pair = (
        jnp.full((section_count * DSLOT,), -1, jnp.int32)
        .at[owner_device * DSLOT + slot_rank]
        .set(pair_ids)
    )
    return (token_pair, slot_pair)


def new_token_terms(queries, new_keys):
    step_ids = jnp.arange(STEPS)
    new_allowed = (step_ids[None, :] <= step_ids[:, None]).reshape(1, STEPS, 1, 1, STEPS)
    new_scores = jnp.einsum(
        "ntkgh,nukh->ntkgu", queries, new_keys, preferred_element_type=jnp.float32
    ) * HEAD_DIM ** (-0.5)
    return (new_scores, new_allowed)


def per_device(prefill_q, kv_pool, decode_q, decode_kv, wo_weight, page_pair, slot_owner):
    section_count = lax.axis_size("section")
    section_index = lax.axis_index("section")
    token_pair, slot_pair = pair_tables(page_pair, slot_owner, section_count)
    kv_local = kv_pool.shape[2] // HEAD_DIM
    group_size = HEADS // KV_HEADS
    local_pair = lax.dynamic_slice_in_dim(token_pair, section_index * TOK_DEV, TOK_DEV)
    cache_keys = kv_pool[0].reshape(TOK_DEV, kv_local, HEAD_DIM)
    cache_values = kv_pool[1].reshape(TOK_DEV, kv_local, HEAD_DIM)
    queries = prefill_q.reshape(TOK_DEV, kv_local, group_size, HEAD_DIM)
    positions = jnp.arange(TOK_DEV)
    allowed = (local_pair[:, None] == local_pair[None, :]) & (
        positions[None, :] <= positions[:, None]
    )
    scores = jnp.einsum(
        "tkgh,skh->kgts", queries, cache_keys, preferred_element_type=jnp.float32
    ) * HEAD_DIM ** (-0.5)
    row_max = jnp.max(jnp.where(allowed, scores, -jnp.inf), axis=-1, keepdims=True)
    weights = jnp.where(allowed, jnp.exp(scores - row_max), 0.0)
    row_total = jnp.sum(weights, axis=-1)
    mixed_sum = jnp.einsum(
        "kgts,skh->tkgh",
        weights.astype(jnp.bfloat16),
        cache_values,
        preferred_element_type=jnp.float32,
    )
    prefill_ctx = (mixed_sum / jnp.transpose(row_total, (2, 0, 1))[..., None]).astype(jnp.bfloat16)
    prefill_ctx = prefill_ctx.reshape(TOK_DEV, kv_local * group_size * HEAD_DIM)
    own_pairs = lax.dynamic_slice_in_dim(slot_pair, section_index * DSLOT, DSLOT)
    own_queries = decode_q.reshape(DSLOT, STEPS, kv_local, group_size, HEAD_DIM)
    new_keys = decode_kv[0].reshape(DSLOT, STEPS, kv_local, HEAD_DIM)
    new_values = decode_kv[1].reshape(DSLOT, STEPS, kv_local, HEAD_DIM)
    portion = lax.all_gather(kv_pool, "section", axis=1, tiled=True)
    run_max = jnp.full((DSLOT, STEPS, kv_local, group_size), -1e30, jnp.float32)
    part_keys = portion[0].reshape(-1, kv_local, HEAD_DIM)
    part_values = portion[1].reshape(-1, kv_local, HEAD_DIM)
    part_scores = jnp.einsum(
        "ntkgh,skh->ntkgs", own_queries, part_keys, preferred_element_type=jnp.float32
    ) * HEAD_DIM ** (-0.5)
    part_allowed = own_pairs[:, None, None, None, None] == token_pair[None, None, None, None, :]
    next_max = jnp.maximum(
        run_max, jnp.max(jnp.where(part_allowed, part_scores, -jnp.inf), axis=-1)
    )
    part_w = jnp.where(part_allowed, jnp.exp(part_scores - next_max[..., None]), 0.0)
    next_sum = jnp.einsum(
        "ntkgs,skh->ntkgh",
        part_w.astype(jnp.bfloat16),
        part_values,
        preferred_element_type=jnp.float32,
    )
    run_total = jnp.sum(part_w, axis=-1)
    new_scores, new_allowed = new_token_terms(own_queries, new_keys)
    final_max = jnp.maximum(
        next_max, jnp.max(jnp.where(new_allowed, new_scores, -jnp.inf), axis=-1)
    )
    rescale = jnp.exp(next_max - final_max)
    new_w = jnp.where(new_allowed, jnp.exp(new_scores - final_max[..., None]), 0.0)
    final_total = run_total * rescale + jnp.sum(new_w, axis=-1)
    final_sum = next_sum * rescale[..., None] + jnp.einsum(
        "ntkgu,nukh->ntkgh",
        new_w.astype(jnp.bfloat16),
        new_values,
        preferred_element_type=jnp.float32,
    )
    contexts = final_sum / final_total[..., None]
    contexts = jnp.where((own_pairs >= 0)[:, None, None, None, None], contexts, 0.0).astype(
        jnp.bfloat16
    )
    contexts = contexts.reshape(DSLOT, STEPS, kv_local * group_size * HEAD_DIM)
    portion = lax.all_gather(contexts, "section", axis=0, tiled=True)
    flat_rows = portion.reshape(-1, portion.shape[2])
    product = jnp.dot(flat_rows, wo_weight, preferred_element_type=jnp.float32)
    partial_out = product.reshape(portion.shape[0], STEPS, wo_weight.shape[1])
    decode_out = lax.psum(partial_out.astype(jnp.bfloat16), "tensor")
    return (prefill_ctx, decode_out)


def solution(mesh):
    placed = (
        P(("groups", "section"), "tensor"),
        P(None, ("groups", "section"), "tensor"),
        P(("groups", "section"), None, "tensor"),
        P(None, ("groups", "section"), None, "tensor"),
        P("tensor", "section"),
        P("groups", None),
        P("groups", None),
    )
    return jax.shard_map(
        per_device,
        mesh=mesh,
        in_specs=placed,
        out_specs=(P(("groups", "section"), "tensor"), P("groups", None, "section")),
        check_vma=False,
    )
```

profile of v0, /device:TPU:0, one launch (start us, length us, event | category | flops | bytes accessed | tf_op | source)
XLA Modules:
  0.0 126.6 jit_solution(15922269844946600227)
XLA Ops:
  7.2 2.1 %copy.88 = bf16[2,512,256]{1,2,0:T(8,128)(2,1)} copy(bf16[2,512,256]{2,1,0:T(8,128)(2,1)} %param.8) | data formatting | bytes 1048576 | tf_op args[1]
  9.4 0.9 convert_reduce_fusion
  10.3 0.7 fusion.52
  11.0 0.8 reshape.101
  11.7 1.0 slice.24
  12.7 0.1 broadcast_in_dim.88
  12.8 0.1 reshape.102
  12.9 1.0 reshape.105
  13.9 0.7 slice.23
  14.6 2.2 %copy.124 = bf16[64,8,16,128]{3,2,1,0:T(8,128)(2,1)S(1)} copy(bf16[64,8,16,128]{3,1,2,0:T(8,128)(2,1)} %bitcast.110) | data formatting | bytes 4194304
  16.8 0.1 copy.91
  17.0 0.1 dynamic_slice.6
  17.1 0.6 scatter_custom_fusion
  17.7 0.1 broadcast_compare_fusion.1
  17.8 0.2 fusion.39
  18.0 0.7 select_reduce_fusion
  18.7 0.1 broadcast_compare_fusion
  18.8 8.2 %fusion.23 = f32[2,512,512,8]{2,1,3,0:T(8,128)} fusion(bf16[512,2,128,1]{0,2,3,1:T(8,128)(2,1)S(1)} %bitcast.112, bf16[512,2,8,128]{3,2,1,0:T(8,128)(2,1)S(1)} %bitcast.109), kind=kOutput, calls=%fused_computation.25 | convolution fusion | flops 1073741824 | bytes 19136512 | tf_op jit(solution)/shard_map/tkgh,skh->kgts/dot_general | solution.py:59
  27.0 16.2 %fusion.60 = (f32[2,8,512]{2,1,0:T(8,128)S(1)}, bf16[2,8,512,512]{2,3,1,0:T(8,128)(2,1)}) fusion(f32[2,512,512,8]{2,1,3,0:T(8,128)} %fusion.23, pred[512,512]{0,1:T(8,128)(4,1)S(1)} %fusion.39), kind=kOutput, calls=%fused_computation.77 | output fusion | flops 29360640 | bytes 25460736 | tf_op jit(solution)/shard_map/sub | solution.py:63
  43.3 15.4 %all-gather.2.cloned.1.call-done = bf16[2,2048,256]{1,2,0:T(8,128)(2,1)} async-done(((bf16[2,512,256]{1,2,0:T(8,128)(2,1)}), bf16[2,2048,256]{1,2,0:T(8,128)(2,1)}) %all-gather.2.cloned.1.call-update) | async-done | bytes 2097168 | tf_op jit(solution)/shard_map/all_gather | solution.py:77
  58.7 1.7 %fusion.59 = (bf16[1,2048,256]{1,2,0:T(8,128)(2,1)S(1)}, bf16[1,2048,256]{1,2,0:T(8,128)(2,1)S(1)}) fusion(bf16[2,2048,256]{1,2,0:T(8,128)(2,1)} %all-gather.2.cloned.1.call-done), kind=kLoop, calls=%fused_computation.76 | loop fusion | bytes 4194304 | tf_op jit(solution)/shard_map/slice | solution.py:79
  60.4 0.9 fusion.12
  61.3 1.1 fusion.16
  62.4 0.2 fusion.44
  62.7 0.9 fusion.34
  63.5 0.2 fusion.37
  63.9 16.0 %all_gather.7 = bf16[32,4,2048]{2,0,1:T(8,128)(2,1)S(1)} all-gather(bf16[8,4,2048]{2,0,1:T(8,128)(2,1)S(1)} %reshape.106), channel_id=1, replica_groups=mesh['groups'=2,'section'=4,'tensor'=4] {'section'}, dimensions={0}, use_global_device_ids=true | all-gather | bytes 655360 | tf_op jit(solution)/shard_map/all_gather | solution.py:114
  79.8 5.5 %fusion.18 = bf16[32,4,2048]{2,0,1:T(8,128)(2,1)} fusion(bf16[32,4,2048]{2,0,1:T(8,128)(2,1)S(1)} %all_gather.7, bf16[2048,2048]{1,0:T(8,128)(2,1)} %param.11), kind=kOutput, calls=%fused_computation.24 | convolution fusion | flops 1074003968 | bytes 9437184 | tf_op jit(solution)/shard_map/dot_general | solution.py:116
  85.3 4.7 %fusion.15 = bf16[512,2,8,128]{0,3,2,1:T(8,128)(2,1)S(1)} fusion(bf16[512,2,128,1]{0,2,3,1:T(8,128)(2,1)S(1)} %bitcast.115, bf16[2,8,512,512]{2,3,1,0:T(8,128)(2,1)} %get-tuple-element.25, f32[512,2,8]{0,2,1:T(8,128)S(1)} %bitcast.118), kind=kOutput, calls=%fused_computation.21 | convolution fusion | flops 1075838976 | bytes 10780672 | tf_op jit(solution)/shard_map/kgts,skh->tkgh/dot_general | solution.py:65
  90.0 2.4 %copy.105 = bf16[512,2048]{1,0:T(8,128)(2,1)} copy(bf16[512,2048]{0,1:T(8,128)(2,1)S(1)} %bitcast.111) | data formatting | bytes 4194304
  92.4 25.1 %all-reduce.2.cloned.1.call-done = bf16[32,4,2048]{2,0,1:T(8,128)(2,1)} async-done(((bf16[32,4,2048]{2,0,1:T(8,128)(2,1)}), bf16[32,4,2048]{2,0,1:T(8,128)(2,1)}) %all-reduce.2.cloned.1.call-update) | async-done | bytes 524304 | tf_op jit(solution)/shard_map/psum | solution.py:118
  117.5 2.2 %copy.106 = bf16[32,4,2048]{2,1,0:T(4,128)(2,1)} copy(bf16[32,4,2048]{2,0,1:T(8,128)(2,1)} %all-reduce.2.cloned.1.call-done) | data formatting | bytes 1048576
  (16 shorter events, 0.3 us)
Async XLA Ops:
  7.2 9.7 %slice-start = ((bf16[2,512,256]{2,1,0:T(8,128)(2,1)}), bf16[1,512,256]{2,1,0:T(8,128)(2,1)S(1)}, s32[]{:S(2)}) async-start(bf16[2,512,256]{2,1,0:T(8,128)(2,1)} %param.8), calls=%async_computation.2 | async-start | bytes 524288 | tf_op jit(solution)/shard_map/slice | solution.py:53
  7.2 10.8 %copy-start = (bf16[2,8,4,256]{3,2,1,0:T(4,128)(2,1)S(1)}, bf16[2,8,4,256]{3,2,1,0:T(4,128)(2,1)}, u32[]{:S(2)}) copy-start(bf16[2,8,4,256]{3,2,1,0:T(4,128)(2,1)} %param.10) | copy-start | bytes 98308
  7.2 51.5 %all-gather.2.cloned.1.call-start = ((), (), s32[]{:S(2)}) async-start(), calls=%async_computation | async-start | bytes 2621440 | tf_op jit(solution)/shard_map/all_gather | solution.py:77
  9.3 108.2 %all-reduce.2.cloned.1.call-start = ((), (), s32[]{:S(2)}) async-start(), calls=%async_computation.1 | async-start | bytes 1048576 | tf_op jit(solution)/shard_map/psum | solution.py:118
Sparse Core Ops, SparseCore 0:
  10.2 48.4 all-gather.1
  85.5 32.0 all-reduce.1
where the time goes:
time: 127 us
  waiting for transfers between devices  40.6 us (32%)
  matrix products  21.1 us (17%)
  other arithmetic  19.6 us (15%)
  blocking collectives  16 us (13%)
  local copies, waits for them, and re-layouts  15.1 us (12%)
  between operations  14.2 us (11%)
    psum x1, waiting for transfers between devices, per_device(): decode_out = lax.psum(partial_out.astype(jnp.bfloat16), 'tensor')  25.1 us
    sub x1, other arithmetic, per_device(): weights = jnp.where(allowed, jnp.exp(scores - row_max), 0.0)  16.2 us
    all_gather x1, blocking collectives, per_device(): portion = lax.all_gather(contexts, 'section', axis=0, tiled=True)  16 us
    all_gather x1, waiting for transfers between devices, per_device(): portion = lax.all_gather(kv_pool, 'section', axis=1, tiled=True)  15.4 us
    unnamed x6, local copies, waits for them, and re-layouts  8.9 us
    dot_general x1, matrix products, per_device(): jnp.einsum('tkgh,skh->kgts', queries, cache_keys, preferred_element_type=...  8.21 us
    dot_general x1, matrix products, per_device(): product = jnp.dot(flat_rows, wo_weight, preferred_element_type=jnp.float32)  5.46 us
    dot_general x1, matrix products, per_device(): jnp.einsum('kgts,skh->tkgh', weights.astype(jnp.bfloat16), cache_values,...  4.66 us
  transfers between devices with their start and end apart: 2, of which 2 were waited for; matrix products, arithmetic and copies ran while one was open for 32% of the time, Pallas kernels for 0%

commit v1 on v0

v1 whole, which is shorter than its diff:
```python
import functools

import jax
import jax.numpy as jnp
from jax import lax
from jax.experimental import pallas as pl
from jax.experimental.pallas import tpu as pltpu
from jax.sharding import PartitionSpec as P

HEAD_DIM = 128
GROUP = 8
PAGE = 16
PAIRS_DEV = 4
STEPS = 4
DSLOT = 8
TOK_DEV = 512
CAP = 2
BLOCK = 128
ROWS = PAIRS_DEV * STEPS
SCALE = HEAD_DIM ** (-0.5)
EXP2_SCALE = SCALE * 1.4426950408889634
MASKED = -1e30
VMEM_LIMIT = 48 * 1024 * 1024

SMEM_SPEC = pl.BlockSpec(memory_space=pltpu.SMEM)
VMEM_SPEC = pl.BlockSpec(memory_space=pltpu.VMEM)


def params():
    return pltpu.CompilerParams(vmem_limit_bytes=VMEM_LIMIT)


def pack_kernel(sections, where_ref, owner_ref, q_ref, kv_ref, *refs):
    outs, packed = refs[:sections], refs[sections]
    width = q_ref.shape[2]
    kv_width = kv_ref.shape[3]
    here = where_ref[0]

    def place(pair, carry):
        slot, rank = carry
        rank = jnp.where(pair % PAIRS_DEV == 0, 0, rank)
        mine = owner_ref[pair] == here

        @pl.when(mine)
        def _():
            to = (pair // PAIRS_DEV) ^ here
            packed[to, rank, :, :width] = q_ref[slot]
            packed[to, rank, :, width : width + kv_width] = kv_ref[0, slot]
            packed[to, rank, :, width + kv_width :] = kv_ref[1, slot]

        step = mine.astype(jnp.int32)
        return slot + step, rank + step

    packed[...] = jnp.zeros_like(packed)
    lax.fori_loop(0, owner_ref.shape[0], place, (jnp.int32(0), jnp.int32(0)))
    for k in range(sections):
        outs[k][...] = packed[k]


def pack(where, owner, decode_q, decode_kv, sections):
    width = decode_q.shape[2] + 2 * decode_kv.shape[3]
    block = (CAP, STEPS, width)
    return pl.pallas_call(
        functools.partial(pack_kernel, sections),
        out_shape=[jax.ShapeDtypeStruct(block, jnp.bfloat16)] * sections,
        in_specs=[SMEM_SPEC, SMEM_SPEC, VMEM_SPEC, VMEM_SPEC],
        out_specs=[VMEM_SPEC] * sections,
        scratch_shapes=[pltpu.VMEM((sections,) + block, jnp.bfloat16)],
        compiler_params=params(),
        name="pack_queries",
    )(where, owner, decode_q, decode_kv)


def prefill_kernel(heads_step, where_ref, page_ref, q_ref, k_ref, v_ref, o_ref, bias, keys, values):
    step = pl.program_id(0)
    blocks = TOK_DEV // BLOCK
    reach = 2

    @pl.when(step == 0)
    def _():
        here = where_ref[0]
        starts = pair_starts(page_ref, here)
        for i in range(blocks):
            low = max(0, i - reach) * BLOCK
            width = (i + 1) * BLOCK - low
            row = lax.broadcasted_iota(jnp.int32, (BLOCK, width), 0) + i * BLOCK
            col = lax.broadcasted_iota(jnp.int32, (BLOCK, width), 1) + low
            first = jnp.zeros((BLOCK, width), jnp.int32)
            for j in range(1, PAIRS_DEV):
                first = jnp.where(row >= starts[j], starts[j], first)
            bias[i, :, :width] = jnp.where((col <= row) & (col >= first), 0.0, MASKED)

    @pl.when(step % (GROUP // heads_step) == 0)
    def _():
        keys[...] = k_ref[0].astype(jnp.float32).T.astype(jnp.bfloat16)
        values[:, :HEAD_DIM] = v_ref[0]
        values[:, HEAD_DIM:] = jnp.ones((TOK_DEV, HEAD_DIM), jnp.bfloat16)

    for h in range(heads_step):
        cols = slice(h * HEAD_DIM, (h + 1) * HEAD_DIM)
        for i in range(blocks):
            low = max(0, i - reach) * BLOCK
            high = (i + 1) * BLOCK
            rows = slice(i * BLOCK, high)
            s = jnp.dot(q_ref[rows, cols], keys[:, low:high], preferred_element_type=jnp.float32)
            s = s + bias[i, :, : high - low]
            m = jnp.max(s, axis=1, keepdims=True)
            p = jnp.exp2((s - m) * EXP2_SCALE).astype(jnp.bfloat16)
            o = jnp.dot(p, values[low:high, :], preferred_element_type=jnp.float32)
            o_ref[rows, cols] = (o[:, :HEAD_DIM] / o[:, HEAD_DIM:]).astype(jnp.bfloat16)


def pair_starts(page_ref, here):
    starts = []
    for j in range(PAIRS_DEV):
        total = jnp.int32(0)
        for g in range(TOK_DEV // PAGE):
            total = total + (page_ref[here, g] < j).astype(jnp.int32)
        starts.append(total * PAGE)
    return starts


def prefill(where, page_pair, prefill_q, kv_pool, heads_step=2):
    heads = prefill_q.shape[1] // HEAD_DIM
    per_key = GROUP // heads_step
    return pl.pallas_call(
        functools.partial(prefill_kernel, heads_step),
        out_shape=jax.ShapeDtypeStruct(prefill_q.shape, jnp.bfloat16),
        grid=(heads // heads_step,),
        in_specs=[
            SMEM_SPEC,
            SMEM_SPEC,
            pl.BlockSpec((TOK_DEV, heads_step * HEAD_DIM), lambda h: (0, h)),
            pl.BlockSpec((1, TOK_DEV, HEAD_DIM), lambda h: (0, 0, h // per_key)),
            pl.BlockSpec((1, TOK_DEV, HEAD_DIM), lambda h: (1, 0, h // per_key)),
        ],
        out_specs=pl.BlockSpec((TOK_DEV, heads_step * HEAD_DIM), lambda h: (0, h)),
        scratch_shapes=[
            pltpu.VMEM((TOK_DEV // BLOCK, BLOCK, 3 * BLOCK), jnp.float32),
            pltpu.VMEM((HEAD_DIM, TOK_DEV), jnp.bfloat16),
            pltpu.VMEM((TOK_DEV, 2 * HEAD_DIM), jnp.bfloat16),
        ],
        compiler_params=params(),
        cost_estimate=pl.CostEstimate(
            flops=heads * TOK_DEV * TOK_DEV * HEAD_DIM * 4,
            bytes_accessed=prefill_q.size * 4 + kv_pool.size * 2,
            transcendentals=heads * TOK_DEV * TOK_DEV,
        ),
        name="prefill_attention",
    )(where, page_pair, prefill_q, kv_pool, kv_pool)


def decode_kernel(sections, where_ref, owner_ref, page_ref, kv_ref, *refs):
    got, ctx_ref, blocks, rows = refs[:sections], refs[sections], refs[sections + 1], refs[sections + 2]
    here = where_ref[0]
    kv_local = kv_ref.shape[2] // HEAD_DIM
    width = kv_local * GROUP * HEAD_DIM
    starts = pair_starts(page_ref, here) + [jnp.int32(TOK_DEV)]
    for k in range(sections):
        blocks[k] = got[k][...]
    owners = [owner_ref[here * PAIRS_DEV + j] for j in range(PAIRS_DEV)]
    for j in range(PAIRS_DEV):
        rank = jnp.int32(0)
        for i in range(j):
            rank = rank + (owners[i] == owners[j]).astype(jnp.int32)
        rows[j * STEPS : (j + 1) * STEPS, :] = blocks[owners[j] ^ here, rank].astype(jnp.float32)
    all_rows = rows[...].astype(jnp.bfloat16)

    many = GROUP * ROWS
    row = lax.broadcasted_iota(jnp.int32, (many, TOK_DEV), 0) % ROWS
    col = lax.broadcasted_iota(jnp.int32, (many, TOK_DEV), 1)
    first = jnp.full((many, TOK_DEV), starts[0], jnp.int32)
    last = jnp.full((many, TOK_DEV), starts[1], jnp.int32)
    for j in range(1, PAIRS_DEV):
        first = jnp.where(row >= j * STEPS, starts[j], first)
        last = jnp.where(row >= j * STEPS, starts[j + 1], last)
    allowed = (col >= first) & (col < last)
    new_row = lax.broadcasted_iota(jnp.int32, (many, ROWS), 0) % ROWS
    new_col = lax.broadcasted_iota(jnp.int32, (many, ROWS), 1)
    new_allowed = (new_row // STEPS == new_col // STEPS) & (new_col <= new_row)
    contract = (((1,), (1,)), ((), ()))
    for k in range(kv_local):
        q = jnp.concatenate(
            [all_rows[:, (k * GROUP + g) * HEAD_DIM : (k * GROUP + g + 1) * HEAD_DIM] for g in range(GROUP)], axis=0
        )
        cols = slice(k * HEAD_DIM, (k + 1) * HEAD_DIM)
        new_keys = all_rows[:, width + k * HEAD_DIM : width + (k + 1) * HEAD_DIM]
        at = width + (kv_local + k) * HEAD_DIM
        new_values = all_rows[:, at : at + HEAD_DIM]
        s = lax.dot_general(q, kv_ref[0, :, cols], contract, preferred_element_type=jnp.float32)
        s = jnp.where(allowed, s, MASKED)
        s_new = lax.dot_general(q, new_keys, contract, preferred_element_type=jnp.float32)
        s_new = jnp.where(new_allowed, s_new, MASKED)
        m = jnp.maximum(jnp.max(s, axis=1, keepdims=True), jnp.max(s_new, axis=1, keepdims=True))
        p = jnp.exp2((s - m) * EXP2_SCALE)
        p_new = jnp.exp2((s_new - m) * EXP2_SCALE)
        total = jnp.sum(p, axis=1, keepdims=True) + jnp.sum(p_new, axis=1, keepdims=True)
        o = jnp.dot(p.astype(jnp.bfloat16), kv_ref[1, :, cols], preferred_element_type=jnp.float32)
        o = o + jnp.dot(p_new.astype(jnp.bfloat16), new_values, preferred_element_type=jnp.float32)
        o = (o / total).astype(jnp.bfloat16)
        for g in range(GROUP):
            ctx_ref[:, (k * GROUP + g) * HEAD_DIM : (k * GROUP + g + 1) * HEAD_DIM] = o[g * ROWS : (g + 1) * ROWS]


def decode(where, owner, page_pair, kv_pool, got, sections):
    block = got[0].shape
    width = kv_pool.shape[2] * GROUP
    return pl.pallas_call(
        functools.partial(decode_kernel, sections),
        out_shape=jax.ShapeDtypeStruct((ROWS, width), jnp.bfloat16),
        in_specs=[SMEM_SPEC, SMEM_SPEC, SMEM_SPEC] + [VMEM_SPEC] * (1 + sections),
        out_specs=VMEM_SPEC,
        scratch_shapes=[
            pltpu.VMEM((sections,) + block, jnp.bfloat16),
            pltpu.VMEM((ROWS, block[2]), jnp.float32),
        ],
        compiler_params=params(),
        name="decode_attention",
    )(where, owner, page_pair, kv_pool, *got)


def project_kernel(sections, half_ref, *refs):
    ctxs, wo_ref, out_ref = refs[:sections], refs[sections], refs[sections + 1]
    del half_ref
    x = jnp.concatenate([c[...] for c in ctxs], axis=0)
    y = jnp.dot(x, wo_ref[...], preferred_element_type=jnp.float32)
    out_ref[...] = y.astype(out_ref.dtype)


def project(half, ctxs, wo, sections, dtype):
    depth, features = wo.shape
    rows = sections * ROWS
    chunk = min(256, features // 2)
    steps = features // 2 // chunk
    return pl.pallas_call(
        functools.partial(project_kernel, sections),
        out_shape=jax.ShapeDtypeStruct((rows, features // 2), dtype),
        grid_spec=pltpu.PrefetchScalarGridSpec(
            num_scalar_prefetch=1,
            grid=(steps,),
            in_specs=[pl.BlockSpec((ROWS, depth), lambda j, half: (0, 0))] * sections
            + [pl.BlockSpec((depth, chunk), lambda j, half: (0, half[0] * steps + j))],
            out_specs=pl.BlockSpec((rows, chunk), lambda j, half: (0, j)),
        ),
        compiler_params=params(),
        cost_estimate=pl.CostEstimate(
            flops=rows * depth * features, bytes_accessed=depth * features, transcendentals=0
        ),
        name="project_half",
    )(half, *ctxs, wo)


def scatter_kernel(sections, where_ref, owner_ref, mine_ref, other_ref, out_ref, table, rows):
    here, half = where_ref[0], where_ref[1]
    pairs = owner_ref.shape[0]
    slots = out_ref.shape[0]
    wide = mine_ref.shape[1]

    def clear(i, _):
        table[i] = -1
        return 0

    lax.fori_loop(0, slots, clear, 0)

    def clear_count(i, _):
        table[slots + i] = 0
        return 0

    lax.fori_loop(0, sections, clear_count, 0)

    def enter(pair, _):
        to = owner_ref[pair]
        rank = table[slots + to]
        table[to * DSLOT + rank] = pair
        table[slots + to] = rank + 1
        return 0

    lax.fori_loop(0, pairs, enter, 0)

    def halves(first, second):
        for p in range(pairs):
            rows[p, :, :wide] = first[p * STEPS : (p + 1) * STEPS, :]
            rows[p, :, wide:] = second[p * STEPS : (p + 1) * STEPS, :]

    @pl.when(half == 0)
    def _():
        halves(mine_ref, other_ref)

    @pl.when(half == 1)
    def _():
        halves(other_ref, mine_ref)

    def write(slot, _):
        pair = table[slot]

        @pl.when(pair >= 0)
        def _():
            at = ((pair // PAIRS_DEV) ^ here) * PAIRS_DEV + pair % PAIRS_DEV
            out_ref[slot] = rows[at]

        @pl.when(pair < 0)
        def _():
            out_ref[slot] = jnp.zeros(out_ref.shape[1:], out_ref.dtype)

        return 0

    lax.fori_loop(0, slots, write, 0)


def scatter(where, owner, mine, other, sections):
    slots = sections * DSLOT
    features = 2 * mine.shape[1]
    return pl.pallas_call(
        functools.partial(scatter_kernel, sections),
        out_shape=jax.ShapeDtypeStruct((slots, STEPS, features), jnp.bfloat16),
        in_specs=[SMEM_SPEC, SMEM_SPEC, VMEM_SPEC, VMEM_SPEC],
        out_specs=VMEM_SPEC,
        scratch_shapes=[
            pltpu.SMEM((slots + sections,), jnp.int32),
            pltpu.VMEM((owner.shape[0], STEPS, features), jnp.bfloat16),
        ],
        compiler_params=params(),
        name="scatter_slots",
    )(where, owner, mine, other)


def swap(x, axis, k):
    count = lax.axis_size(axis)
    return lax.ppermute(x, axis, [(i, i ^ k) for i in range(count)])


def per_device(prefill_q, kv_pool, decode_q, decode_kv, wo_weight, page_pair, slot_owner):
    sections = lax.axis_size("section")
    here = lax.axis_index("section")
    half = lax.axis_index("tensor") % 2
    where = jnp.stack([here, half]).astype(jnp.int32)
    owner = slot_owner.reshape(-1)

    packed = pack(where, owner, decode_q, decode_kv, sections)
    got = [packed[0]] + [swap(packed[k], "section", k) for k in range(1, sections)]
    prefill_ctx = prefill(where, page_pair, prefill_q, kv_pool)
    ctx = decode(where, owner, page_pair, kv_pool, got, sections)
    ctxs = [ctx] + [swap(ctx, "section", k) for k in range(1, sections)]

    away = project((1 - where[1:2]), ctxs, wo_weight, sections, jnp.bfloat16)
    came = swap(away, "tensor", 1)
    keep = project(where[1:2], ctxs, wo_weight, sections, jnp.float32)
    chip = keep + came.astype(jnp.float32)
    k = 2
    while k < lax.axis_size("tensor"):
        far = swap(chip.astype(jnp.bfloat16), "tensor", k)
        chip = chip + far.astype(jnp.float32)
        k *= 2
    mine = chip.astype(jnp.bfloat16)
    other = swap(mine, "tensor", 1)
    decode_out = scatter(where, owner, mine, other, sections)
    return (prefill_ctx, decode_out)


def solution(mesh):
    placed = (
        P(("groups", "section"), "tensor"),
        P(None, ("groups", "section"), "tensor"),
        P(("groups", "section"), None, "tensor"),
        P(None, ("groups", "section"), None, "tensor"),
        P("tensor", "section"),
        P("groups", None),
        P("groups", None),
    )
    return jax.shard_map(
        per_device,
        mesh=mesh,
        in_specs=placed,
        out_specs=(P(("groups", "section"), "tensor"), P("groups", None, "section")),
        check_vma=False,
    )
```

time: 127 us -> 55.5 us (0.44)
  waiting for transfers between devices: 40.6 us -> 12.8 us
  Pallas kernels: 0 us -> 24.8 us
  matrix products: 21.1 us -> 0 us
  other arithmetic: 19.6 us -> 0.16 us
  blocking collectives: 16 us -> 0 us
  between operations: 14.2 us -> 0.77 us
  starting transfers between devices: 0.08 us -> 11.8 us
  local copies, waits for them, and re-layouts: 15.1 us -> 4.72 us
    psum x1 -> x0, waiting for transfers between devices: 25.1 us -> none  [per_device(): decode_out = lax.psum(partial_out.astype(jnp.bfloat16), 'tensor')]
    pallas_call x0 -> x6, Pallas kernels: none -> 24.8 us  [the longest x1 12.8 us: prefill(): pl.pallas_call(functools.partial(prefill_kernel, heads_step), out_shape=j...]
    dot_general x7 -> x0, matrix products: 21.1 us -> none  [the longest x1 8.21 us: per_device(): jnp.einsum('tkgh,skh->kgts', queries, cache_keys, preferred_element_type=...]
    sub x1 -> x0, other arithmetic: 16.2 us -> none  [per_device(): weights = jnp.where(allowed, jnp.exp(scores - row_max), 0.0)]
    all_gather x1 -> x0, blocking collectives: 16 us -> none  [per_device(): portion = lax.all_gather(contexts, 'section', axis=0, tiled=True)]
    all_gather x1 -> x0, waiting for transfers between devices: 15.4 us -> none  [per_device(): portion = lax.all_gather(kv_pool, 'section', axis=1, tiled=True)]
    ppermute x0 -> x9, waiting for transfers between devices: none -> 12.8 us  [swap(): return lax.ppermute(x, axis, [(i, i ^ k) for i in range(count)])]
    ppermute x0 -> x9, starting transfers between devices: none -> 11.8 us  [swap(): return lax.ppermute(x, axis, [(i, i ^ k) for i in range(count)])]
  transfers between devices with their start and end apart: 2 -> 9, of which waited for: 2 -> 5; matrix products, arithmetic and copies ran while one was open for 32% -> 0% of each run, Pallas kernels for 0% -> 30%
where the time goes in v1:
time: 55.5 us; the launch traced here: 55.1 us
  Pallas kernels  24.8 us (45%)
  waiting for transfers between devices  12.8 us (23%)
  starting transfers between devices  11.8 us (21%)
  local copies, waits for them, and re-layouts  4.72 us (9%)
  between operations  0.77 us (1%)
    pallas_call x1, Pallas kernels, prefill(): pl.pallas_call(functools.partial(prefill_kernel, heads_step), out_shape=j...  12.8 us
    ppermute x9, waiting for transfers between devices, swap(): return lax.ppermute(x, axis, [(i, i ^ k) for i in range(count)])  12.8 us
    ppermute x9, starting transfers between devices, swap(): return lax.ppermute(x, axis, [(i, i ^ k) for i in range(count)])  11.8 us
    pallas_call x2, Pallas kernels, project(): pl.pallas_call(functools.partial(project_kernel, sections), out_shape=jax...  7.2 us
    unnamed x20, local copies, waits for them, and re-layouts  4.72 us
    pallas_call x1, Pallas kernels, scatter(): pl.pallas_call(functools.partial(scatter_kernel, sections), out_shape=jax...  2.56 us
    pallas_call x1, Pallas kernels, decode(): pl.pallas_call(functools.partial(decode_kernel, sections), out_shape=jax....  1.41 us
  transfers between devices with their start and end apart: 9, of which 5 were waited for; matrix products, arithmetic and copies ran while one was open for 0% of the time, Pallas kernels for 30%

profile of v1, /device:TPU:0, one launch (start us, length us, event | category | flops | bytes accessed | tf_op | source)
XLA Modules:
  0.0 55.1 jit_solution(3881576005157250258)
XLA Ops:
  0.6 0.1 pad_add_fusion.where_ref
  0.7 0.9 %copy-done.2 = bf16[8,4,2048]{2,1,0:T(4,128)(2,1)S(1)} copy-done((bf16[8,4,2048]{2,1,0:T(4,128)(2,1)S(1)}, bf16[8,4,2048]{2,1,0:T(4,128)(2,1)}, u32[]{:S(2)}) %copy-start.2) | copy-done | bytes 131096
  1.6 0.8 %copy-done.3 = bf16[2,8,4,256]{3,2,1,0:T(4,128)(2,1)S(1)} copy-done((bf16[2,8,4,256]{3,2,1,0:T(4,128)(2,1)S(1)}, bf16[2,8,4,256]{3,2,1,0:T(4,128)(2,1)}, u32[]{:S(2)}) %copy-start.3) | copy-done | bytes 32792
  2.4 0.7 %copy-done.4 = s32[16,1]{0,1:T(1,128)S(1)} copy-done((s32[16,1]{0,1:T(1,128)S(1)}, s32[16,1]{0,1:T(1,128)}, u32[]{:S(2)}) %copy-start.4) | copy-done | bytes 88
  3.0 0.8 %pack_queries.1 = (bf16[2,4,2560]{2,1,0:T(4,128)(2,1)S(1)}, bf16[2,4,2560]{2,1,0:T(4,128)(2,1)S(1)}, bf16[2,4,2560]{2,1,0:T(4,128)(2,1)S(1)}, bf16[2,4,2560]{2,1,0:T(4,128)(2,1)S(1)}) custom-call(s32[2]{0:T(128)S(1)} %pad_add_fusion.where_ref, s32[16]{0:T(128)S(1)} %bitcast.3, bf16[8,4,2048]{2,1,0:T(4,128)(2,1)S(1)} %copy-done.2, ...), custom_call_target="tpu_custom_call" | custom-call | tf_op jit(solution)/shard_map/pack_queries/pallas_call | solution.py:63
  3.9 3.1 %collective-permute-start = (bf16[2,4,2560]{2,1,0:T(4,128)(2,1)S(1)}, bf16[2,4,2560]{2,1,0:T(4,128)(2,1)S(1)}, u32[]{:S(2)}, u32[]{:S(2)}) collective-permute-start(bf16[2,4,2560]{2,1,0:T(4,128)(2,1)S(1)} %get-tuple-element.7), channel_id=1, source_target_pairs={{0,4},{4,0},{8,12},{12,8},{1,5},{5,1},{9,13},{13,9},{2,6},{6,2},{1... | collective-permute-start | bytes 122888 | tf_op jit(solution)/shard_map/ppermute | solution.py:329
  7.0 2.6 %collective-permute-start.1 = (bf16[2,4,2560]{2,1,0:T(4,128)(2,1)S(1)}, bf16[2,4,2560]{2,1,0:T(4,128)(2,1)S(1)}, u32[]{:S(2)}, u32[]{:S(2)}) collective-permute-start(bf16[2,4,2560]{2,1,0:T(4,128)(2,1)S(1)} %get-tuple-element.8), channel_id=1, source_target_pairs={{0,8},{4,12},{8,0},{12,4},{1,9},{5,13},{9,1},{13,5},{2,10},{6,14},... | collective-permute-start | bytes 122888 | tf_op jit(solution)/shard_map/ppermute | solution.py:329
  9.6 3.1 %collective-permute-done.1.refs_2_ = bf16[2,4,2560]{2,1,0:T(4,128)(2,1)S(1)} collective-permute-done((bf16[2,4,2560]{2,1,0:T(4,128)(2,1)S(1)}, bf16[2,4,2560]{2,1,0:T(4,128)(2,1)S(1)}, u32[]{:S(2)}, u32[]{:S(2)}) %collective-permute-start.1) | collective-permute-done | bytes 40992 | tf_op jit(solution)/shard_map/ppermute | solution.py:329
  12.7 2.7 %collective-permute-done.2.refs_3_ = bf16[2,4,2560]{2,1,0:T(4,128)(2,1)S(1)} collective-permute-done((bf16[2,4,2560]{2,1,0:T(4,128)(2,1)S(1)}, bf16[2,4,2560]{2,1,0:T(4,128)(2,1)S(1)}, u32[]{:S(2)}, u32[]{:S(2)}) %collective-permute-start.2) | collective-permute-done | bytes 40992 | tf_op jit(solution)/shard_map/ppermute | solution.py:329
  15.4 1.0 %copy-done = bf16[2,512,256]{2,1,0:T(8,128)(2,1)S(1)} copy-done((bf16[2,512,256]{2,1,0:T(8,128)(2,1)S(1)}, bf16[2,512,256]{2,1,0:T(8,128)(2,1)}, u32[]{:S(2)}) %copy-start) | copy-done | bytes 524312
  16.4 0.7 %copy-done.5 = s32[16,1]{0,1:T(1,128)S(1)} copy-done((s32[16,1]{0,1:T(1,128)S(1)}, s32[16,1]{0,1:T(1,128)}, u32[]{:S(2)}) %copy-start.5) | copy-done | bytes 88
  17.1 0.7 %copy-done.7 = s32[4,32]{1,0:T(4,128)S(1)} copy-done((s32[4,32]{1,0:T(4,128)S(1)}, s32[4,32]{1,0:T(4,128)}, u32[]{:S(2)}) %copy-start.7) | copy-done | bytes 536
  17.7 1.4 %decode_attention.1.refs_0_ = bf16[16,2048]{1,0:T(8,128)(2,1)S(1)} custom-call(s32[2]{0:T(128)S(1)} %pad_add_fusion.where_ref, s32[16]{0:T(128)S(1)} %bitcast.4, s32[4,32]{1,0:T(4,128)S(1)} %copy-done.7, bf16[2,512,256]{2,1,0:T(8,128)(2,1)S(1)} %copy-done, bf16[2,4,2560]{2,1,0:T(4,128)(2,1)S(1)} %get-tuple-element.6.refs_0_, ...), custom_call_target="tpu_custom_call" | custom-call | tf_op jit(solution)/shard_map/decode_attention/pallas_call | solution.py:208
  19.2 0.6 %collective-permute-start.5 = (bf16[16,2048]{1,0:T(8,128)(2,1)S(1)}, bf16[16,2048]{1,0:T(8,128)(2,1)S(1)}, u32[]{:S(2)}, u32[]{:S(2)}) collective-permute-start(bf16[16,2048]{1,0:T(8,128)(2,1)S(1)} %decode_attention.1.refs_0_), channel_id=1, source_target_pairs={{0,12},{4,8},{8,4},{12,0},{1,13},{5,9},{9,5},{13,1},{2,14},{6,10},... | collective-permute-start | bytes 196616 | tf_op jit(solution)/shard_map/ppermute | solution.py:329
  19.8 0.0 collective-permute-start.4
  19.8 3.8 %collective-permute-start.3 = (bf16[16,2048]{1,0:T(8,128)(2,1)S(1)}, bf16[16,2048]{1,0:T(8,128)(2,1)S(1)}, u32[]{:S(2)}, u32[]{:S(2)}) collective-permute-start(bf16[16,2048]{1,0:T(8,128)(2,1)S(1)} %decode_attention.1.refs_0_), channel_id=1, source_target_pairs={{0,4},{4,0},{8,12},{12,8},{1,5},{5,1},{9,13},{13,9},{2,6},{6,2},{1... | collective-permute-start | bytes 196616 | tf_op jit(solution)/shard_map/ppermute | solution.py:329
  23.6 1.8 %collective-permute-done.5.refs_3_ = bf16[16,2048]{1,0:T(8,128)(2,1)S(1)} collective-permute-done((bf16[16,2048]{1,0:T(8,128)(2,1)S(1)}, bf16[16,2048]{1,0:T(8,128)(2,1)S(1)}, u32[]{:S(2)}, u32[]{:S(2)}) %collective-permute-start.5) | collective-permute-done | bytes 65568 | tf_op jit(solution)/shard_map/ppermute | solution.py:329
  25.4 0.9 %collective-permute-done.4.refs_2_ = bf16[16,2048]{1,0:T(8,128)(2,1)S(1)} collective-permute-done((bf16[16,2048]{1,0:T(8,128)(2,1)S(1)}, bf16[16,2048]{1,0:T(8,128)(2,1)S(1)}, u32[]{:S(2)}, u32[]{:S(2)}) %collective-permute-start.4) | collective-permute-done | bytes 65568 | tf_op jit(solution)/shard_map/ppermute | solution.py:329
  26.3 3.5 %project_half.3 = bf16[64,1024]{1,0:T(8,128)(2,1)S(1)} custom-call(s32[1]{0:T(128)S(6)} %sub.3.half_ref, bf16[16,2048]{1,0:T(8,128)(2,1)S(1)} %decode_attention.1.refs_0_, bf16[16,2048]{1,0:T(8,128)(2,1)S(1)} %collective-permute-done.3.refs_1_, bf16[16,2048]{1,0:T(8,128)(2,1)S(1)} %collective-permute-done.4.refs_2_, ...), custom_call_target="tpu_custom_call" | custom-call | flops 268435456 | bytes 4194304 | tf_op jit(solution)/shard_map/project_half/pallas_call | solution.py:235
  29.9 0.0 copy-start.1
  29.9 0.0 copy-start.8
  29.9 0.0 copy-start.9
  29.9 0.1 collective-permute-start.6
  30.0 3.7 %project_half.2 = f32[64,1024]{1,0:T(8,128)S(1)} custom-call(s32[1]{0:T(128)} %bitcast.1.half_ref, bf16[16,2048]{1,0:T(8,128)(2,1)S(1)} %decode_attention.1.refs_0_, bf16[16,2048]{1,0:T(8,128)(2,1)S(1)} %collective-permute-done.3.refs_1_, bf16[16,2048]{1,0:T(8,128)(2,1)S(1)} %collective-permute-done.4.refs_2_, ...), custom_call_target="tpu_custom_call" | custom-call | flops 268435456 | bytes 4194304 | tf_op jit(solution)/shard_map/project_half/pallas_call | solution.py:235
  33.7 1.6 %collective-permute-start.7 = (bf16[64,1024]{1,0:T(8,128)(2,1)S(1)}, bf16[64,1024]{1,0:T(8,128)(2,1)S(1)}, u32[]{:S(2)}, u32[]{:S(2)}) collective-permute-start(bf16[64,1024]{1,0:T(8,128)(2,1)S(1)} %fusion), channel_id=1, source_target_pairs={{0,2},{1,3},{2,0},{3,1},{4,6},{5,7},{6,4},{7,5},{8,10},{9,11},{10,... | collective-permute-start | bytes 393224 | tf_op jit(solution)/shard_map/ppermute | solution.py:329
  35.3 4.2 %collective-permute-done.7 = bf16[64,1024]{1,0:T(8,128)(2,1)S(1)} collective-permute-done((bf16[64,1024]{1,0:T(8,128)(2,1)S(1)}, bf16[64,1024]{1,0:T(8,128)(2,1)S(1)}, u32[]{:S(2)}, u32[]{:S(2)}) %collective-permute-start.7) | collective-permute-done | bytes 131104 | tf_op jit(solution)/shard_map/ppermute | solution.py:329
  39.5 0.1 add_convert_fusion.mine_ref
  39.6 0.0 copy-start.6
  39.6 0.1 collective-permute-start.8
  39.7 12.8 %prefill_attention.1 = bf16[512,2048]{1,0:T(8,128)(2,1)} custom-call(s32[2]{0:T(128)S(1)} %pad_add_fusion.where_ref, s32[4,32]{1,0:T(4,128)S(1)} %copy-done.8, bf16[512,2048]{1,0:T(8,128)(2,1)S(1)} %copy-done.9, bf16[2,512,256]{2,1,0:T(8,128)(2,1)S(1)} %copy-done.1, bf16[2,512,256]{2,1,0:T(8,128)(2,1)S(1)} %copy-done.1), custom_call_target="tpu_custom_call" | custom-call | flops 2147483648 | bytes 4718592 | tf_op jit(solution)/shard_map/prefill_attention/pallas_call | solution.py:126
  52.5 0.0 collective-permute-done.8.other_ref
  52.5 2.6 %scatter_slots.1 = bf16[32,4,2048]{2,1,0:T(4,128)(2,1)} custom-call(s32[2]{0:T(128)S(1)} %pad_add_fusion.where_ref, s32[16]{0:T(128)S(1)} %bitcast.5, bf16[64,1024]{1,0:T(8,128)(2,1)S(1)} %add_convert_fusion.mine_ref, bf16[64,1024]{1,0:T(8,128)(2,1)S(1)} %collective-permute-done.8.other_ref), custom_call_target="tpu_custom_call" | custom-call | tf_op jit(solution)/shard_map/scatter_slots/pallas_call | solution.py:313
  (15 shorter events, 0.1 us)
Async XLA Ops:
  0.7 0.9 %copy-start.2 = (bf16[8,4,2048]{2,1,0:T(4,128)(2,1)S(1)}, bf16[8,4,2048]{2,1,0:T(4,128)(2,1)}, u32[]{:S(2)}) copy-start(bf16[8,4,2048]{2,1,0:T(4,128)(2,1)} %q_ref.3) | copy-start | bytes 393220
  1.6 0.8 %copy-start.3 = (bf16[2,8,4,256]{3,2,1,0:T(4,128)(2,1)S(1)}, bf16[2,8,4,256]{3,2,1,0:T(4,128)(2,1)}, u32[]{:S(2)}) copy-start(bf16[2,8,4,256]{3,2,1,0:T(4,128)(2,1)} %kv_ref.2) | copy-start | bytes 98308
  2.4 0.7 %copy-start.4 = (s32[16,1]{0,1:T(1,128)S(1)}, s32[16,1]{0,1:T(1,128)}, u32[]{:S(2)}) copy-start(s32[16,1]{0,1:T(1,128)} %param.13) | copy-start | bytes 196
  3.9 5.7 %collective-permute-start = (bf16[2,4,2560]{2,1,0:T(4,128)(2,1)S(1)}, bf16[2,4,2560]{2,1,0:T(4,128)(2,1)S(1)}, u32[]{:S(2)}, u32[]{:S(2)}) collective-permute-start(bf16[2,4,2560]{2,1,0:T(4,128)(2,1)S(1)} %get-tuple-element.7), channel_id=1, source_target_pairs={{0,4},{4,0},{8,12},{12,8},{1,5},{5,1},{9,13},{13,9},{2,6},{6,2},{1... | collective-permute-start | bytes 122888 | tf_op jit(solution)/shard_map/ppermute | solution.py:329
  7.0 5.7 %collective-permute-start.1 = (bf16[2,4,2560]{2,1,0:T(4,128)(2,1)S(1)}, bf16[2,4,2560]{2,1,0:T(4,128)(2,1)S(1)}, u32[]{:S(2)}, u32[]{:S(2)}) collective-permute-start(bf16[2,4,2560]{2,1,0:T(4,128)(2,1)S(1)} %get-tuple-element.8), channel_id=1, source_target_pairs={{0,8},{4,12},{8,0},{12,4},{1,9},{5,13},{9,1},{13,5},{2,10},{6,14},... | collective-permute-start | bytes 122888 | tf_op jit(solution)/shard_map/ppermute | solution.py:329
  9.6 5.8 %collective-permute-start.2 = (bf16[2,4,2560]{2,1,0:T(4,128)(2,1)S(1)}, bf16[2,4,2560]{2,1,0:T(4,128)(2,1)S(1)}, u32[]{:S(2)}, u32[]{:S(2)}) collective-permute-start(bf16[2,4,2560]{2,1,0:T(4,128)(2,1)S(1)} %get-tuple-element.9), channel_id=1, source_target_pairs={{0,12},{4,8},{8,4},{12,0},{1,13},{5,9},{9,5},{13,1},{2,14},{6,10},... | collective-permute-start | bytes 122888 | tf_op jit(solution)/shard_map/ppermute | solution.py:329
  15.4 1.0 %copy-start = (bf16[2,512,256]{2,1,0:T(8,128)(2,1)S(1)}, bf16[2,512,256]{2,1,0:T(8,128)(2,1)}, u32[]{:S(2)}) copy-start(bf16[2,512,256]{2,1,0:T(8,128)(2,1)} %kv_ref.3) | copy-start | bytes 1572868
  16.4 0.7 %copy-start.5 = (s32[16,1]{0,1:T(1,128)S(1)}, s32[16,1]{0,1:T(1,128)}, u32[]{:S(2)}) copy-start(s32[16,1]{0,1:T(1,128)} %param.13) | copy-start | bytes 196
  17.1 0.7 %copy-start.7 = (s32[4,32]{1,0:T(4,128)S(1)}, s32[4,32]{1,0:T(4,128)}, u32[]{:S(2)}) copy-start(s32[4,32]{1,0:T(4,128)} %page_ref.3) | copy-start | bytes 1540
  19.2 6.3 %collective-permute-start.5 = (bf16[16,2048]{1,0:T(8,128)(2,1)S(1)}, bf16[16,2048]{1,0:T(8,128)(2,1)S(1)}, u32[]{:S(2)}, u32[]{:S(2)}) collective-permute-start(bf16[16,2048]{1,0:T(8,128)(2,1)S(1)} %decode_attention.1.refs_0_), channel_id=1, source_target_pairs={{0,12},{4,8},{8,4},{12,0},{1,13},{5,9},{9,5},{13,1},{2,14},{6,10},... | collective-permute-start | bytes 196616 | tf_op jit(solution)/shard_map/ppermute | solution.py:329
  19.8 6.6 %collective-permute-start.4 = (bf16[16,2048]{1,0:T(8,128)(2,1)S(1)}, bf16[16,2048]{1,0:T(8,128)(2,1)S(1)}, u32[]{:S(2)}, u32[]{:S(2)}) collective-permute-start(bf16[16,2048]{1,0:T(8,128)(2,1)S(1)} %decode_attention.1.refs_0_), channel_id=1, source_target_pairs={{0,8},{4,12},{8,0},{12,4},{1,9},{5,13},{9,1},{13,5},{2,10},{6,14},... | collective-permute-start | bytes 196616 | tf_op jit(solution)/shard_map/ppermute | solution.py:329
  19.8 6.5 %collective-permute-start.3 = (bf16[16,2048]{1,0:T(8,128)(2,1)S(1)}, bf16[16,2048]{1,0:T(8,128)(2,1)S(1)}, u32[]{:S(2)}, u32[]{:S(2)}) collective-permute-start(bf16[16,2048]{1,0:T(8,128)(2,1)S(1)} %decode_attention.1.refs_0_), channel_id=1, source_target_pairs={{0,4},{4,0},{8,12},{12,8},{1,5},{5,1},{9,13},{13,9},{2,6},{6,2},{1... | collective-permute-start | bytes 196616 | tf_op jit(solution)/shard_map/ppermute | solution.py:329
  29.9 9.8 %copy-start.1 = (bf16[2,512,256]{2,1,0:T(8,128)(2,1)S(1)}, bf16[2,512,256]{2,1,0:T(8,128)(2,1)}, u32[]{:S(2)}) copy-start(bf16[2,512,256]{2,1,0:T(8,128)(2,1)} %kv_ref.3) | copy-start | bytes 1572868
  29.9 9.8 %copy-start.8 = (s32[4,32]{1,0:T(4,128)S(1)}, s32[4,32]{1,0:T(4,128)}, u32[]{:S(2)}) copy-start(s32[4,32]{1,0:T(4,128)} %page_ref.3) | copy-start | bytes 1540
  29.9 9.8 %copy-start.9 = (bf16[512,2048]{1,0:T(8,128)(2,1)S(1)}, bf16[512,2048]{1,0:T(8,128)(2,1)}, u32[]{:S(2)}) copy-start(bf16[512,2048]{1,0:T(8,128)(2,1)} %q_ref.2) | copy-start | bytes 6291460
  29.9 3.8 %collective-permute-start.6 = (bf16[64,1024]{1,0:T(8,128)(2,1)S(1)}, bf16[64,1024]{1,0:T(8,128)(2,1)S(1)}, u32[]{:S(2)}, u32[]{:S(2)}) collective-permute-start(bf16[64,1024]{1,0:T(8,128)(2,1)S(1)} %project_half.3), channel_id=1, source_target_pairs={{0,1},{1,0},{2,3},{3,2},{4,5},{5,4},{6,7},{7,6},{8,9},{9,8},{10,11... | collective-permute-start | bytes 393224 | tf_op jit(solution)/shard_map/ppermute | solution.py:329
  33.7 5.8 %collective-permute-start.7 = (bf16[64,1024]{1,0:T(8,128)(2,1)S(1)}, bf16[64,1024]{1,0:T(8,128)(2,1)S(1)}, u32[]{:S(2)}, u32[]{:S(2)}) collective-permute-start(bf16[64,1024]{1,0:T(8,128)(2,1)S(1)} %fusion), channel_id=1, source_target_pairs={{0,2},{1,3},{2,0},{3,1},{4,6},{5,7},{6,4},{7,5},{8,10},{9,11},{10,... | collective-permute-start | bytes 393224 | tf_op jit(solution)/shard_map/ppermute | solution.py:329
  39.6 12.9 %copy-start.6 = (s32[16,1]{0,1:T(1,128)S(1)}, s32[16,1]{0,1:T(1,128)}, u32[]{:S(2)}) copy-start(s32[16,1]{0,1:T(1,128)} %param.13) | copy-start | bytes 196
  39.6 12.9 %collective-permute-start.8 = (bf16[64,1024]{1,0:T(8,128)(2,1)S(1)}, bf16[64,1024]{1,0:T(8,128)(2,1)S(1)}, u32[]{:S(2)}, u32[]{:S(2)}) collective-permute-start(bf16[64,1024]{1,0:T(8,128)(2,1)S(1)} %add_convert_fusion.mine_ref), channel_id=1, source_target_pairs={{0,1},{1,0},{2,3},{3,2},{4,5},{5,4},{6,7},{7,6},{8,9},{9,8},{10,11... | collective-permute-start | bytes 393224 | tf_op jit(solution)/shard_map/ppermute | solution.py:329

commit v2 on v0

v2 whole, which is shorter than its diff:
```python
import functools

import jax
import jax.numpy as jnp
from jax import lax
from jax.experimental import pallas as pl
from jax.experimental.pallas import tpu as pltpu
from jax.sharding import PartitionSpec as P

HEAD_DIM = 128
GROUP = 8
PAGE = 16
PAIRS_DEV = 4
STEPS = 4
DSLOT = 8
TOK_DEV = 512
CAP = 2
BLOCK = 128
ROWS = PAIRS_DEV * STEPS
SCALE = HEAD_DIM ** (-0.5)
EXP2_SCALE = SCALE * 1.4426950408889634
MASKED = -1e30
VMEM_LIMIT = 20 * 1024 * 1024
REACH = 2
LATEST = (REACH + 1) * BLOCK

SMEM_SPEC = pl.BlockSpec(memory_space=pltpu.SMEM)
VMEM_SPEC = pl.BlockSpec(memory_space=pltpu.VMEM)
ANY_SPEC = pl.BlockSpec(memory_space=pl.ANY)


def params():
    return pltpu.CompilerParams(vmem_limit_bytes=VMEM_LIMIT)


def in_hbm(x):
    return pltpu.with_memory_space_constraint(x, pltpu.HBM)


def pack_kernel(sections, owner_hbm, q_hbm, kv_hbm, *refs):
    outs = refs[:sections]
    owner, q, kv, packed, sems = refs[sections:]
    copies = [
        pltpu.make_async_copy(owner_hbm, owner, sems.at[0]),
        pltpu.make_async_copy(q_hbm, q, sems.at[1]),
        pltpu.make_async_copy(kv_hbm, kv, sems.at[2]),
    ]
    for copy in copies:
        copy.start()
    here = lax.axis_index("section")
    width, kv_width = q.shape[2], kv.shape[3]
    packed[...] = jnp.zeros_like(packed)
    for copy in copies:
        copy.wait()

    def place(pair, carry):
        slot, rank = carry
        rank = jnp.where(pair % PAIRS_DEV == 0, 0, rank)
        mine = owner[pair] == here

        @pl.when(mine)
        def _():
            to = (pair // PAIRS_DEV) ^ here
            packed[to, rank, :, :width] = q[slot]
            packed[to, rank, :, width : width + kv_width] = kv[0, slot]
            packed[to, rank, :, width + kv_width :] = kv[1, slot]

        step = mine.astype(jnp.int32)
        return slot + step, rank + step

    lax.fori_loop(0, owner.shape[0], place, (jnp.int32(0), jnp.int32(0)))
    for k in range(sections):
        outs[k][...] = packed[k]


def pack(owner, decode_q, decode_kv, sections):
    width = decode_q.shape[2] + 2 * decode_kv.shape[3]
    block = (CAP, STEPS, width)
    return pl.pallas_call(
        functools.partial(pack_kernel, sections),
        out_shape=[jax.ShapeDtypeStruct(block, jnp.bfloat16)] * sections,
        in_specs=[ANY_SPEC] * 3,
        out_specs=[VMEM_SPEC] * sections,
        scratch_shapes=[
            pltpu.SMEM(owner.shape, jnp.int32),
            pltpu.VMEM(decode_q.shape, jnp.bfloat16),
            pltpu.VMEM(decode_kv.shape, jnp.bfloat16),
            pltpu.VMEM((sections,) + block, jnp.bfloat16),
            pltpu.SemaphoreType.DMA((3,)),
        ],
        compiler_params=params(),
        name="pack_queries",
    )(in_hbm(owner), in_hbm(decode_q), in_hbm(decode_kv))


def pair_starts(page, here):
    rows = lax.broadcasted_iota(jnp.int32, page.shape, 0)
    starts = [jnp.zeros((1, 1), jnp.int32)]
    for j in range(1, PAIRS_DEV):
        lower = jnp.where((rows == here) & (page[...] < j), 1, 0)
        starts.append(jnp.sum(jnp.sum(lower, axis=1, keepdims=True), axis=0, keepdims=True) * PAGE)
    return starts + [jnp.full((1, 1), TOK_DEV, jnp.int32)]


def prefill_masks(starts, bias):
    for i in range(TOK_DEV // BLOCK):
        low = max(0, i - REACH) * BLOCK
        width = (i + 1) * BLOCK - low
        row = lax.broadcasted_iota(jnp.int32, (BLOCK, 1), 0) + i * BLOCK
        first = jnp.zeros((BLOCK, 1), jnp.int32)
        for j in range(1, PAIRS_DEV):
            first = jnp.where(row >= starts[j], starts[j], first)
        row = lax.broadcasted_iota(jnp.int32, (BLOCK, width), 0) + i * BLOCK
        col = lax.broadcasted_iota(jnp.int32, (BLOCK, width), 1) + low
        bias[i, :, :width] = jnp.where((col <= row) & (col >= first), 0.0, MASKED)


def decode_masks(starts, bias):
    row = lax.broadcasted_iota(jnp.int32, (ROWS, 1), 0) // STEPS
    first, last = jnp.zeros((ROWS, 1), jnp.int32), jnp.zeros((ROWS, 1), jnp.int32)
    for j in range(PAIRS_DEV):
        first = jnp.where(row == j, starts[j], first)
        last = jnp.where(row == j, starts[j + 1], last)
    col = lax.broadcasted_iota(jnp.int32, bias.shape, 1)
    bias[...] = jnp.where((col >= first) & (col < last), 0.0, MASKED)


def owner_tables(owner, here, pick, spread):
    pairs = owner.shape[1]
    down = lax.broadcasted_iota(jnp.int32, (pairs, pairs), 0)
    along = lax.broadcasted_iota(jnp.int32, (pairs, pairs), 1)
    owner_along = jnp.broadcast_to(owner[...], (pairs, pairs))
    owner_down = jnp.sum(jnp.where(down == along, owner_along, 0), axis=1, keepdims=True)
    same = owner_along == owner_down
    slot_rank = jnp.sum(jnp.where(same & (down < along), 1, 0), axis=0, keepdims=True)
    slot = owner[...] * DSLOT + slot_rank

    at_home = down // PAIRS_DEV == along // PAIRS_DEV
    home_rank = jnp.sum(jnp.where(same & at_home & (along < down), 1, 0), axis=1, keepdims=True)
    base = ((owner_down ^ here) * CAP + home_rank) * STEPS
    row = lax.broadcasted_iota(jnp.int32, pick.shape, 0)
    col = lax.broadcasted_iota(jnp.int32, pick.shape, 1)
    pair = lax.broadcasted_iota(jnp.int32, (pairs, 1), 0)
    at = row % STEPS
    for j in range(PAIRS_DEV):
        mine = jnp.sum(jnp.where(pair == here * PAIRS_DEV + j, base, 0), axis=0, keepdims=True)
        at = at + jnp.where(row // STEPS == j, mine, 0)
    pick[...] = (col == at).astype(jnp.float32).astype(pick.dtype)

    wide = spread.shape[1]
    pair = lax.broadcasted_iota(jnp.int32, (pairs, wide), 0)
    place = lax.broadcasted_iota(jnp.int32, (pairs, wide), 1) // STEPS
    holds = place == ((pair // PAIRS_DEV) ^ here) * PAIRS_DEV + pair % PAIRS_DEV
    slot_down = jnp.sum(jnp.where(down == along, jnp.broadcast_to(slot, (pairs, pairs)), 0), axis=1, keepdims=True)
    slot_of_place = jnp.sum(jnp.where(holds, slot_down, 0), axis=0, keepdims=True)
    row = lax.broadcasted_iota(jnp.int32, spread.shape, 0)
    col = lax.broadcasted_iota(jnp.int32, spread.shape, 1)
    spread[...] = (row == slot_of_place * STEPS + col % STEPS).astype(jnp.float32).astype(spread.dtype)


def region(ref, unit):
    k, i = unit
    wide = GROUP * HEAD_DIM
    return ref.at[pl.ds(i * BLOCK, BLOCK), pl.ds(k * wide, wide)]


def attend(unit, q, bias, keys, values, o):
    k, i = unit
    low, high = max(0, i - REACH) * BLOCK, (i + 1) * BLOCK
    width = high - low
    rows = jnp.concatenate([q[:, g * HEAD_DIM : (g + 1) * HEAD_DIM] for g in range(GROUP)], axis=0)
    s = jnp.dot(rows, keys[k, :, low:high], preferred_element_type=jnp.float32)
    s = (s.reshape(GROUP, BLOCK, width) + bias[i, :, :width][None]).reshape(GROUP * BLOCK, width)
    m = jnp.max(s, axis=1, keepdims=True)
    p = jnp.exp2((s - m) * EXP2_SCALE).astype(jnp.bfloat16)
    y = jnp.dot(p, values[k, low:high, :], preferred_element_type=jnp.float32)
    y = (y[:, :HEAD_DIM] / y[:, HEAD_DIM:]).astype(jnp.bfloat16)
    for g in range(GROUP):
        o[:, g * HEAD_DIM : (g + 1) * HEAD_DIM] = y[g * BLOCK : (g + 1) * BLOCK]


def half_columns(ref, flip):
    wide = ref.shape[-1] // 2
    half = lax.axis_index("tensor") % 2
    half = 1 - half if flip else half
    return ref.at[(slice(None),) * (len(ref.shape) - 1) + (pl.ds(pl.multiple_of(half * wide, wide), wide),)]


def flushes(units, blocks, ctx_hbm, sems):
    return [pltpu.make_async_copy(blocks.at[n], region(ctx_hbm, u), sems.at[n]) for n, u in enumerate(units)]


def first_kernel(
    units, later, page_hbm, owner_hbm, q_hbm, kv_hbm, wo_hbm, after,
    o, q_later, bias, keys, values, seen, pick, spread, wo_away,
    page, owner, kv, q, q_sems, late_sems, sems,
):
    del after
    small = [
        pltpu.make_async_copy(page_hbm, page, sems.at[0]),
        pltpu.make_async_copy(owner_hbm, owner, sems.at[1]),
    ]
    cache = pltpu.make_async_copy(kv_hbm, kv, sems.at[2])
    soon = [pltpu.make_async_copy(region(q_hbm, u), q.at[n], q_sems.at[n]) for n, u in enumerate(units)]
    late = [pltpu.make_async_copy(region(q_hbm, u), q_later.at[n], late_sems.at[n]) for n, u in enumerate(later)]
    weights = pltpu.make_async_copy(half_columns(wo_hbm, True), wo_away, sems.at[3])
    for copy in small + [cache] + soon + [weights] + late:
        copy.start()
    here = lax.axis_index("section")
    for copy in small:
        copy.wait()
    starts = pair_starts(page, here)
    prefill_masks(starts, bias)
    decode_masks(starts, seen)
    owner_tables(owner, here, pick, spread)
    cache.wait()
    for k in range(keys.shape[0]):
        cols = slice(k * HEAD_DIM, (k + 1) * HEAD_DIM)
        keys[k] = kv[0, :, cols].astype(jnp.float32).T.astype(jnp.bfloat16)
        values[k, :, :HEAD_DIM] = kv[1, :, cols]
        values[k, :, HEAD_DIM:] = jnp.ones((TOK_DEV, HEAD_DIM), jnp.bfloat16)
    for n, unit in enumerate(units):
        soon[n].wait()
        attend(unit, q.at[n], bias, keys, values, o.at[n])
    for copy in late + [weights]:
        copy.wait()


def second_kernel(units, done, q, bias, keys, values, done_o, wo_hbm, after, ctx_hbm, o, wo_keep, sems, wo_sem):
    del after
    copies = flushes(done, done_o, ctx_hbm, sems)
    copies.append(pltpu.make_async_copy(half_columns(wo_hbm, False), wo_keep, wo_sem))
    for copy in copies:
        copy.start()
    for n, unit in enumerate(units):
        attend(unit, q.at[n], bias, keys, values, o.at[n])
    for copy in copies:
        copy.wait()


def third_kernel(units, offset, done, q, bias, keys, values, done_o, ctx_in, chip_in, ctx_hbm, o, chip, sems):
    del ctx_in, chip_in, chip
    copies = flushes(done, done_o, ctx_hbm, sems)
    for copy in copies:
        copy.start()
    for n, unit in enumerate(units):
        attend(unit, q.at[offset + n], bias, keys, values, o.at[n])
    for copy in copies:
        copy.wait()


def unit_cost(units):
    pairs = sum(min(i + 1, REACH + 1) for _, i in units) * GROUP * BLOCK * BLOCK
    return pl.CostEstimate(
        flops=pairs * HEAD_DIM * 8, bytes_accessed=len(units) * BLOCK * GROUP * HEAD_DIM * 4, transcendentals=pairs
    )


def block_shape(units):
    return jax.ShapeDtypeStruct((len(units), BLOCK, GROUP * HEAD_DIM), jnp.bfloat16)


def prefill_first(units, later, page_pair, owner, prefill_q, kv_pool, wo, after, sections):
    kv_local = kv_pool.shape[2] // HEAD_DIM
    return pl.pallas_call(
        functools.partial(first_kernel, units, later),
        out_shape=[
            block_shape(units),
            block_shape(later),
            jax.ShapeDtypeStruct((TOK_DEV // BLOCK, BLOCK, LATEST), jnp.float32),
            jax.ShapeDtypeStruct((kv_local, HEAD_DIM, TOK_DEV), jnp.bfloat16),
            jax.ShapeDtypeStruct((kv_local, TOK_DEV, 2 * HEAD_DIM), jnp.bfloat16),
            jax.ShapeDtypeStruct((ROWS, TOK_DEV), jnp.float32),
            jax.ShapeDtypeStruct((ROWS, sections * CAP * STEPS), jnp.bfloat16),
            jax.ShapeDtypeStruct((sections * DSLOT * STEPS, sections * ROWS), jnp.bfloat16),
            jax.ShapeDtypeStruct((wo.shape[0], wo.shape[1] // 2), wo.dtype),
        ],
        in_specs=[ANY_SPEC] * 6,
        out_specs=[VMEM_SPEC] * 9,
        scratch_shapes=[
            pltpu.VMEM(page_pair.shape, jnp.int32),
            pltpu.VMEM(owner.shape, jnp.int32),
            pltpu.VMEM(kv_pool.shape, jnp.bfloat16),
            pltpu.VMEM(block_shape(units).shape, jnp.bfloat16),
            pltpu.SemaphoreType.DMA((len(units),)),
            pltpu.SemaphoreType.DMA((len(later),)),
            pltpu.SemaphoreType.DMA((4,)),
        ],
        compiler_params=params(),
        cost_estimate=unit_cost(units),
        name="prefill_first",
    )(in_hbm(page_pair), in_hbm(owner), in_hbm(prefill_q), in_hbm(kv_pool), in_hbm(wo), after)


def prefill_second(units, done, q, tables, done_o, wo, ctx_shape, after):
    return pl.pallas_call(
        functools.partial(second_kernel, units, done),
        out_shape=[
            ctx_shape,
            block_shape(units),
            jax.ShapeDtypeStruct((wo.shape[0], wo.shape[1] // 2), wo.dtype),
        ],
        in_specs=[VMEM_SPEC] * 5 + [ANY_SPEC] * 2,
        out_specs=[ANY_SPEC, VMEM_SPEC, VMEM_SPEC],
        scratch_shapes=[pltpu.SemaphoreType.DMA((len(done),)), pltpu.SemaphoreType.DMA],
        compiler_params=params(),
        cost_estimate=unit_cost(units),
        name="prefill_second",
    )(q, *tables, done_o, in_hbm(wo), after)


def prefill_third(units, offset, done, q, tables, done_o, ctx, chip):
    return pl.pallas_call(
        functools.partial(third_kernel, units, offset, done),
        out_shape=[
            jax.ShapeDtypeStruct(ctx.shape, ctx.dtype),
            block_shape(units),
            jax.ShapeDtypeStruct(chip.shape, chip.dtype),
        ],
        in_specs=[VMEM_SPEC] * 5 + [ANY_SPEC, VMEM_SPEC],
        out_specs=[ANY_SPEC, VMEM_SPEC, VMEM_SPEC],
        scratch_shapes=[pltpu.SemaphoreType.DMA((len(done),))],
        input_output_aliases={5: 0, 6: 2},
        compiler_params=params(),
        cost_estimate=unit_cost(units),
        name="prefill_third",
    )(q, *tables, done_o, ctx, chip)


def split_units(kv_local):
    order = [(0, 0), (0, 3), (0, 1), (0, 2)]
    units = [(k, i) for k in range(kv_local) for _, i in order]
    first, second = len(units) // 4, len(units) // 2
    return units[:first], units[first:second], units[second:]


def decode_kernel(sections, seen, pick, keys, values, *refs):
    got, ctx_ref, rows = refs[:sections], refs[sections], refs[sections + 1]
    kv_local = keys.shape[0]
    width = kv_local * GROUP * HEAD_DIM
    for k in range(sections):
        for r in range(CAP):
            at = (k * CAP + r) * STEPS
            rows[at : at + STEPS, :] = got[k][r].astype(jnp.float32)
    all_rows = jnp.dot(pick[...], rows[...].astype(jnp.bfloat16), preferred_element_type=jnp.float32)
    all_rows = all_rows.astype(jnp.bfloat16)

    many = GROUP * ROWS
    new_row = lax.broadcasted_iota(jnp.int32, (many, ROWS), 0) % ROWS
    new_col = lax.broadcasted_iota(jnp.int32, (many, ROWS), 1)
    new_allowed = (new_row // STEPS == new_col // STEPS) & (new_col <= new_row)
    contract = (((1,), (1,)), ((), ()))
    for k in range(kv_local):
        q = jnp.concatenate(
            [all_rows[:, (k * GROUP + g) * HEAD_DIM : (k * GROUP + g + 1) * HEAD_DIM] for g in range(GROUP)], axis=0
        )
        new_keys = all_rows[:, width + k * HEAD_DIM : width + (k + 1) * HEAD_DIM]
        at = width + (kv_local + k) * HEAD_DIM
        new_values = all_rows[:, at : at + HEAD_DIM]
        s = jnp.dot(q, keys[k], preferred_element_type=jnp.float32)
        s = (s.reshape(GROUP, ROWS, TOK_DEV) + seen[...][None]).reshape(many, TOK_DEV)
        s_new = lax.dot_general(q, new_keys, contract, preferred_element_type=jnp.float32)
        s_new = jnp.where(new_allowed, s_new, MASKED)
        m = jnp.maximum(jnp.max(s, axis=1, keepdims=True), jnp.max(s_new, axis=1, keepdims=True))
        p = jnp.exp2((s - m) * EXP2_SCALE)
        p_new = jnp.exp2((s_new - m) * EXP2_SCALE)
        o = jnp.dot(p.astype(jnp.bfloat16), values[k], preferred_element_type=jnp.float32)
        total = o[:, HEAD_DIM:] + jnp.sum(p_new, axis=1, keepdims=True)
        o = o[:, :HEAD_DIM] + jnp.dot(p_new.astype(jnp.bfloat16), new_values, preferred_element_type=jnp.float32)
        o = (o / total).astype(jnp.bfloat16)
        for g in range(GROUP):
            ctx_ref[:, (k * GROUP + g) * HEAD_DIM : (k * GROUP + g + 1) * HEAD_DIM] = o[g * ROWS : (g + 1) * ROWS]


def decode(seen, pick, keys, values, got, sections):
    block = got[0].shape
    width = keys.shape[0] * GROUP * HEAD_DIM
    return pl.pallas_call(
        functools.partial(decode_kernel, sections),
        out_shape=jax.ShapeDtypeStruct((ROWS, width), jnp.bfloat16),
        in_specs=[VMEM_SPEC] * (4 + sections),
        out_specs=VMEM_SPEC,
        scratch_shapes=[pltpu.VMEM((sections * CAP * STEPS, block[2]), jnp.float32)],
        compiler_params=params(),
        name="decode_attention",
    )(seen, pick, keys, values, *got)


def project_kernel(sections, *refs):
    ctxs, wo, out_ref = refs[:sections], refs[sections], refs[-1]
    x = jnp.concatenate([c[...] for c in ctxs], axis=0)
    out_ref[...] = jnp.dot(x, wo[...], preferred_element_type=jnp.float32).astype(out_ref.dtype)


def project(ctxs, wo_half, after, sections, dtype):
    rows = sections * ROWS
    depth, wide = wo_half.shape
    return pl.pallas_call(
        functools.partial(project_kernel, sections),
        out_shape=jax.ShapeDtypeStruct((rows, wide), dtype),
        in_specs=[VMEM_SPEC] * (sections + 1) + [ANY_SPEC] * len(after),
        out_specs=VMEM_SPEC,
        compiler_params=params(),
        cost_estimate=pl.CostEstimate(
            flops=rows * depth * wide * 2, bytes_accessed=depth * wide * 2, transcendentals=0
        ),
        name="project_half",
    )(*ctxs, wo_half, *after)


def spread_rows(flip, spread, rows, held, out_hbm, sem):
    y = jnp.dot(spread[...], rows[...], preferred_element_type=jnp.float32)
    for slot in range(held.shape[0]):
        held[slot] = y[slot * STEPS : (slot + 1) * STEPS].astype(held.dtype)
    copy = pltpu.make_async_copy(held, half_columns(out_hbm, flip), sem)
    copy.start()
    copy.wait()


def spread_own_kernel(done, spread, rows, done_o, ctx_in, out_hbm, ctx_hbm, held, sem, sems):
    del ctx_in
    copies = flushes(done, done_o, ctx_hbm, sems)
    for copy in copies:
        copy.start()
    spread_rows(False, spread, rows, held, out_hbm, sem)
    for copy in copies:
        copy.wait()


def spread_own(done, spread, rows, done_o, ctx, sections):
    shape = (sections * DSLOT, STEPS, rows.shape[1])
    return pl.pallas_call(
        functools.partial(spread_own_kernel, done),
        out_shape=[
            jax.ShapeDtypeStruct(shape[:2] + (2 * shape[2],), jnp.bfloat16),
            jax.ShapeDtypeStruct(ctx.shape, ctx.dtype),
        ],
        in_specs=[VMEM_SPEC] * 3 + [ANY_SPEC],
        out_specs=[ANY_SPEC] * 2,
        scratch_shapes=[
            pltpu.VMEM(shape, jnp.bfloat16),
            pltpu.SemaphoreType.DMA,
            pltpu.SemaphoreType.DMA((len(done),)),
        ],
        input_output_aliases={3: 1},
        compiler_params=params(),
        name="spread_own",
    )(spread, rows, done_o, ctx)


def spread_other_kernel(spread, rows, out_in, out_hbm, held, sem):
    del out_in
    spread_rows(True, spread, rows, held, out_hbm, sem)


def spread_other(spread, rows, out):
    shape = out.shape[:2] + (rows.shape[1],)
    return pl.pallas_call(
        spread_other_kernel,
        out_shape=jax.ShapeDtypeStruct(out.shape, out.dtype),
        in_specs=[VMEM_SPEC] * 2 + [ANY_SPEC],
        out_specs=ANY_SPEC,
        scratch_shapes=[pltpu.VMEM(shape, jnp.bfloat16), pltpu.SemaphoreType.DMA],
        input_output_aliases={2: 0},
        compiler_params=params(),
        name="spread_other",
    )(spread, rows, out)


def swap(x, axis, k):
    count = lax.axis_size(axis)
    return lax.ppermute(x, axis, [(i, i ^ k) for i in range(count)])


def per_device(prefill_q, kv_pool, decode_q, decode_kv, wo_weight, page_pair, slot_owner):
    sections = lax.axis_size("section")
    owner = slot_owner.reshape(-1)
    units = split_units(kv_pool.shape[2] // HEAD_DIM)
    ctx_shape = jax.ShapeDtypeStruct(prefill_q.shape, prefill_q.dtype)

    packed = pack(owner, decode_q, decode_kv, sections)
    got = [packed[0]] + [swap(packed[k], "section", k) for k in range(1, sections)]
    done_o, q_later, bias, keys, values, seen, pick, spread, wo_away = prefill_first(
        units[0], units[1] + units[2], page_pair, owner.reshape(1, -1), prefill_q, kv_pool, wo_weight, packed[0], sections
    )
    tables = (bias, keys, values)
    ctx = decode(seen, pick, keys, values, got, sections)
    ctxs = [ctx] + [swap(ctx, "section", k) for k in range(1, sections)]
    prefill_ctx, done_o, wo_keep = prefill_second(
        units[1], units[0], q_later, tables, done_o, wo_weight, ctx_shape, ctx
    )

    away = project(ctxs, wo_away, [wo_keep], sections, jnp.bfloat16)
    came = swap(away, "tensor", 1)
    keep = project(ctxs, wo_keep, [], sections, jnp.float32)
    chip = keep + came.astype(jnp.float32)
    k = 2
    while k < lax.axis_size("tensor"):
        far = swap(chip.astype(jnp.bfloat16), "tensor", k)
        if k == 2:
            prefill_ctx, done_o, chip = prefill_third(
                units[2], len(units[1]), units[1], q_later, tables, done_o, prefill_ctx, chip
            )
        chip = chip + far.astype(jnp.float32)
        k *= 2
    mine = chip.astype(jnp.bfloat16)
    other = swap(mine, "tensor", 1)
    decode_out, prefill_ctx = spread_own(units[2], spread, mine, done_o, prefill_ctx, sections)
    decode_out = spread_other(spread, other, decode_out)
    return (prefill_ctx, decode_out)


def solution(mesh):
    placed = (
        P(("groups", "section"), "tensor"),
        P(None, ("groups", "section"), "tensor"),
        P(("groups", "section"), None, "tensor"),
        P(None, ("groups", "section"), None, "tensor"),
        P("tensor", "section"),
        P("groups", None),
        P("groups", None),
    )
    return jax.shard_map(
        per_device,
        mesh=mesh,
        in_specs=placed,
        out_specs=(P(("groups", "section"), "tensor"), P("groups", None, "section")),
        check_vma=False,
    )
```

time: 127 us -> 32.8 us (0.26)
  waiting for transfers between devices: 40.6 us -> 5.15 us
  matrix products: 21.1 us -> 0 us
  other arithmetic: 19.6 us -> 0.06 us
  blocking collectives: 16 us -> 0 us
  local copies, waits for them, and re-layouts: 15.1 us -> 0 us
  Pallas kernels: 0 us -> 14.7 us
  between operations: 14.2 us -> 0.76 us
  starting transfers between devices: 0.08 us -> 11.9 us
    psum x1 -> x0, waiting for transfers between devices: 25.1 us -> none  [per_device(): decode_out = lax.psum(partial_out.astype(jnp.bfloat16), 'tensor')]
    dot_general x7 -> x0, matrix products: 21.1 us -> none  [the longest x1 8.21 us: per_device(): jnp.einsum('tkgh,skh->kgts', queries, cache_keys, preferred_element_type=...]
    sub x1 -> x0, other arithmetic: 16.2 us -> none  [per_device(): weights = jnp.where(allowed, jnp.exp(scores - row_max), 0.0)]
    all_gather x1 -> x0, blocking collectives: 16 us -> none  [per_device(): portion = lax.all_gather(contexts, 'section', axis=0, tiled=True)]
    all_gather x1 -> x0, waiting for transfers between devices: 15.4 us -> none  [per_device(): portion = lax.all_gather(kv_pool, 'section', axis=1, tiled=True)]
    pallas_call x0 -> x9, Pallas kernels: none -> 14.7 us  [the longest x1 3.51 us: prefill_first(): pl.pallas_call(functools.partial(first_kernel, units, later), out_shape=[...]
    ppermute x0 -> x9, starting transfers between devices: none -> 11.9 us  [swap(): return lax.ppermute(x, axis, [(i, i ^ k) for i in range(count)])]
    unnamed x6 -> x0, local copies, waits for them, and re-layouts: 8.9 us -> none
  transfers between devices with their start and end apart: 2 -> 9, of which waited for: 2 -> 5; matrix products, arithmetic and copies ran while one was open for 32% -> 0% of each run, Pallas kernels for 0% -> 34%
where the time goes in v2:
time: 32.8 us; the launch traced here: 32.5 us
  Pallas kernels  14.7 us (45%)
  starting transfers between devices  11.9 us (36%)
  waiting for transfers between devices  5.15 us (16%)
  between operations  0.76 us (2%)
    ppermute x9, starting transfers between devices, swap(): return lax.ppermute(x, axis, [(i, i ^ k) for i in range(count)])  11.9 us
    ppermute x9, waiting for transfers between devices, swap(): return lax.ppermute(x, axis, [(i, i ^ k) for i in range(count)])  5.15 us
    pallas_call x1, Pallas kernels, prefill_first(): pl.pallas_call(functools.partial(first_kernel, units, later), out_shape=[...  3.51 us
    pallas_call x1, Pallas kernels, prefill_second(): pl.pallas_call(functools.partial(second_kernel, units, done), out_shape=[...  3.13 us
    pallas_call x1, Pallas kernels, prefill_third(): pl.pallas_call(functools.partial(third_kernel, units, offset, done), out_...  2.48 us
    pallas_call x2, Pallas kernels, project(): pl.pallas_call(functools.partial(project_kernel, sections), out_shape=jax...  1.68 us
    pallas_call x1, Pallas kernels, spread_own(): pl.pallas_call(functools.partial(spread_own_kernel, done), out_shape=[jax...  1.11 us
    pallas_call x1, Pallas kernels, pack(): pl.pallas_call(functools.partial(pack_kernel, sections), out_shape=[jax.S...  0.99 us
  transfers between devices with their start and end apart: 9, of which 5 were waited for; matrix products, arithmetic and copies ran while one was open for 0% of the time, Pallas kernels for 34%

profile of v2, /device:TPU:0, one launch (start us, length us, event | category | flops | bytes accessed | tf_op | source)
XLA Modules:
  0.0 32.5 jit_solution(11733301112111556621)
XLA Ops:
  0.6 1.0 %pack_queries.1 = (bf16[2,4,2560]{2,1,0:T(4,128)(2,1)S(1)}, bf16[2,4,2560]{2,1,0:T(4,128)(2,1)S(1)}, bf16[2,4,2560]{2,1,0:T(4,128)(2,1)S(1)}, bf16[2,4,2560]{2,1,0:T(4,128)(2,1)S(1)}) custom-call(s32[16]{0:T(128)} %bitcast.2, bf16[8,4,2048]{2,1,0:T(4,128)(2,1)} %q_hbm.2, bf16[2,8,4,256]{3,2,1,0:T(4,128)(2,1)} %kv_hbm.2), custom_call_target="tpu_custom_call" | custom-call | tf_op jit(solution)/shard_map/pack_queries/pallas_call | solution.py:79
  1.6 3.1 %collective-permute-start = (bf16[2,4,2560]{2,1,0:T(4,128)(2,1)S(1)}, bf16[2,4,2560]{2,1,0:T(4,128)(2,1)S(1)}, u32[]{:S(2)}, u32[]{:S(2)}) collective-permute-start(bf16[2,4,2560]{2,1,0:T(4,128)(2,1)S(1)} %get-tuple-element.32), channel_id=1, source_target_pairs={{0,4},{4,0},{8,12},{12,8},{1,5},{5,1},{9,13},{13,9},{2,6},{6,2},{1... | collective-permute-start | bytes 122888 | tf_op jit(solution)/shard_map/ppermute | solution.py:472
  4.7 2.6 %collective-permute-start.1 = (bf16[2,4,2560]{2,1,0:T(4,128)(2,1)S(1)}, bf16[2,4,2560]{2,1,0:T(4,128)(2,1)S(1)}, u32[]{:S(2)}, u32[]{:S(2)}) collective-permute-start(bf16[2,4,2560]{2,1,0:T(4,128)(2,1)S(1)} %get-tuple-element.33), channel_id=1, source_target_pairs={{0,8},{4,12},{8,0},{12,4},{1,9},{5,13},{9,1},{13,5},{2,10},{6,14},... | collective-permute-start | bytes 122888 | tf_op jit(solution)/shard_map/ppermute | solution.py:472
  7.3 0.1 collective-permute-start.2
  7.3 3.5 %prefill_first.1 = (bf16[2,128,1024]{2,1,0:T(8,128)(2,1)S(1)}, bf16[6,128,1024]{2,1,0:T(8,128)(2,1)S(1)}, f32[4,128,384]{2,1,0:T(8,128)S(1)}, bf16[2,128,512]{2,...) custom-call(s32[4,32]{1,0:T(4,128)} %page_hbm.1, ...), custom_call_target="tpu_custom_call" | custom-call | flops 536870912 | bytes 1048576 | tf_op jit(solution)/shard_map/prefill_first/pallas_call | solution.py:265
  10.9 0.0 collective-permute-done.refs_1_
  10.9 0.0 collective-permute-done.1.refs_2_
  10.9 2.2 %collective-permute-done.2.refs_3_ = bf16[2,4,2560]{2,1,0:T(4,128)(2,1)S(1)} collective-permute-done((bf16[2,4,2560]{2,1,0:T(4,128)(2,1)S(1)}, bf16[2,4,2560]{2,1,0:T(4,128)(2,1)S(1)}, u32[]{:S(2)}, u32[]{:S(2)}) %collective-permute-start.2) | collective-permute-done | bytes 40992 | tf_op jit(solution)/shard_map/ppermute | solution.py:472
  13.1 0.9 %decode_attention.1.after.refs_0_ = bf16[16,2048]{1,0:T(8,128)(2,1)S(1)} custom-call(f32[16,512]{1,0:T(8,128)S(1)} %get-tuple-element.30.seen, bf16[16,32]{1,0:T(8,128)(2,1)S(1)} %get-tuple-element.31.pick, bf16[2,128,512]{2,1,0:T(8,128)(2,1)S(1)} %get-tuple-element.27.keys, bf16[2,512,256]{2,1,0:T(8,128)(2,1)S(1)} %get-tuple-element.28.values, ...), custom_call_target="tpu_custom_call" | custom-call | tf_op jit(solution)/shard_map/decode_attention/pallas_call | solution.py:378
  14.0 0.1 collective-permute-start.3
  14.1 2.1 %collective-permute-start.4 = (bf16[16,2048]{1,0:T(8,128)(2,1)S(1)}, bf16[16,2048]{1,0:T(8,128)(2,1)S(1)}, u32[]{:S(2)}, u32[]{:S(2)}) collective-permute-start(bf16[16,2048]{1,0:T(8,128)(2,1)S(1)} %decode_attention.1.after.refs_0_), channel_id=1, source_target_pairs={{0,8},{4,12},{8,0},{12,4},{1,9},{5,13},{9,1},{13,5},{2,10},{6,14},... | collective-permute-start | bytes 196616 | tf_op jit(solution)/shard_map/ppermute | solution.py:472
  16.2 2.3 %collective-permute-start.5 = (bf16[16,2048]{1,0:T(8,128)(2,1)S(1)}, bf16[16,2048]{1,0:T(8,128)(2,1)S(1)}, u32[]{:S(2)}, u32[]{:S(2)}) collective-permute-start(bf16[16,2048]{1,0:T(8,128)(2,1)S(1)} %decode_attention.1.after.refs_0_), channel_id=1, source_target_pairs={{0,12},{4,8},{8,4},{12,0},{1,13},{5,9},{9,5},{13,1},{2,14},{6,10},... | collective-permute-start | bytes 196616 | tf_op jit(solution)/shard_map/ppermute | solution.py:472
  18.4 3.1 %prefill_second.1 = (bf16[512,2048]{1,0:T(8,128)(2,1)}, bf16[2,128,1024]{2,1,0:T(8,128)(2,1)S(1)}, bf16[2048,1024]{1,0:T(8,128)(2,1)S(1)}) custom-call(bf16[6,128,1024]{2,1,0:T(8,128)(2,1)S(1)} %get-tuple-element.25.q, f32[4,128,384]{2,1,0:T(8,128)S(1)} %get-tuple-element.26.bias, bf16[2,128,512]{2,1,0:T(8,128)(2,1)S(1)} %get-tuple-element.27.keys, ...), custom_call_target="tpu_custom_call" | custom-call | flops 671088640 | bytes 1048576 | tf_op jit(solution)/shard_map/prefill_second/pallas_call | solution.py:296
  21.6 0.0 collective-permute-done.3.refs_1_
  21.6 0.0 collective-permute-done.4.refs_2_
  21.6 0.7 %collective-permute-done.5.refs_3_ = bf16[16,2048]{1,0:T(8,128)(2,1)S(1)} collective-permute-done((bf16[16,2048]{1,0:T(8,128)(2,1)S(1)}, bf16[16,2048]{1,0:T(8,128)(2,1)S(1)}, u32[]{:S(2)}, u32[]{:S(2)}) %collective-permute-start.5) | collective-permute-done | bytes 65568 | tf_op jit(solution)/shard_map/ppermute | solution.py:472
  22.2 0.8 %project_half.3 = bf16[64,1024]{1,0:T(8,128)(2,1)S(1)} custom-call(bf16[16,2048]{1,0:T(8,128)(2,1)S(1)} %decode_attention.1.after.refs_0_, bf16[16,2048]{1,0:T(8,128)(2,1)S(1)} %collective-permute-done.3.refs_1_, bf16[16,2048]{1,0:T(8,128)(2,1)S(1)} %collective-permute-done.4.refs_2_, bf16[16,2048]{1,0:T(8,128)(2,1)S(1)} %collective-permute-done.5.refs_3_, ...), custom_call_target="tpu_custom_call" | custom-call | flops 268435456 | bytes 4194304 | tf_op jit(solution)/shard_map/project_half/pallas_call | solution.py:398
  23.1 0.1 collective-permute-start.6
  23.2 0.8 %project_half.2 = f32[64,1024]{1,0:T(8,128)S(1)} custom-call(bf16[16,2048]{1,0:T(8,128)(2,1)S(1)} %decode_attention.1.after.refs_0_, bf16[16,2048]{1,0:T(8,128)(2,1)S(1)} %collective-permute-done.3.refs_1_, bf16[16,2048]{1,0:T(8,128)(2,1)S(1)} %collective-permute-done.4.refs_2_, bf16[16,2048]{1,0:T(8,128)(2,1)S(1)} %collective-permute-done.5.refs_3_, ...), custom_call_target="tpu_custom_call" | custom-call | flops 268435456 | bytes 4194304 | tf_op jit(solution)/shard_map/project_half/pallas_call | solution.py:398
  24.0 0.5 %collective-permute-done.6 = bf16[64,1024]{1,0:T(8,128)(2,1)S(1)} collective-permute-done((bf16[64,1024]{1,0:T(8,128)(2,1)S(1)}, bf16[64,1024]{1,0:T(8,128)(2,1)S(1)}, u32[]{:S(2)}, u32[]{:S(2)}) %collective-permute-start.6) | collective-permute-done | bytes 131104 | tf_op jit(solution)/shard_map/ppermute | solution.py:472
  24.5 1.6 %collective-permute-start.7 = (bf16[64,1024]{1,0:T(8,128)(2,1)S(1)}, bf16[64,1024]{1,0:T(8,128)(2,1)S(1)}, u32[]{:S(2)}, u32[]{:S(2)}) collective-permute-start(bf16[64,1024]{1,0:T(8,128)(2,1)S(1)} %get-tuple-element.44), channel_id=1, source_target_pairs={{0,2},{1,3},{2,0},{3,1},{4,6},{5,7},{6,4},{7,5},{8,10},{9,11},{10,... | collective-permute-start | bytes 393224 | tf_op jit(solution)/shard_map/ppermute | solution.py:472
  26.1 2.5 %prefill_third.1 = (bf16[512,2048]{1,0:T(8,128)(2,1)}, bf16[4,128,1024]{2,1,0:T(8,128)(2,1)S(1)}, f32[64,1024]{1,0:T(8,128)S(1)}) custom-call(bf16[6,128,1024]{2,1,0:T(8,128)(2,1)S(1)} %get-tuple-element.25.q, f32[4,128,384]{2,1,0:T(8,128)S(1)} %get-tuple-element.26.bias, ...), custom_call_target="tpu_custom_call", output_to_operand_aliasing={{0}: (5, {}), {2}: (6, {})} | custom-call | flops 1207959552 | bytes 2097152 | tf_op jit(solution)/shard_map/prefill_third/pallas_call | solution.py:313
  28.6 1.6 %collective-permute-done.7 = bf16[64,1024]{1,0:T(8,128)(2,1)S(1)} collective-permute-done((bf16[64,1024]{1,0:T(8,128)(2,1)S(1)}, bf16[64,1024]{1,0:T(8,128)(2,1)S(1)}, u32[]{:S(2)}, u32[]{:S(2)}) %collective-permute-start.7) | collective-permute-done | bytes 131104 | tf_op jit(solution)/shard_map/ppermute | solution.py:472
  30.2 0.1 collective-permute-start.8
  30.3 1.1 %spread_own.1 = (bf16[32,4,2048]{2,1,0:T(4,128)(2,1)}, bf16[512,2048]{1,0:T(8,128)(2,1)}) custom-call(bf16[128,64]{1,0:T(8,128)(2,1)S(1)} %get-tuple-element.24.spread, bf16[64,1024]{1,0:T(8,128)(2,1)S(1)} %add_convert_fusion.rows, bf16[4,128,1024]{2,1,0:T(8,128)(2,1)S(1)} %get-tuple-element.40.done_o, ...), custom_call_target="tpu_custom_call", output_to_operand_aliasing={{1}: (3, {})} | custom-call | tf_op jit(solution)/shard_map/spread_own/pallas_call | solution.py:432
  31.4 0.2 collective-permute-done.8.rows
  31.6 0.9 %spread_other.1 = bf16[32,4,2048]{2,1,0:T(4,128)(2,1)} custom-call(bf16[128,64]{1,0:T(8,128)(2,1)S(1)} %get-tuple-element.24.spread, bf16[64,1024]{1,0:T(8,128)(2,1)S(1)} %collective-permute-done.8.rows, bf16[32,4,2048]{2,1,0:T(4,128)(2,1)} %get-tuple-element.43.out_in), custom_call_target="tpu_custom_call", output_to_operand_aliasing={{}: (2, {})} | custom-call | tf_op jit(solution)/shard_map/spread_other/pallas_call | solution.py:458
  (2 shorter events, 0.1 us)
Async XLA Ops:
  1.6 9.2 %collective-permute-start = (bf16[2,4,2560]{2,1,0:T(4,128)(2,1)S(1)}, bf16[2,4,2560]{2,1,0:T(4,128)(2,1)S(1)}, u32[]{:S(2)}, u32[]{:S(2)}) collective-permute-start(bf16[2,4,2560]{2,1,0:T(4,128)(2,1)S(1)} %get-tuple-element.32), channel_id=1, source_target_pairs={{0,4},{4,0},{8,12},{12,8},{1,5},{5,1},{9,13},{13,9},{2,6},{6,2},{1... | collective-permute-start | bytes 122888 | tf_op jit(solution)/shard_map/ppermute | solution.py:472
  4.7 6.2 %collective-permute-start.1 = (bf16[2,4,2560]{2,1,0:T(4,128)(2,1)S(1)}, bf16[2,4,2560]{2,1,0:T(4,128)(2,1)S(1)}, u32[]{:S(2)}, u32[]{:S(2)}) collective-permute-start(bf16[2,4,2560]{2,1,0:T(4,128)(2,1)S(1)} %get-tuple-element.33), channel_id=1, source_target_pairs={{0,8},{4,12},{8,0},{12,4},{1,9},{5,13},{9,1},{13,5},{2,10},{6,14},... | collective-permute-start | bytes 122888 | tf_op jit(solution)/shard_map/ppermute | solution.py:472
  7.3 5.8 %collective-permute-start.2 = (bf16[2,4,2560]{2,1,0:T(4,128)(2,1)S(1)}, bf16[2,4,2560]{2,1,0:T(4,128)(2,1)S(1)}, u32[]{:S(2)}, u32[]{:S(2)}) collective-permute-start(bf16[2,4,2560]{2,1,0:T(4,128)(2,1)S(1)} %get-tuple-element.34), channel_id=1, source_target_pairs={{0,12},{4,8},{8,4},{12,0},{1,13},{5,9},{9,5},{13,1},{2,14},{6,10},... | collective-permute-start | bytes 122888 | tf_op jit(solution)/shard_map/ppermute | solution.py:472
  14.0 7.6 %collective-permute-start.3 = (bf16[16,2048]{1,0:T(8,128)(2,1)S(1)}, bf16[16,2048]{1,0:T(8,128)(2,1)S(1)}, u32[]{:S(2)}, u32[]{:S(2)}) collective-permute-start(bf16[16,2048]{1,0:T(8,128)(2,1)S(1)} %decode_attention.1.after.refs_0_), channel_id=1, source_target_pairs={{0,4},{4,0},{8,12},{12,8},{1,5},{5,1},{9,13},{13,9},{2,6},{6,2},{1... | collective-permute-start | bytes 196616 | tf_op jit(solution)/shard_map/ppermute | solution.py:472
  14.1 7.5 %collective-permute-start.4 = (bf16[16,2048]{1,0:T(8,128)(2,1)S(1)}, bf16[16,2048]{1,0:T(8,128)(2,1)S(1)}, u32[]{:S(2)}, u32[]{:S(2)}) collective-permute-start(bf16[16,2048]{1,0:T(8,128)(2,1)S(1)} %decode_attention.1.after.refs_0_), channel_id=1, source_target_pairs={{0,8},{4,12},{8,0},{12,4},{1,9},{5,13},{9,1},{13,5},{2,10},{6,14},... | collective-permute-start | bytes 196616 | tf_op jit(solution)/shard_map/ppermute | solution.py:472
  16.2 6.1 %collective-permute-start.5 = (bf16[16,2048]{1,0:T(8,128)(2,1)S(1)}, bf16[16,2048]{1,0:T(8,128)(2,1)S(1)}, u32[]{:S(2)}, u32[]{:S(2)}) collective-permute-start(bf16[16,2048]{1,0:T(8,128)(2,1)S(1)} %decode_attention.1.after.refs_0_), channel_id=1, source_target_pairs={{0,12},{4,8},{8,4},{12,0},{1,13},{5,9},{9,5},{13,1},{2,14},{6,10},... | collective-permute-start | bytes 196616 | tf_op jit(solution)/shard_map/ppermute | solution.py:472
  23.1 1.4 %collective-permute-start.6 = (bf16[64,1024]{1,0:T(8,128)(2,1)S(1)}, bf16[64,1024]{1,0:T(8,128)(2,1)S(1)}, u32[]{:S(2)}, u32[]{:S(2)}) collective-permute-start(bf16[64,1024]{1,0:T(8,128)(2,1)S(1)} %project_half.3), channel_id=1, source_target_pairs={{0,1},{1,0},{2,3},{3,2},{4,5},{5,4},{6,7},{7,6},{8,9},{9,8},{10,11... | collective-permute-start | bytes 393224 | tf_op jit(solution)/shard_map/ppermute | solution.py:472
  24.5 5.6 %collective-permute-start.7 = (bf16[64,1024]{1,0:T(8,128)(2,1)S(1)}, bf16[64,1024]{1,0:T(8,128)(2,1)S(1)}, u32[]{:S(2)}, u32[]{:S(2)}) collective-permute-start(bf16[64,1024]{1,0:T(8,128)(2,1)S(1)} %get-tuple-element.44), channel_id=1, source_target_pairs={{0,2},{1,3},{2,0},{3,1},{4,6},{5,7},{6,4},{7,5},{8,10},{9,11},{10,... | collective-permute-start | bytes 393224 | tf_op jit(solution)/shard_map/ppermute | solution.py:472
  30.2 1.4 %collective-permute-start.8 = (bf16[64,1024]{1,0:T(8,128)(2,1)S(1)}, bf16[64,1024]{1,0:T(8,128)(2,1)S(1)}, u32[]{:S(2)}, u32[]{:S(2)}) collective-permute-start(bf16[64,1024]{1,0:T(8,128)(2,1)S(1)} %add_convert_fusion.rows), channel_id=1, source_target_pairs={{0,1},{1,0},{2,3},{3,2},{4,5},{5,4},{6,7},{7,6},{8,9},{9,8},{10,11... | collective-permute-start | bytes 393224 | tf_op jit(solution)/shard_map/ppermute | solution.py:472

commit v3 on v2

--- a/solution.py
+++ b/solution.py
@@ -37,6 +37,17 @@
     return pltpu.with_memory_space_constraint(x, pltpu.HBM)
 
 
+def half_columns(ref, flip):
+    wide = ref.shape[-1] // 2
+    half = lax.axis_index("tensor") % 2
+    half = 1 - half if flip else half
+    return ref.at[(slice(None),) * (len(ref.shape) - 1) + (pl.ds(pl.multiple_of(half * wide, wide), wide),)]
+
+
+def half_shape(x):
+    return jax.ShapeDtypeStruct((*x.shape[:-1], x.shape[-1] // 2), x.dtype)
+
+
 def pack_kernel(sections, owner_hbm, q_hbm, kv_hbm, *refs):
     outs = refs[:sections]
     owner, q, kv, packed, sems = refs[sections:]
@@ -91,6 +102,10 @@
         compiler_params=params(),
         name="pack_queries",
     )(in_hbm(owner), in_hbm(decode_q), in_hbm(decode_kv))
+
+
+def in_order(arrays):
+    return [arrays[0], *arrays[:0:-1]]
 
 
 def pair_starts(page, here):
@@ -179,20 +194,13 @@
         o[:, g * HEAD_DIM : (g + 1) * HEAD_DIM] = y[g * BLOCK : (g + 1) * BLOCK]
 
 
-def half_columns(ref, flip):
-    wide = ref.shape[-1] // 2
-    half = lax.axis_index("tensor") % 2
-    half = 1 - half if flip else half
-    return ref.at[(slice(None),) * (len(ref.shape) - 1) + (pl.ds(pl.multiple_of(half * wide, wide), wide),)]
-
-
 def flushes(units, blocks, ctx_hbm, sems):
     return [pltpu.make_async_copy(blocks.at[n], region(ctx_hbm, u), sems.at[n]) for n, u in enumerate(units)]
 
 
 def first_kernel(
     units, later, page_hbm, owner_hbm, q_hbm, kv_hbm, wo_hbm, after,
-    o, q_later, bias, keys, values, seen, pick, spread, wo_away,
+    o, q_later, bias, keys, values, seen, pick, spread, wo_half,
     page, owner, kv, q, q_sems, late_sems, sems,
 ):
     del after
@@ -203,7 +211,7 @@
     cache = pltpu.make_async_copy(kv_hbm, kv, sems.at[2])
     soon = [pltpu.make_async_copy(region(q_hbm, u), q.at[n], q_sems.at[n]) for n, u in enumerate(units)]
     late = [pltpu.make_async_copy(region(q_hbm, u), q_later.at[n], late_sems.at[n]) for n, u in enumerate(later)]
-    weights = pltpu.make_async_copy(half_columns(wo_hbm, True), wo_away, sems.at[3])
+    weights = pltpu.make_async_copy(half_columns(wo_hbm, True), wo_half, sems.at[3])
     for copy in small + [cache] + soon + [weights] + late:
         copy.start()
     here = lax.axis_index("section")
@@ -226,25 +234,37 @@
         copy.wait()
 
 
-def second_kernel(units, done, q, bias, keys, values, done_o, wo_hbm, after, ctx_hbm, o, wo_keep, sems, wo_sem):
+def second_kernel(
+    units, later, done, q, bias, keys, values, done_o, q_hbm, wo_hbm, after,
+    ctx_hbm, o, q_later, wo_half, sems, late_sems, wo_sem,
+):
     del after
     copies = flushes(done, done_o, ctx_hbm, sems)
-    copies.append(pltpu.make_async_copy(half_columns(wo_hbm, False), wo_keep, wo_sem))
+    copies.append(pltpu.make_async_copy(half_columns(wo_hbm, False), wo_half, wo_sem))
+    copies += [pltpu.make_async_copy(region(q_hbm, u), q_later.at[n], late_sems.at[n]) for n, u in enumerate(later)]
     for copy in copies:
         copy.start()
-    for n, unit in enumerate(units):
-        attend(unit, q.at[n], bias, keys, values, o.at[n])
+
+    @beside
+    def _():
+        for n, unit in enumerate(units):
+            attend(unit, q.at[n], bias, keys, values, o.at[n])
+
     for copy in copies:
         copy.wait()
 
 
-def third_kernel(units, offset, done, q, bias, keys, values, done_o, ctx_in, chip_in, ctx_hbm, o, chip, sems):
+def third_kernel(units, done, q, bias, keys, values, done_o, ctx_in, chip_in, ctx_hbm, o, chip, sems):
     del ctx_in, chip_in, chip
     copies = flushes(done, done_o, ctx_hbm, sems)
     for copy in copies:
         copy.start()
-    for n, unit in enumerate(units):
-        attend(unit, q.at[offset + n], bias, keys, values, o.at[n])
+
+    @beside
+    def _():
+        for n, unit in enumerate(units):
+            attend(unit, q.at[n], bias, keys, values, o.at[n])
+
     for copy in copies:
         copy.wait()
 
@@ -254,6 +274,10 @@
     return pl.CostEstimate(
         flops=pairs * HEAD_DIM * 8, bytes_accessed=len(units) * BLOCK * GROUP * HEAD_DIM * 4, transcendentals=pairs
     )
+
+
+def beside(body):
+    pl.when(lax.axis_index("section") >= 0)(body)
 
 
 def block_shape(units):
@@ -273,7 +297,7 @@
             jax.ShapeDtypeStruct((ROWS, TOK_DEV), jnp.float32),
             jax.ShapeDtypeStruct((ROWS, sections * CAP * STEPS), jnp.bfloat16),
             jax.ShapeDtypeStruct((sections * DSLOT * STEPS, sections * ROWS), jnp.bfloat16),
-            jax.ShapeDtypeStruct((wo.shape[0], wo.shape[1] // 2), wo.dtype),
+            half_shape(wo),
         ],
         in_specs=[ANY_SPEC] * 6,
         out_specs=[VMEM_SPEC] * 9,
@@ -292,26 +316,31 @@
     )(in_hbm(page_pair), in_hbm(owner), in_hbm(prefill_q), in_hbm(kv_pool), in_hbm(wo), after)
 
 
-def prefill_second(units, done, q, tables, done_o, wo, ctx_shape, after):
-    return pl.pallas_call(
-        functools.partial(second_kernel, units, done),
+def prefill_second(units, later, done, q, tables, done_o, prefill_q, wo, after):
+    return pl.pallas_call(
+        functools.partial(second_kernel, units, later, done),
         out_shape=[
-            ctx_shape,
+            jax.ShapeDtypeStruct(prefill_q.shape, prefill_q.dtype),
             block_shape(units),
-            jax.ShapeDtypeStruct((wo.shape[0], wo.shape[1] // 2), wo.dtype),
-        ],
-        in_specs=[VMEM_SPEC] * 5 + [ANY_SPEC] * 2,
-        out_specs=[ANY_SPEC, VMEM_SPEC, VMEM_SPEC],
-        scratch_shapes=[pltpu.SemaphoreType.DMA((len(done),)), pltpu.SemaphoreType.DMA],
+            block_shape(later),
+            half_shape(wo),
+        ],
+        in_specs=[VMEM_SPEC] * 5 + [ANY_SPEC] * 3,
+        out_specs=[ANY_SPEC] + [VMEM_SPEC] * 3,
+        scratch_shapes=[
+            pltpu.SemaphoreType.DMA((len(done),)),
+            pltpu.SemaphoreType.DMA((len(later),)),
+            pltpu.SemaphoreType.DMA,
+        ],
         compiler_params=params(),
         cost_estimate=unit_cost(units),
         name="prefill_second",
-    )(q, *tables, done_o, in_hbm(wo), after)
-
-
-def prefill_third(units, offset, done, q, tables, done_o, ctx, chip):
-    return pl.pallas_call(
-        functools.partial(third_kernel, units, offset, done),
+    )(q, *tables, done_o, in_hbm(prefill_q), in_hbm(wo), after)
+
+
+def prefill_third(units, done, q, tables, done_o, ctx, chip):
+    return pl.pallas_call(
+        functools.partial(third_kernel, units, done),
         out_shape=[
             jax.ShapeDtypeStruct(ctx.shape, ctx.dtype),
             block_shape(units),
@@ -328,14 +357,14 @@
 
 
 def split_units(kv_local):
-    order = [(0, 0), (0, 3), (0, 1), (0, 2)]
+    order = [(0, 0), (0, 1), (0, 2), (0, 3)]
     units = [(k, i) for k in range(kv_local) for _, i in order]
     first, second = len(units) // 4, len(units) // 2
     return units[:first], units[first:second], units[second:]
 
 
 def decode_kernel(sections, seen, pick, keys, values, *refs):
-    got, ctx_ref, rows = refs[:sections], refs[sections], refs[sections + 1]
+    got, (ctx_ref, rows) = in_order(refs[:sections]), refs[sections:]
     kv_local = keys.shape[0]
     width = kv_local * GROUP * HEAD_DIM
     for k in range(sections):
@@ -383,11 +412,11 @@
         scratch_shapes=[pltpu.VMEM((sections * CAP * STEPS, block[2]), jnp.float32)],
         compiler_params=params(),
         name="decode_attention",
-    )(seen, pick, keys, values, *got)
+    )(seen, pick, keys, values, *in_order(got))
 
 
 def project_kernel(sections, *refs):
-    ctxs, wo, out_ref = refs[:sections], refs[sections], refs[-1]
+    ctxs, wo, out_ref = in_order(refs[:sections]), refs[sections], refs[-1]
     x = jnp.concatenate([c[...] for c in ctxs], axis=0)
     out_ref[...] = jnp.dot(x, wo[...], preferred_element_type=jnp.float32).astype(out_ref.dtype)
 
@@ -401,11 +430,9 @@
         in_specs=[VMEM_SPEC] * (sections + 1) + [ANY_SPEC] * len(after),
         out_specs=VMEM_SPEC,
         compiler_params=params(),
-        cost_estimate=pl.CostEstimate(
-            flops=rows * depth * wide * 2, bytes_accessed=depth * wide * 2, transcendentals=0
-        ),
+        cost_estimate=pl.CostEstimate(flops=rows * depth * wide * 2, bytes_accessed=depth * wide * 2, transcendentals=0),
         name="project_half",
-    )(*ctxs, wo_half, *after)
+    )(*in_order(ctxs), wo_half, *after)
 
 
 def spread_rows(flip, spread, rows, held, out_hbm, sem):
@@ -476,18 +503,17 @@
     sections = lax.axis_size("section")
     owner = slot_owner.reshape(-1)
     units = split_units(kv_pool.shape[2] // HEAD_DIM)
-    ctx_shape = jax.ShapeDtypeStruct(prefill_q.shape, prefill_q.dtype)
 
     packed = pack(owner, decode_q, decode_kv, sections)
     got = [packed[0]] + [swap(packed[k], "section", k) for k in range(1, sections)]
     done_o, q_later, bias, keys, values, seen, pick, spread, wo_away = prefill_first(
-        units[0], units[1] + units[2], page_pair, owner.reshape(1, -1), prefill_q, kv_pool, wo_weight, packed[0], sections
+        units[0], units[1], page_pair, owner.reshape(1, -1), prefill_q, kv_pool, wo_weight, packed[0], sections
     )
     tables = (bias, keys, values)
     ctx = decode(seen, pick, keys, values, got, sections)
     ctxs = [ctx] + [swap(ctx, "section", k) for k in range(1, sections)]
-    prefill_ctx, done_o, wo_keep = prefill_second(
-        units[1], units[0], q_later, tables, done_o, wo_weight, ctx_shape, ctx
+    prefill_ctx, done_o, q_later, wo_keep = prefill_second(
+        units[1], units[2], units[0], q_later, tables, done_o, prefill_q, wo_weight, ctx
     )
 
     away = project(ctxs, wo_away, [wo_keep], sections, jnp.bfloat16)
@@ -499,7 +525,7 @@
         far = swap(chip.astype(jnp.bfloat16), "tensor", k)
         if k == 2:
             prefill_ctx, done_o, chip = prefill_third(
-                units[2], len(units[1]), units[1], q_later, tables, done_o, prefill_ctx, chip
+                units[2], units[1], q_later, tables, done_o, prefill_ctx, chip
             )
         chip = chip + far.astype(jnp.float32)
         k *= 2

time: 32.8 us -> 31.3 us (0.954)
  Pallas kernels: 14.7 us -> 13.8 us
  waiting for transfers between devices: 5.15 us -> 4.56 us
    pallas_call x1, Pallas kernels: 3.51 us -> 2.77 us  [prefill_first(): pl.pallas_call(functools.partial(first_kernel, units, later), out_shape=[...]
    ppermute x9, waiting for transfers between devices: 5.15 us -> 4.56 us  [swap(): return lax.ppermute(x, axis, [(i, i ^ k) for i in range(count)])]
  transfers between devices with their start and end apart: 9 -> 9, of which waited for: 5 -> 5; matrix products, arithmetic and copies ran while one was open for 0% -> 0% of each run, Pallas kernels for 34% -> 32%
where the time goes in v3:
time: 31.3 us; the launch traced here: 30.9 us
  Pallas kernels  13.8 us (44%)
  starting transfers between devices  11.8 us (38%)
  waiting for transfers between devices  4.56 us (15%)
  between operations  0.74 us (2%)
    ppermute x9, starting transfers between devices, swap(): return lax.ppermute(x, axis, [(i, i ^ k) for i in range(count)])  11.8 us
    ppermute x9, waiting for transfers between devices, swap(): return lax.ppermute(x, axis, [(i, i ^ k) for i in range(count)])  4.56 us
    pallas_call x1, Pallas kernels, prefill_first(): pl.pallas_call(functools.partial(first_kernel, units, later), out_shape=[...  2.77 us
    pallas_call x1, Pallas kernels, prefill_second(): pl.pallas_call(functools.partial(second_kernel, units, later, done), out_...  2.76 us
    pallas_call x1, Pallas kernels, prefill_third(): pl.pallas_call(functools.partial(third_kernel, units, done), out_shape=[j...  2.52 us
    pallas_call x2, Pallas kernels, project(): pl.pallas_call(functools.partial(project_kernel, sections), out_shape=jax...  1.69 us
    pallas_call x1, Pallas kernels, pack(): pl.pallas_call(functools.partial(pack_kernel, sections), out_shape=[jax.S...  1.13 us
    pallas_call x1, Pallas kernels, spread_own(): pl.pallas_call(functools.partial(spread_own_kernel, done), out_shape=[jax...  1.11 us
  transfers between devices with their start and end apart: 9, of which 5 were waited for; matrix products, arithmetic and copies ran while one was open for 0% of the time, Pallas kernels for 32%

profile of v3, /device:TPU:0, one launch (start us, length us, event | category | flops | bytes accessed | tf_op | source)
XLA Modules:
  0.0 30.9 jit_solution(5109177144836160336)
XLA Ops:
  0.6 1.1 %pack_queries.1 = (bf16[2,4,2560]{2,1,0:T(4,128)(2,1)S(1)}, bf16[2,4,2560]{2,1,0:T(4,128)(2,1)S(1)}, bf16[2,4,2560]{2,1,0:T(4,128)(2,1)S(1)}, bf16[2,4,2560]{2,1,0:T(4,128)(2,1)S(1)}) custom-call(s32[16]{0:T(128)} %bitcast.2, bf16[8,4,2048]{2,1,0:T(4,128)(2,1)} %q_hbm.3, bf16[2,8,4,256]{3,2,1,0:T(4,128)(2,1)} %kv_hbm.2), custom_call_target="tpu_custom_call" | custom-call | tf_op jit(solution)/shard_map/pack_queries/pallas_call | solution.py:90
  1.8 5.0 %collective-permute-start = (bf16[2,4,2560]{2,1,0:T(4,128)(2,1)S(1)}, bf16[2,4,2560]{2,1,0:T(4,128)(2,1)S(1)}, u32[]{:S(2)}, u32[]{:S(2)}) collective-permute-start(bf16[2,4,2560]{2,1,0:T(4,128)(2,1)S(1)} %get-tuple-element.33), channel_id=1, source_target_pairs={{0,12},{4,8},{8,4},{12,0},{1,13},{5,9},{9,5},{13,1},{2,14},{6,10},... | collective-permute-start | bytes 122888 | tf_op jit(solution)/shard_map/ppermute | solution.py:499
  6.7 0.0 collective-permute-start.1
  6.7 0.6 %collective-permute-start.2 = (bf16[2,4,2560]{2,1,0:T(4,128)(2,1)S(1)}, bf16[2,4,2560]{2,1,0:T(4,128)(2,1)S(1)}, u32[]{:S(2)}, u32[]{:S(2)}) collective-permute-start(bf16[2,4,2560]{2,1,0:T(4,128)(2,1)S(1)} %get-tuple-element.35), channel_id=1, source_target_pairs={{0,4},{4,0},{8,12},{12,8},{1,5},{5,1},{9,13},{13,9},{2,6},{6,2},{1... | collective-permute-start | bytes 122888 | tf_op jit(solution)/shard_map/ppermute | solution.py:499
  7.4 2.8 %prefill_first.1 = (bf16[2,128,1024]{2,1,0:T(8,128)(2,1)S(1)}, bf16[2,128,1024]{2,1,0:T(8,128)(2,1)S(1)}, f32[4,128,384]{2,1,0:T(8,128)S(1)}, bf16[2,128,512]{2,...) custom-call(s32[4,32]{1,0:T(4,128)} %page_hbm.1, ...), custom_call_target="tpu_custom_call" | custom-call | flops 402653184 | bytes 1048576 | tf_op jit(solution)/shard_map/prefill_first/pallas_call | solution.py:289
  10.2 0.0 collective-permute-done.refs_1_
  10.2 1.5 %collective-permute-done.1.refs_2_ = bf16[2,4,2560]{2,1,0:T(4,128)(2,1)S(1)} collective-permute-done((bf16[2,4,2560]{2,1,0:T(4,128)(2,1)S(1)}, bf16[2,4,2560]{2,1,0:T(4,128)(2,1)S(1)}, u32[]{:S(2)}, u32[]{:S(2)}) %collective-permute-start.1) | collective-permute-done | bytes 40992 | tf_op jit(solution)/shard_map/ppermute | solution.py:499
  11.6 0.0 collective-permute-done.2.refs_3_
  11.6 0.9 %decode_attention.1.after.refs_0_ = bf16[16,2048]{1,0:T(8,128)(2,1)S(1)} custom-call(f32[16,512]{1,0:T(8,128)S(1)} %get-tuple-element.31.seen, bf16[16,32]{1,0:T(8,128)(2,1)S(1)} %get-tuple-element.32.pick, bf16[2,128,512]{2,1,0:T(8,128)(2,1)S(1)} %get-tuple-element.28.keys, bf16[2,512,256]{2,1,0:T(8,128)(2,1)S(1)} %get-tuple-element.29.values, ...), custom_call_target="tpu_custom_call" | custom-call | tf_op jit(solution)/shard_map/decode_attention/pallas_call | solution.py:407
  12.5 2.4 %collective-permute-start.3 = (bf16[16,2048]{1,0:T(8,128)(2,1)S(1)}, bf16[16,2048]{1,0:T(8,128)(2,1)S(1)}, u32[]{:S(2)}, u32[]{:S(2)}) collective-permute-start(bf16[16,2048]{1,0:T(8,128)(2,1)S(1)} %decode_attention.1.after.refs_0_), channel_id=1, source_target_pairs={{0,12},{4,8},{8,4},{12,0},{1,13},{5,9},{9,5},{13,1},{2,14},{6,10},... | collective-permute-start | bytes 196616 | tf_op jit(solution)/shard_map/ppermute | solution.py:499
  14.9 0.0 collective-permute-start.4
  14.9 2.1 %collective-permute-start.5 = (bf16[16,2048]{1,0:T(8,128)(2,1)S(1)}, bf16[16,2048]{1,0:T(8,128)(2,1)S(1)}, u32[]{:S(2)}, u32[]{:S(2)}) collective-permute-start(bf16[16,2048]{1,0:T(8,128)(2,1)S(1)} %decode_attention.1.after.refs_0_), channel_id=1, source_target_pairs={{0,4},{4,0},{8,12},{12,8},{1,5},{5,1},{9,13},{13,9},{2,6},{6,2},{1... | collective-permute-start | bytes 196616 | tf_op jit(solution)/shard_map/ppermute | solution.py:499
  17.0 2.8 %prefill_second.1 = (bf16[512,2048]{1,0:T(8,128)(2,1)}, bf16[2,128,1024]{2,1,0:T(8,128)(2,1)S(1)}, bf16[4,128,1024]{2,1,0:T(8,128)(2,1)S(1)}, bf16[2048,1024]{1,0:T(8,128)(2,1)S(1)}) custom-call(bf16[2,128,1024]{2,1,0:T(8,128)(2,1)S(1)} %get-tuple-element.26.q, f32[4,128,384]{2,1,0:T(8,128)S(1)} %get-tuple-element.27.bias, ...), custom_call_target="tpu_custom_call" | custom-call | flops 805306368 | bytes 1048576 | tf_op jit(solution)/shard_map/prefill_second/pallas_call | solution.py:320
  19.8 0.0 collective-permute-done.3.refs_1_
  19.8 0.8 %collective-permute-done.4.refs_2_ = bf16[16,2048]{1,0:T(8,128)(2,1)S(1)} collective-permute-done((bf16[16,2048]{1,0:T(8,128)(2,1)S(1)}, bf16[16,2048]{1,0:T(8,128)(2,1)S(1)}, u32[]{:S(2)}, u32[]{:S(2)}) %collective-permute-start.4) | collective-permute-done | bytes 65568 | tf_op jit(solution)/shard_map/ppermute | solution.py:499
  20.6 0.0 collective-permute-done.5.refs_3_
  20.6 0.8 %project_half.3 = bf16[64,1024]{1,0:T(8,128)(2,1)S(1)} custom-call(bf16[16,2048]{1,0:T(8,128)(2,1)S(1)} %decode_attention.1.after.refs_0_, bf16[16,2048]{1,0:T(8,128)(2,1)S(1)} %collective-permute-done.3.refs_1_, bf16[16,2048]{1,0:T(8,128)(2,1)S(1)} %collective-permute-done.4.refs_2_, bf16[16,2048]{1,0:T(8,128)(2,1)S(1)} %collective-permute-done.5.refs_3_, ...), custom_call_target="tpu_custom_call" | custom-call | flops 268435456 | bytes 4194304 | tf_op jit(solution)/shard_map/project_half/pallas_call | solution.py:427
  21.5 0.1 collective-permute-start.6
  21.5 0.8 %project_half.2 = f32[64,1024]{1,0:T(8,128)S(1)} custom-call(bf16[16,2048]{1,0:T(8,128)(2,1)S(1)} %decode_attention.1.after.refs_0_, bf16[16,2048]{1,0:T(8,128)(2,1)S(1)} %collective-permute-done.3.refs_1_, bf16[16,2048]{1,0:T(8,128)(2,1)S(1)} %collective-permute-done.4.refs_2_, bf16[16,2048]{1,0:T(8,128)(2,1)S(1)} %collective-permute-done.5.refs_3_, ...), custom_call_target="tpu_custom_call" | custom-call | flops 268435456 | bytes 4194304 | tf_op jit(solution)/shard_map/project_half/pallas_call | solution.py:427
  22.4 0.5 %collective-permute-done.6 = bf16[64,1024]{1,0:T(8,128)(2,1)S(1)} collective-permute-done((bf16[64,1024]{1,0:T(8,128)(2,1)S(1)}, bf16[64,1024]{1,0:T(8,128)(2,1)S(1)}, u32[]{:S(2)}, u32[]{:S(2)}) %collective-permute-start.6) | collective-permute-done | bytes 131104 | tf_op jit(solution)/shard_map/ppermute | solution.py:499
  22.9 1.6 %collective-permute-start.7 = (bf16[64,1024]{1,0:T(8,128)(2,1)S(1)}, bf16[64,1024]{1,0:T(8,128)(2,1)S(1)}, u32[]{:S(2)}, u32[]{:S(2)}) collective-permute-start(bf16[64,1024]{1,0:T(8,128)(2,1)S(1)} %get-tuple-element.46), channel_id=1, source_target_pairs={{0,2},{1,3},{2,0},{3,1},{4,6},{5,7},{6,4},{7,5},{8,10},{9,11},{10,... | collective-permute-start | bytes 393224 | tf_op jit(solution)/shard_map/ppermute | solution.py:499
  24.5 2.5 %prefill_third.1 = (bf16[512,2048]{1,0:T(8,128)(2,1)}, bf16[4,128,1024]{2,1,0:T(8,128)(2,1)S(1)}, f32[64,1024]{1,0:T(8,128)S(1)}) custom-call(bf16[4,128,1024]{2,1,0:T(8,128)(2,1)S(1)} %get-tuple-element.36.q, f32[4,128,384]{2,1,0:T(8,128)S(1)} %get-tuple-element.27.bias, ...), custom_call_target="tpu_custom_call", output_to_operand_aliasing={{0}: (5, {}), {2}: (6, {})} | custom-call | flops 1207959552 | bytes 2097152 | tf_op jit(solution)/shard_map/prefill_third/pallas_call | solution.py:342
  27.0 1.5 %collective-permute-done.7 = bf16[64,1024]{1,0:T(8,128)(2,1)S(1)} collective-permute-done((bf16[64,1024]{1,0:T(8,128)(2,1)S(1)}, bf16[64,1024]{1,0:T(8,128)(2,1)S(1)}, u32[]{:S(2)}, u32[]{:S(2)}) %collective-permute-start.7) | collective-permute-done | bytes 131104 | tf_op jit(solution)/shard_map/ppermute | solution.py:499
  28.6 0.1 collective-permute-start.8
  28.6 1.1 %spread_own.1 = (bf16[32,4,2048]{2,1,0:T(4,128)(2,1)}, bf16[512,2048]{1,0:T(8,128)(2,1)}) custom-call(bf16[128,64]{1,0:T(8,128)(2,1)S(1)} %get-tuple-element.25.spread, bf16[64,1024]{1,0:T(8,128)(2,1)S(1)} %add_convert_fusion.rows, bf16[4,128,1024]{2,1,0:T(8,128)(2,1)S(1)} %get-tuple-element.42.done_o, ...), custom_call_target="tpu_custom_call", output_to_operand_aliasing={{1}: (3, {})} | custom-call | tf_op jit(solution)/shard_map/spread_own/pallas_call | solution.py:459
  29.8 0.2 collective-permute-done.8.rows
  30.0 0.9 %spread_other.1 = bf16[32,4,2048]{2,1,0:T(4,128)(2,1)} custom-call(bf16[128,64]{1,0:T(8,128)(2,1)S(1)} %get-tuple-element.25.spread, bf16[64,1024]{1,0:T(8,128)(2,1)S(1)} %collective-permute-done.8.rows, bf16[32,4,2048]{2,1,0:T(4,128)(2,1)} %get-tuple-element.45.out_in), custom_call_target="tpu_custom_call", output_to_operand_aliasing={{}: (2, {})} | custom-call | tf_op jit(solution)/shard_map/spread_other/pallas_call | solution.py:485
  (2 shorter events, 0.1 us)
Async XLA Ops:
  1.8 8.4 %collective-permute-start = (bf16[2,4,2560]{2,1,0:T(4,128)(2,1)S(1)}, bf16[2,4,2560]{2,1,0:T(4,128)(2,1)S(1)}, u32[]{:S(2)}, u32[]{:S(2)}) collective-permute-start(bf16[2,4,2560]{2,1,0:T(4,128)(2,1)S(1)} %get-tuple-element.33), channel_id=1, source_target_pairs={{0,12},{4,8},{8,4},{12,0},{1,13},{5,9},{9,5},{13,1},{2,14},{6,10},... | collective-permute-start | bytes 122888 | tf_op jit(solution)/shard_map/ppermute | solution.py:499
  6.7 4.9 %collective-permute-start.1 = (bf16[2,4,2560]{2,1,0:T(4,128)(2,1)S(1)}, bf16[2,4,2560]{2,1,0:T(4,128)(2,1)S(1)}, u32[]{:S(2)}, u32[]{:S(2)}) collective-permute-start(bf16[2,4,2560]{2,1,0:T(4,128)(2,1)S(1)} %get-tuple-element.34), channel_id=1, source_target_pairs={{0,8},{4,12},{8,0},{12,4},{1,9},{5,13},{9,1},{13,5},{2,10},{6,14},... | collective-permute-start | bytes 122888 | tf_op jit(solution)/shard_map/ppermute | solution.py:499
  6.7 4.9 %collective-permute-start.2 = (bf16[2,4,2560]{2,1,0:T(4,128)(2,1)S(1)}, bf16[2,4,2560]{2,1,0:T(4,128)(2,1)S(1)}, u32[]{:S(2)}, u32[]{:S(2)}) collective-permute-start(bf16[2,4,2560]{2,1,0:T(4,128)(2,1)S(1)} %get-tuple-element.35), channel_id=1, source_target_pairs={{0,4},{4,0},{8,12},{12,8},{1,5},{5,1},{9,13},{13,9},{2,6},{6,2},{1... | collective-permute-start | bytes 122888 | tf_op jit(solution)/shard_map/ppermute | solution.py:499
  12.5 7.2 %collective-permute-start.3 = (bf16[16,2048]{1,0:T(8,128)(2,1)S(1)}, bf16[16,2048]{1,0:T(8,128)(2,1)S(1)}, u32[]{:S(2)}, u32[]{:S(2)}) collective-permute-start(bf16[16,2048]{1,0:T(8,128)(2,1)S(1)} %decode_attention.1.after.refs_0_), channel_id=1, source_target_pairs={{0,12},{4,8},{8,4},{12,0},{1,13},{5,9},{9,5},{13,1},{2,14},{6,10},... | collective-permute-start | bytes 196616 | tf_op jit(solution)/shard_map/ppermute | solution.py:499
  14.9 5.7 %collective-permute-start.4 = (bf16[16,2048]{1,0:T(8,128)(2,1)S(1)}, bf16[16,2048]{1,0:T(8,128)(2,1)S(1)}, u32[]{:S(2)}, u32[]{:S(2)}) collective-permute-start(bf16[16,2048]{1,0:T(8,128)(2,1)S(1)} %decode_attention.1.after.refs_0_), channel_id=1, source_target_pairs={{0,8},{4,12},{8,0},{12,4},{1,9},{5,13},{9,1},{13,5},{2,10},{6,14},... | collective-permute-start | bytes 196616 | tf_op jit(solution)/shard_map/ppermute | solution.py:499
  14.9 5.7 %collective-permute-start.5 = (bf16[16,2048]{1,0:T(8,128)(2,1)S(1)}, bf16[16,2048]{1,0:T(8,128)(2,1)S(1)}, u32[]{:S(2)}, u32[]{:S(2)}) collective-permute-start(bf16[16,2048]{1,0:T(8,128)(2,1)S(1)} %decode_attention.1.after.refs_0_), channel_id=1, source_target_pairs={{0,4},{4,0},{8,12},{12,8},{1,5},{5,1},{9,13},{13,9},{2,6},{6,2},{1... | collective-permute-start | bytes 196616 | tf_op jit(solution)/shard_map/ppermute | solution.py:499
  21.5 1.4 %collective-permute-start.6 = (bf16[64,1024]{1,0:T(8,128)(2,1)S(1)}, bf16[64,1024]{1,0:T(8,128)(2,1)S(1)}, u32[]{:S(2)}, u32[]{:S(2)}) collective-permute-start(bf16[64,1024]{1,0:T(8,128)(2,1)S(1)} %project_half.3), channel_id=1, source_target_pairs={{0,1},{1,0},{2,3},{3,2},{4,5},{5,4},{6,7},{7,6},{8,9},{9,8},{10,11... | collective-permute-start | bytes 393224 | tf_op jit(solution)/shard_map/ppermute | solution.py:499
  22.9 5.6 %collective-permute-start.7 = (bf16[64,1024]{1,0:T(8,128)(2,1)S(1)}, bf16[64,1024]{1,0:T(8,128)(2,1)S(1)}, u32[]{:S(2)}, u32[]{:S(2)}) collective-permute-start(bf16[64,1024]{1,0:T(8,128)(2,1)S(1)} %get-tuple-element.46), channel_id=1, source_target_pairs={{0,2},{1,3},{2,0},{3,1},{4,6},{5,7},{6,4},{7,5},{8,10},{9,11},{10,... | collective-permute-start | bytes 393224 | tf_op jit(solution)/shard_map/ppermute | solution.py:499
  28.6 1.4 %collective-permute-start.8 = (bf16[64,1024]{1,0:T(8,128)(2,1)S(1)}, bf16[64,1024]{1,0:T(8,128)(2,1)S(1)}, u32[]{:S(2)}, u32[]{:S(2)}) collective-permute-start(bf16[64,1024]{1,0:T(8,128)(2,1)S(1)} %add_convert_fusion.rows), channel_id=1, source_target_pairs={{0,1},{1,0},{2,3},{3,2},{4,5},{5,4},{6,7},{7,6},{8,9},{9,8},{10,11... | collective-permute-start | bytes 393224 | tf_op jit(solution)/shard_map/ppermute | solution.py:499

commit v4 on v3

--- a/solution.py
+++ b/solution.py
@@ -37,6 +37,40 @@
     return pltpu.with_memory_space_constraint(x, pltpu.HBM)
 
 
+FIRST_ROUND = ((0, 1, 2, 3), (1, 3, 0, 2), (3, 2, 1, 0), (2, 0, 3, 1))
+SECOND_ROUND = ((0, 1, 2, 3), (3, 2, 1, 0), (2, 3, 0, 1), (1, 0, 3, 2))
+
+
+def routes(table, sections):
+    if sections == len(table):
+        return table
+    return tuple(tuple(i ^ k for i in range(sections)) for k in range(sections))
+
+
+def back(route):
+    return tuple(route.index(i) for i in range(len(route)))
+
+
+def entry(route, here):
+    if all(to == i ^ route[0] for i, to in enumerate(route)):
+        return here ^ route[0]
+    value = jnp.int32(route[0])
+    for i, to in enumerate(route[1:], 1):
+        value = jnp.where(here == i, to, value)
+    return value
+
+
+def arrival(round_routes, here, source):
+    at = jnp.zeros_like(source)
+    for k, route in enumerate(round_routes):
+        at = at + jnp.where(source == entry(back(route), here), k, 0)
+    return at
+
+
+def send(x, route):
+    return lax.ppermute(x, "section", list(enumerate(route)))
+
+
 def half_columns(ref, flip):
     wide = ref.shape[-1] // 2
     half = lax.axis_index("tensor") % 2
@@ -48,9 +82,13 @@
     return jax.ShapeDtypeStruct((*x.shape[:-1], x.shape[-1] // 2), x.dtype)
 
 
+def beside(body):
+    pl.when(lax.axis_index("section") >= 0)(body)
+
+
 def pack_kernel(sections, owner_hbm, q_hbm, kv_hbm, *refs):
     outs = refs[:sections]
-    owner, q, kv, packed, sems = refs[sections:]
+    owner, before, q, kv, sems = refs[sections:]
     copies = [
         pltpu.make_async_copy(owner_hbm, owner, sems.at[0]),
         pltpu.make_async_copy(q_hbm, q, sems.at[1]),
@@ -60,28 +98,28 @@
         copy.start()
     here = lax.axis_index("section")
     width, kv_width = q.shape[2], kv.shape[3]
-    packed[...] = jnp.zeros_like(packed)
-    for copy in copies:
+    for k in range(sections):
+        outs[k][...] = jnp.zeros_like(outs[k])
+    copies[0].wait()
+
+    def place(pair, slot):
+        before[pair] = slot
+        return slot + (owner[pair] == here).astype(jnp.int32)
+
+    lax.fori_loop(0, owner.shape[0], place, jnp.int32(0), unroll=min(owner.shape[0], 16))
+    for copy in copies[1:]:
         copy.wait()
-
-    def place(pair, carry):
-        slot, rank = carry
-        rank = jnp.where(pair % PAIRS_DEV == 0, 0, rank)
-        mine = owner[pair] == here
-
-        @pl.when(mine)
-        def _():
-            to = (pair // PAIRS_DEV) ^ here
-            packed[to, rank, :, :width] = q[slot]
-            packed[to, rank, :, width : width + kv_width] = kv[0, slot]
-            packed[to, rank, :, width + kv_width :] = kv[1, slot]
-
-        step = mine.astype(jnp.int32)
-        return slot + step, rank + step
-
-    lax.fori_loop(0, owner.shape[0], place, (jnp.int32(0), jnp.int32(0)))
     for k in range(sections):
-        outs[k][...] = packed[k]
+        home = entry(routes(FIRST_ROUND, sections)[k], here) * PAIRS_DEV
+        for j in range(PAIRS_DEV):
+
+            @pl.when(owner[home + j] == here)
+            def _():
+                slot = before[home + j]
+                rank = slot - before[home]
+                outs[k][rank, :, :width] = q[slot]
+                outs[k][rank, :, width : width + kv_width] = kv[0, slot]
+                outs[k][rank, :, width + kv_width :] = kv[1, slot]
 
 
 def pack(owner, decode_q, decode_kv, sections):
@@ -94,18 +132,14 @@
         out_specs=[VMEM_SPEC] * sections,
         scratch_shapes=[
             pltpu.SMEM(owner.shape, jnp.int32),
+            pltpu.SMEM(owner.shape, jnp.int32),
             pltpu.VMEM(decode_q.shape, jnp.bfloat16),
             pltpu.VMEM(decode_kv.shape, jnp.bfloat16),
-            pltpu.VMEM((sections,) + block, jnp.bfloat16),
             pltpu.SemaphoreType.DMA((3,)),
         ],
         compiler_params=params(),
         name="pack_queries",
     )(in_hbm(owner), in_hbm(decode_q), in_hbm(decode_kv))
-
-
-def in_order(arrays):
-    return [arrays[0], *arrays[:0:-1]]
 
 
 def pair_starts(page, here):
@@ -140,33 +174,40 @@
     bias[...] = jnp.where((col >= first) & (col < last), 0.0, MASKED)
 
 
-def owner_tables(owner, here, pick, spread):
+def owner_grid(owner):
     pairs = owner.shape[1]
     down = lax.broadcasted_iota(jnp.int32, (pairs, pairs), 0)
     along = lax.broadcasted_iota(jnp.int32, (pairs, pairs), 1)
     owner_along = jnp.broadcast_to(owner[...], (pairs, pairs))
     owner_down = jnp.sum(jnp.where(down == along, owner_along, 0), axis=1, keepdims=True)
-    same = owner_along == owner_down
-    slot_rank = jnp.sum(jnp.where(same & (down < along), 1, 0), axis=0, keepdims=True)
-    slot = owner[...] * DSLOT + slot_rank
-
+    return down, along, owner_down, owner_along == owner_down
+
+
+def home_rows(sections, owner, here, pick):
+    down, along, owner_down, same = owner_grid(owner)
     at_home = down // PAIRS_DEV == along // PAIRS_DEV
     home_rank = jnp.sum(jnp.where(same & at_home & (along < down), 1, 0), axis=1, keepdims=True)
-    base = ((owner_down ^ here) * CAP + home_rank) * STEPS
+    base = (arrival(routes(FIRST_ROUND, sections), here, owner_down) * CAP + home_rank) * STEPS
     row = lax.broadcasted_iota(jnp.int32, pick.shape, 0)
     col = lax.broadcasted_iota(jnp.int32, pick.shape, 1)
-    pair = lax.broadcasted_iota(jnp.int32, (pairs, 1), 0)
+    pair = lax.broadcasted_iota(jnp.int32, base.shape, 0)
     at = row % STEPS
     for j in range(PAIRS_DEV):
         mine = jnp.sum(jnp.where(pair == here * PAIRS_DEV + j, base, 0), axis=0, keepdims=True)
         at = at + jnp.where(row // STEPS == j, mine, 0)
     pick[...] = (col == at).astype(jnp.float32).astype(pick.dtype)
 
-    wide = spread.shape[1]
-    pair = lax.broadcasted_iota(jnp.int32, (pairs, wide), 0)
-    place = lax.broadcasted_iota(jnp.int32, (pairs, wide), 1) // STEPS
-    holds = place == ((pair // PAIRS_DEV) ^ here) * PAIRS_DEV + pair % PAIRS_DEV
-    slot_down = jnp.sum(jnp.where(down == along, jnp.broadcast_to(slot, (pairs, pairs)), 0), axis=1, keepdims=True)
+
+def slot_rows(sections, owner, here, spread):
+    down, along, _, same = owner_grid(owner)
+    slot_rank = jnp.sum(jnp.where(same & (down < along), 1, 0), axis=0, keepdims=True)
+    slot_along = jnp.broadcast_to(owner[...] * DSLOT + slot_rank, down.shape)
+    slot_down = jnp.sum(jnp.where(down == along, slot_along, 0), axis=1, keepdims=True)
+    shape = (down.shape[0], spread.shape[1])
+    pair = lax.broadcasted_iota(jnp.int32, shape, 0)
+    place = lax.broadcasted_iota(jnp.int32, shape, 1) // STEPS
+    position = arrival(routes(SECOND_ROUND, sections), here, pair // PAIRS_DEV)
+    holds = place == position * PAIRS_DEV + pair % PAIRS_DEV
     slot_of_place = jnp.sum(jnp.where(holds, slot_down, 0), axis=0, keepdims=True)
     row = lax.broadcasted_iota(jnp.int32, spread.shape, 0)
     col = lax.broadcasted_iota(jnp.int32, spread.shape, 1)
@@ -198,55 +239,51 @@
     return [pltpu.make_async_copy(blocks.at[n], region(ctx_hbm, u), sems.at[n]) for n, u in enumerate(units)]
 
 
-def first_kernel(
-    units, later, page_hbm, owner_hbm, q_hbm, kv_hbm, wo_hbm, after,
-    o, q_later, bias, keys, values, seen, pick, spread, wo_half,
-    page, owner, kv, q, q_sems, late_sems, sems,
+def tables_kernel(
+    sections, units, page_hbm, owner_hbm, kv_hbm, q_hbm, after,
+    page, owner, keys, values, seen, pick, q, kv, sems, q_sems,
 ):
     del after
-    small = [
+    copies = [
         pltpu.make_async_copy(page_hbm, page, sems.at[0]),
         pltpu.make_async_copy(owner_hbm, owner, sems.at[1]),
+        pltpu.make_async_copy(kv_hbm, kv, sems.at[2]),
     ]
-    cache = pltpu.make_async_copy(kv_hbm, kv, sems.at[2])
-    soon = [pltpu.make_async_copy(region(q_hbm, u), q.at[n], q_sems.at[n]) for n, u in enumerate(units)]
-    late = [pltpu.make_async_copy(region(q_hbm, u), q_later.at[n], late_sems.at[n]) for n, u in enumerate(later)]
-    weights = pltpu.make_async_copy(half_columns(wo_hbm, True), wo_half, sems.at[3])
-    for copy in small + [cache] + soon + [weights] + late:
+    later = [pltpu.make_async_copy(region(q_hbm, u), q.at[n], q_sems.at[n]) for n, u in enumerate(units)]
+    for copy in copies + later:
         copy.start()
     here = lax.axis_index("section")
-    for copy in small:
+    for copy in copies:
         copy.wait()
-    starts = pair_starts(page, here)
-    prefill_masks(starts, bias)
-    decode_masks(starts, seen)
-    owner_tables(owner, here, pick, spread)
-    cache.wait()
-    for k in range(keys.shape[0]):
-        cols = slice(k * HEAD_DIM, (k + 1) * HEAD_DIM)
-        keys[k] = kv[0, :, cols].astype(jnp.float32).T.astype(jnp.bfloat16)
-        values[k, :, :HEAD_DIM] = kv[1, :, cols]
-        values[k, :, HEAD_DIM:] = jnp.ones((TOK_DEV, HEAD_DIM), jnp.bfloat16)
-    for n, unit in enumerate(units):
-        soon[n].wait()
-        attend(unit, q.at[n], bias, keys, values, o.at[n])
-    for copy in late + [weights]:
+
+    @beside
+    def _():
+        decode_masks(pair_starts(page, here), seen)
+        home_rows(sections, owner, here, pick)
+        for k in range(keys.shape[0]):
+            cols = slice(k * HEAD_DIM, (k + 1) * HEAD_DIM)
+            keys[k] = kv[0, :, cols].astype(jnp.float32).T.astype(jnp.bfloat16)
+            values[k, :, :HEAD_DIM] = kv[1, :, cols]
+            values[k, :, HEAD_DIM:] = jnp.ones((TOK_DEV, HEAD_DIM), jnp.bfloat16)
+
+    for copy in later:
         copy.wait()
 
 
-def second_kernel(
-    units, later, done, q, bias, keys, values, done_o, q_hbm, wo_hbm, after,
-    ctx_hbm, o, q_later, wo_half, sems, late_sems, wo_sem,
+def first_kernel(
+    sections, units, later, page, owner, q, keys, values, q_hbm, after,
+    o, q_later, bias, spread, sems,
 ):
     del after
-    copies = flushes(done, done_o, ctx_hbm, sems)
-    copies.append(pltpu.make_async_copy(half_columns(wo_hbm, False), wo_half, wo_sem))
-    copies += [pltpu.make_async_copy(region(q_hbm, u), q_later.at[n], late_sems.at[n]) for n, u in enumerate(later)]
+    copies = [pltpu.make_async_copy(region(q_hbm, u), q_later.at[n], sems.at[n]) for n, u in enumerate(later)]
     for copy in copies:
         copy.start()
 
     @beside
     def _():
+        here = lax.axis_index("section")
+        prefill_masks(pair_starts(page, here), bias)
+        slot_rows(sections, owner, here, spread)
         for n, unit in enumerate(units):
             attend(unit, q.at[n], bias, keys, values, o.at[n])
 
@@ -254,8 +291,8 @@
         copy.wait()
 
 
-def third_kernel(units, done, q, bias, keys, values, done_o, ctx_in, chip_in, ctx_hbm, o, chip, sems):
-    del ctx_in, chip_in, chip
+def second_kernel(units, done, q, bias, keys, values, done_o, chip_in, ctx_hbm, o, chip, sems):
+    del chip_in, chip
     copies = flushes(done, done_o, ctx_hbm, sems)
     for copy in copies:
         copy.start()
@@ -276,95 +313,75 @@
     )
 
 
-def beside(body):
-    pl.when(lax.axis_index("section") >= 0)(body)
-
-
 def block_shape(units):
     return jax.ShapeDtypeStruct((len(units), BLOCK, GROUP * HEAD_DIM), jnp.bfloat16)
 
 
-def prefill_first(units, later, page_pair, owner, prefill_q, kv_pool, wo, after, sections):
+def make_tables(units, page_pair, owner, kv_pool, prefill_q, after, sections):
     kv_local = kv_pool.shape[2] // HEAD_DIM
     return pl.pallas_call(
-        functools.partial(first_kernel, units, later),
+        functools.partial(tables_kernel, sections, units),
+        out_shape=[
+            jax.ShapeDtypeStruct(page_pair.shape, jnp.int32),
+            jax.ShapeDtypeStruct(owner.shape, jnp.int32),
+            jax.ShapeDtypeStruct((kv_local, HEAD_DIM, TOK_DEV), jnp.bfloat16),
+            jax.ShapeDtypeStruct((kv_local, TOK_DEV, 2 * HEAD_DIM), jnp.bfloat16),
+            jax.ShapeDtypeStruct((ROWS, TOK_DEV), jnp.float32),
+            jax.ShapeDtypeStruct((ROWS, sections * CAP * STEPS), jnp.bfloat16),
+            block_shape(units),
+        ],
+        in_specs=[ANY_SPEC] * 5,
+        out_specs=[VMEM_SPEC] * 7,
+        scratch_shapes=[
+            pltpu.VMEM(kv_pool.shape, jnp.bfloat16),
+            pltpu.SemaphoreType.DMA((3,)),
+            pltpu.SemaphoreType.DMA((len(units),)),
+        ],
+        compiler_params=params(),
+        cost_estimate=unit_cost(units),
+        name="make_tables",
+    )(in_hbm(page_pair), in_hbm(owner), in_hbm(kv_pool), in_hbm(prefill_q), after)
+
+
+def prefill_first(units, later, page, owner, q, keys, values, prefill_q, after, sections):
+    return pl.pallas_call(
+        functools.partial(first_kernel, sections, units, later),
         out_shape=[
             block_shape(units),
             block_shape(later),
             jax.ShapeDtypeStruct((TOK_DEV // BLOCK, BLOCK, LATEST), jnp.float32),
-            jax.ShapeDtypeStruct((kv_local, HEAD_DIM, TOK_DEV), jnp.bfloat16),
-            jax.ShapeDtypeStruct((kv_local, TOK_DEV, 2 * HEAD_DIM), jnp.bfloat16),
-            jax.ShapeDtypeStruct((ROWS, TOK_DEV), jnp.float32),
-            jax.ShapeDtypeStruct((ROWS, sections * CAP * STEPS), jnp.bfloat16),
             jax.ShapeDtypeStruct((sections * DSLOT * STEPS, sections * ROWS), jnp.bfloat16),
-            half_shape(wo),
         ],
-        in_specs=[ANY_SPEC] * 6,
-        out_specs=[VMEM_SPEC] * 9,
-        scratch_shapes=[
-            pltpu.VMEM(page_pair.shape, jnp.int32),
-            pltpu.VMEM(owner.shape, jnp.int32),
-            pltpu.VMEM(kv_pool.shape, jnp.bfloat16),
-            pltpu.VMEM(block_shape(units).shape, jnp.bfloat16),
-            pltpu.SemaphoreType.DMA((len(units),)),
-            pltpu.SemaphoreType.DMA((len(later),)),
-            pltpu.SemaphoreType.DMA((4,)),
-        ],
+        in_specs=[VMEM_SPEC] * 5 + [ANY_SPEC] * 2,
+        out_specs=[VMEM_SPEC] * 4,
+        scratch_shapes=[pltpu.SemaphoreType.DMA((len(later),))],
         compiler_params=params(),
         cost_estimate=unit_cost(units),
         name="prefill_first",
-    )(in_hbm(page_pair), in_hbm(owner), in_hbm(prefill_q), in_hbm(kv_pool), in_hbm(wo), after)
-
-
-def prefill_second(units, later, done, q, tables, done_o, prefill_q, wo, after):
-    return pl.pallas_call(
-        functools.partial(second_kernel, units, later, done),
-        out_shape=[
-            jax.ShapeDtypeStruct(prefill_q.shape, prefill_q.dtype),
-            block_shape(units),
-            block_shape(later),
-            half_shape(wo),
-        ],
-        in_specs=[VMEM_SPEC] * 5 + [ANY_SPEC] * 3,
-        out_specs=[ANY_SPEC] + [VMEM_SPEC] * 3,
-        scratch_shapes=[
-            pltpu.SemaphoreType.DMA((len(done),)),
-            pltpu.SemaphoreType.DMA((len(later),)),
-            pltpu.SemaphoreType.DMA,
-        ],
+    )(page, owner, q, keys, values, in_hbm(prefill_q), after)
+
+
+def prefill_second(units, done, q, bias, keys, values, done_o, ctx_shape, chip):
+    return pl.pallas_call(
+        functools.partial(second_kernel, units, done),
+        out_shape=[ctx_shape, block_shape(units), jax.ShapeDtypeStruct(chip.shape, chip.dtype)],
+        in_specs=[VMEM_SPEC] * 6,
+        out_specs=[ANY_SPEC, VMEM_SPEC, VMEM_SPEC],
+        scratch_shapes=[pltpu.SemaphoreType.DMA((len(done),))],
+        input_output_aliases={5: 2},
         compiler_params=params(),
         cost_estimate=unit_cost(units),
         name="prefill_second",
-    )(q, *tables, done_o, in_hbm(prefill_q), in_hbm(wo), after)
-
-
-def prefill_third(units, done, q, tables, done_o, ctx, chip):
-    return pl.pallas_call(
-        functools.partial(third_kernel, units, done),
-        out_shape=[
-            jax.ShapeDtypeStruct(ctx.shape, ctx.dtype),
-            block_shape(units),
-            jax.ShapeDtypeStruct(chip.shape, chip.dtype),
-        ],
-        in_specs=[VMEM_SPEC] * 5 + [ANY_SPEC, VMEM_SPEC],
-        out_specs=[ANY_SPEC, VMEM_SPEC, VMEM_SPEC],
-        scratch_shapes=[pltpu.SemaphoreType.DMA((len(done),))],
-        input_output_aliases={5: 0, 6: 2},
-        compiler_params=params(),
-        cost_estimate=unit_cost(units),
-        name="prefill_third",
-    )(q, *tables, done_o, ctx, chip)
+    )(q, bias, keys, values, done_o, chip)
 
 
 def split_units(kv_local):
-    order = [(0, 0), (0, 1), (0, 2), (0, 3)]
-    units = [(k, i) for k in range(kv_local) for _, i in order]
-    first, second = len(units) // 4, len(units) // 2
-    return units[:first], units[first:second], units[second:]
+    units = [(k, i) for k in range(kv_local) for i in range(TOK_DEV // BLOCK)]
+    return units[: len(units) // 2], units[len(units) // 2 :]
 
 
 def decode_kernel(sections, seen, pick, keys, values, *refs):
-    got, (ctx_ref, rows) = in_order(refs[:sections]), refs[sections:]
+    got, (ctx_ref, rows) = refs[:sections], refs[sections:]
     kv_local = keys.shape[0]
     width = kv_local * GROUP * HEAD_DIM
     for k in range(sections):
@@ -412,27 +429,30 @@
         scratch_shapes=[pltpu.VMEM((sections * CAP * STEPS, block[2]), jnp.float32)],
         compiler_params=params(),
         name="decode_attention",
-    )(seen, pick, keys, values, *in_order(got))
-
-
-def project_kernel(sections, *refs):
-    ctxs, wo, out_ref = in_order(refs[:sections]), refs[sections], refs[-1]
+    )(seen, pick, keys, values, *got)
+
+
+def project_kernel(sections, flip, *refs):
+    ctxs, wo, out_ref = refs[:sections][::-1], refs[sections], refs[-1]
     x = jnp.concatenate([c[...] for c in ctxs], axis=0)
-    out_ref[...] = jnp.dot(x, wo[...], preferred_element_type=jnp.float32).astype(out_ref.dtype)
-
-
-def project(ctxs, wo_half, after, sections, dtype):
+    rows = x.shape[0]
+    if rows < BLOCK:
+        x = jnp.concatenate([x] * (BLOCK // rows), axis=0)
+    out_ref[...] = jnp.dot(x, half_columns(wo, flip)[...], preferred_element_type=jnp.float32)[:rows].astype(out_ref.dtype)
+
+
+def project(flip, ctxs, wo, after, sections, dtype):
     rows = sections * ROWS
-    depth, wide = wo_half.shape
-    return pl.pallas_call(
-        functools.partial(project_kernel, sections),
+    depth, wide = wo.shape[0], wo.shape[1] // 2
+    return pl.pallas_call(
+        functools.partial(project_kernel, sections, flip),
         out_shape=jax.ShapeDtypeStruct((rows, wide), dtype),
         in_specs=[VMEM_SPEC] * (sections + 1) + [ANY_SPEC] * len(after),
         out_specs=VMEM_SPEC,
         compiler_params=params(),
         cost_estimate=pl.CostEstimate(flops=rows * depth * wide * 2, bytes_accessed=depth * wide * 2, transcendentals=0),
         name="project_half",
-    )(*in_order(ctxs), wo_half, *after)
+    )(*ctxs[::-1], wo, *after)
 
 
 def spread_rows(flip, spread, rows, held, out_hbm, sem):
@@ -503,35 +523,36 @@
     sections = lax.axis_size("section")
     owner = slot_owner.reshape(-1)
     units = split_units(kv_pool.shape[2] // HEAD_DIM)
+    ctx_shape = jax.ShapeDtypeStruct(prefill_q.shape, prefill_q.dtype)
 
     packed = pack(owner, decode_q, decode_kv, sections)
-    got = [packed[0]] + [swap(packed[k], "section", k) for k in range(1, sections)]
-    done_o, q_later, bias, keys, values, seen, pick, spread, wo_away = prefill_first(
-        units[0], units[1], page_pair, owner.reshape(1, -1), prefill_q, kv_pool, wo_weight, packed[0], sections
+    first, second = routes(FIRST_ROUND, sections), routes(SECOND_ROUND, sections)
+    got = [packed[0]] + [send(x, route) for x, route in zip(packed[1:], first[1:])]
+    page, owner, keys, values, seen, pick, q = make_tables(
+        units[0], page_pair, owner.reshape(1, -1), kv_pool, prefill_q, packed[0], sections
     )
-    tables = (bias, keys, values)
     ctx = decode(seen, pick, keys, values, got, sections)
-    ctxs = [ctx] + [swap(ctx, "section", k) for k in range(1, sections)]
-    prefill_ctx, done_o, q_later, wo_keep = prefill_second(
-        units[1], units[2], units[0], q_later, tables, done_o, prefill_q, wo_weight, ctx
+    ctxs = [ctx] + [send(ctx, route) for route in second[1:]]
+    done_o, q, bias, spread = prefill_first(
+        units[0], units[1], page, owner, q, keys, values, prefill_q, ctx, sections
     )
 
-    away = project(ctxs, wo_away, [wo_keep], sections, jnp.bfloat16)
+    away = project(True, ctxs, wo_weight, [q], sections, jnp.bfloat16)
     came = swap(away, "tensor", 1)
-    keep = project(ctxs, wo_keep, [], sections, jnp.float32)
+    keep = project(False, ctxs, wo_weight, [], sections, jnp.float32)
     chip = keep + came.astype(jnp.float32)
     k = 2
     while k < lax.axis_size("tensor"):
         far = swap(chip.astype(jnp.bfloat16), "tensor", k)
         if k == 2:
-            prefill_ctx, done_o, chip = prefill_third(
-                units[2], units[1], q_later, tables, done_o, prefill_ctx, chip
+            prefill_ctx, done_o, chip = prefill_second(
+                units[1], units[0], q, bias, keys, values, done_o, ctx_shape, chip
             )
         chip = chip + far.astype(jnp.float32)
         k *= 2
     mine = chip.astype(jnp.bfloat16)
     other = swap(mine, "tensor", 1)
-    decode_out, prefill_ctx = spread_own(units[2], spread, mine, done_o, prefill_ctx, sections)
+    decode_out, prefill_ctx = spread_own(units[1], spread, mine, done_o, prefill_ctx, sections)
     decode_out = spread_other(spread, other, decode_out)
     return (prefill_ctx, decode_out)
 

time: 31.3 us -> 30.5 us (0.974)
  Pallas kernels: 13.8 us -> 12.1 us
  starting transfers between devices: 11.8 us -> 13.3 us
  waiting for transfers between devices: 4.56 us -> 4.08 us
    ppermute x0 -> x6, starting transfers between devices: none -> 11.6 us  [send(): return lax.ppermute(x, 'section', list(enumerate(route)))]
    ppermute x9 -> x3, starting transfers between devices: 11.8 us -> 1.7 us  [swap(): return lax.ppermute(x, axis, [(i, i ^ k) for i in range(count)])]
    ppermute x9 -> x3, waiting for transfers between devices: 4.56 us -> 2.38 us  [swap(): return lax.ppermute(x, axis, [(i, i ^ k) for i in range(count)])]
    ppermute x0 -> x6, waiting for transfers between devices: none -> 1.7 us  [send(): return lax.ppermute(x, 'section', list(enumerate(route)))]
    pallas_call x5, Pallas kernels: 9.74 us -> 8.23 us  [the longest x1 2.52 us: prefill_first(): pl.pallas_call(functools.partial(first_kernel, sections, units, later), o...]
  transfers between devices with their start and end apart: 9 -> 9, of which waited for: 5 -> 6; matrix products, arithmetic and copies ran while one was open for 0% -> 0% of each run, Pallas kernels for 32% -> 28%
where the time goes in v4:
time: 30.5 us; the launch traced here: 30.3 us
  starting transfers between devices  13.3 us (44%)
  Pallas kernels  12.1 us (40%)
  waiting for transfers between devices  4.08 us (13%)
  between operations  0.74 us (2%)
    ppermute x6, starting transfers between devices, send(): return lax.ppermute(x, 'section', list(enumerate(route)))  11.6 us
    pallas_call x1, Pallas kernels, prefill_first(): pl.pallas_call(functools.partial(first_kernel, sections, units, later), o...  2.52 us
    pallas_call x1, Pallas kernels, prefill_second(): pl.pallas_call(functools.partial(second_kernel, units, done), out_shape=[...  2.49 us
    ppermute x3, waiting for transfers between devices, swap(): return lax.ppermute(x, axis, [(i, i ^ k) for i in range(count)])  2.38 us
    pallas_call x1, Pallas kernels, make_tables(): pl.pallas_call(functools.partial(tables_kernel, sections, units), out_sha...  1.77 us
    ppermute x6, waiting for transfers between devices, send(): return lax.ppermute(x, 'section', list(enumerate(route)))  1.7 us
    ppermute x3, starting transfers between devices, swap(): return lax.ppermute(x, axis, [(i, i ^ k) for i in range(count)])  1.7 us
    pallas_call x2, Pallas kernels, project(): pl.pallas_call(functools.partial(project_kernel, sections, flip), out_sha...  1.45 us
  transfers between devices with their start and end apart: 9, of which 6 were waited for; matrix products, arithmetic and copies ran while one was open for 0% of the time, Pallas kernels for 28%

profile of v4, /device:TPU:0, one launch (start us, length us, event | category | flops | bytes accessed | tf_op | source)
XLA Modules:
  0.0 30.3 jit_solution(9528199997574567756)
XLA Ops:
  0.6 1.0 %pack_queries.1 = (bf16[2,4,2560]{2,1,0:T(4,128)(2,1)S(1)}, bf16[2,4,2560]{2,1,0:T(4,128)(2,1)S(1)}, bf16[2,4,2560]{2,1,0:T(4,128)(2,1)S(1)}, bf16[2,4,2560]{2,1,0:T(4,128)(2,1)S(1)}) custom-call(s32[16]{0:T(128)} %bitcast.2, bf16[8,4,2048]{2,1,0:T(4,128)(2,1)} %q_hbm.3, bf16[2,8,4,256]{3,2,1,0:T(4,128)(2,1)} %kv_hbm.2), custom_call_target="tpu_custom_call" | custom-call | tf_op jit(solution)/shard_map/pack_queries/pallas_call | solution.py:128
  1.6 3.0 %collective-permute-start = (bf16[2,4,2560]{2,1,0:T(4,128)(2,1)S(1)}, bf16[2,4,2560]{2,1,0:T(4,128)(2,1)S(1)}, u32[]{:S(2)}, u32[]{:S(2)}) collective-permute-start(bf16[2,4,2560]{2,1,0:T(4,128)(2,1)S(1)} %get-tuple-element.30), channel_id=1, source_target_pairs={{0,4},{4,12},{8,0},{12,8},{1,5},{5,13},{9,1},{13,9},{2,6},{6,14},{... | collective-permute-start | bytes 122888 | tf_op jit(solution)/shard_map/ppermute | solution.py:71
  4.7 2.5 %collective-permute-start.1 = (bf16[2,4,2560]{2,1,0:T(4,128)(2,1)S(1)}, bf16[2,4,2560]{2,1,0:T(4,128)(2,1)S(1)}, u32[]{:S(2)}, u32[]{:S(2)}) collective-permute-start(bf16[2,4,2560]{2,1,0:T(4,128)(2,1)S(1)} %get-tuple-element.31), channel_id=1, source_target_pairs={{0,12},{4,8},{8,4},{12,0},{1,13},{5,9},{9,5},{13,1},{2,14},{6,10},... | collective-permute-start | bytes 122888 | tf_op jit(solution)/shard_map/ppermute | solution.py:71
  7.1 1.7 %collective-permute-start.2 = (bf16[2,4,2560]{2,1,0:T(4,128)(2,1)S(1)}, bf16[2,4,2560]{2,1,0:T(4,128)(2,1)S(1)}, u32[]{:S(2)}, u32[]{:S(2)}) collective-permute-start(bf16[2,4,2560]{2,1,0:T(4,128)(2,1)S(1)} %get-tuple-element.32), channel_id=1, source_target_pairs={{0,8},{4,0},{8,12},{12,4},{1,9},{5,1},{9,13},{13,5},{2,10},{6,2},{... | collective-permute-start | bytes 122888 | tf_op jit(solution)/shard_map/ppermute | solution.py:71
  8.8 0.0 copy-start
  8.8 1.8 %make_tables.1 = (s32[4,32]{1,0:T(4,128)S(1)}, s32[1,16]{1,0:T(1,128)S(1)}, bf16[2,128,512]{2,1,0:T(8,128)(2,1)S(1)}, bf16[2,512,256]{2,1,0:T(8,128)(2,1)S(1)}, ...) custom-call(s32[4,32]{1,0:T(4,128)} %page_hbm.1, s32[1,16]{1,0:T(1,128)} %bitcast.3, ...), custom_call_target="tpu_custom_call" | custom-call | flops 1207959552 | bytes 2097152 | tf_op jit(solution)/shard_map/make_tables/pallas_call | solution.py:322
  10.6 0.0 collective-permute-done.refs_1_
  10.6 0.2 collective-permute-done.1.refs_2_
  10.7 0.4 %collective-permute-done.2.refs_3_ = bf16[2,4,2560]{2,1,0:T(4,128)(2,1)S(1)} collective-permute-done((bf16[2,4,2560]{2,1,0:T(4,128)(2,1)S(1)}, bf16[2,4,2560]{2,1,0:T(4,128)(2,1)S(1)}, u32[]{:S(2)}, u32[]{:S(2)}) %collective-permute-start.2) | collective-permute-done | bytes 40992 | tf_op jit(solution)/shard_map/ppermute | solution.py:71
  11.2 0.9 %decode_attention.1.after.refs_3_ = bf16[16,2048]{1,0:T(8,128)(2,1)S(1)} custom-call(f32[16,512]{1,0:T(8,128)S(1)} %get-tuple-element.28.seen, bf16[16,32]{1,0:T(8,128)(2,1)S(1)} %get-tuple-element.29.pick, bf16[2,128,512]{2,1,0:T(8,128)(2,1)S(1)} %get-tuple-element.26.keys, bf16[2,512,256]{2,1,0:T(8,128)(2,1)S(1)} %get-tuple-element.27.values, ...), custom_call_target="tpu_custom_call" | custom-call | tf_op jit(solution)/shard_map/decode_attention/pallas_call | solution.py:424
  12.1 2.2 %collective-permute-start.5 = (bf16[16,2048]{1,0:T(8,128)(2,1)S(1)}, bf16[16,2048]{1,0:T(8,128)(2,1)S(1)}, u32[]{:S(2)}, u32[]{:S(2)}) collective-permute-start(bf16[16,2048]{1,0:T(8,128)(2,1)S(1)} %decode_attention.1.after.refs_3_), channel_id=1, source_target_pairs={{0,12},{4,8},{8,4},{12,0},{1,13},{5,9},{9,5},{13,1},{2,14},{6,10},... | collective-permute-start | bytes 196616 | tf_op jit(solution)/shard_map/ppermute | solution.py:71
  14.3 0.4 %collective-permute-start.4 = (bf16[16,2048]{1,0:T(8,128)(2,1)S(1)}, bf16[16,2048]{1,0:T(8,128)(2,1)S(1)}, u32[]{:S(2)}, u32[]{:S(2)}) collective-permute-start(bf16[16,2048]{1,0:T(8,128)(2,1)S(1)} %decode_attention.1.after.refs_3_), channel_id=1, source_target_pairs={{0,8},{4,12},{8,0},{12,4},{1,9},{5,13},{9,1},{13,5},{2,10},{6,14},... | collective-permute-start | bytes 196616 | tf_op jit(solution)/shard_map/ppermute | solution.py:71
  14.7 1.8 %collective-permute-start.3 = (bf16[16,2048]{1,0:T(8,128)(2,1)S(1)}, bf16[16,2048]{1,0:T(8,128)(2,1)S(1)}, u32[]{:S(2)}, u32[]{:S(2)}) collective-permute-start(bf16[16,2048]{1,0:T(8,128)(2,1)S(1)} %decode_attention.1.after.refs_3_), channel_id=1, source_target_pairs={{0,4},{4,0},{8,12},{12,8},{1,5},{5,1},{9,13},{13,9},{2,6},{6,2},{1... | collective-permute-start | bytes 196616 | tf_op jit(solution)/shard_map/ppermute | solution.py:71
  16.5 2.5 %prefill_first.1 = (bf16[4,128,1024]{2,1,0:T(8,128)(2,1)S(1)}, bf16[4,128,1024]{2,1,0:T(8,128)(2,1)S(1)}, f32[4,128,384]{2,1,0:T(8,128)S(1)}, bf16[128,64]{1,0:T(8,128)(2,1)S(1)}) custom-call(s32[4,32]{1,0:T(4,128)S(1)} %get-tuple-element.23.page, s32[1,16]{1,0:T(1,128)S(1)} %get-tuple-element.24.owner, bf16[4,128,1024]{2,1,0:T(8,128)(2,1)S(1)} %get-tuple-element.25.q, ...), custom_call_target="tpu_custom_call" | custom-call | flops 1207959552 | bytes 2097152 | tf_op jit(solution)/shard_map/prefill_first/pallas_call | solution.py:347
  19.1 0.0 collective-permute-done.5.refs_2_
  19.1 1.1 %collective-permute-done.4.refs_1_ = bf16[16,2048]{1,0:T(8,128)(2,1)S(1)} collective-permute-done((bf16[16,2048]{1,0:T(8,128)(2,1)S(1)}, bf16[16,2048]{1,0:T(8,128)(2,1)S(1)}, u32[]{:S(2)}, u32[]{:S(2)}) %collective-permute-start.4) | collective-permute-done | bytes 65568 | tf_op jit(solution)/shard_map/ppermute | solution.py:71
  20.2 0.0 collective-permute-done.3.refs_0_
  20.2 0.0 copy-done
  20.2 0.7 %project_half.3 = bf16[64,1024]{1,0:T(8,128)(2,1)S(1)} custom-call(bf16[16,2048]{1,0:T(8,128)(2,1)S(1)} %collective-permute-done.3.refs_0_, bf16[16,2048]{1,0:T(8,128)(2,1)S(1)} %collective-permute-done.4.refs_1_, bf16[16,2048]{1,0:T(8,128)(2,1)S(1)} %collective-permute-done.5.refs_2_, bf16[16,2048]{1,0:T(8,128)(2,1)S(1)} %decode_attention.1.after.refs_3_, ...), custom_call_target="tpu_custom_call" | custom-call | flops 268435456 | bytes 4194304 | tf_op jit(solution)/shard_map/project_half/pallas_call | solution.py:447
  20.9 0.1 collective-permute-start.6
  21.0 0.7 %project_half.2 = f32[64,1024]{1,0:T(8,128)S(1)} custom-call(bf16[16,2048]{1,0:T(8,128)(2,1)S(1)} %collective-permute-done.3.refs_0_, bf16[16,2048]{1,0:T(8,128)(2,1)S(1)} %collective-permute-done.4.refs_1_, bf16[16,2048]{1,0:T(8,128)(2,1)S(1)} %collective-permute-done.5.refs_2_, bf16[16,2048]{1,0:T(8,128)(2,1)S(1)} %decode_attention.1.after.refs_3_, ...), custom_call_target="tpu_custom_call" | custom-call | flops 268435456 | bytes 4194304 | tf_op jit(solution)/shard_map/project_half/pallas_call | solution.py:447
  21.7 0.6 %collective-permute-done.6 = bf16[64,1024]{1,0:T(8,128)(2,1)S(1)} collective-permute-done((bf16[64,1024]{1,0:T(8,128)(2,1)S(1)}, bf16[64,1024]{1,0:T(8,128)(2,1)S(1)}, u32[]{:S(2)}, u32[]{:S(2)}) %collective-permute-start.6) | collective-permute-done | bytes 131104 | tf_op jit(solution)/shard_map/ppermute | solution.py:519
  22.4 1.6 %collective-permute-start.7 = (bf16[64,1024]{1,0:T(8,128)(2,1)S(1)}, bf16[64,1024]{1,0:T(8,128)(2,1)S(1)}, u32[]{:S(2)}, u32[]{:S(2)}) collective-permute-start(bf16[64,1024]{1,0:T(8,128)(2,1)S(1)} %get-tuple-element.42), channel_id=1, source_target_pairs={{0,2},{1,3},{2,0},{3,1},{4,6},{5,7},{6,4},{7,5},{8,10},{9,11},{10,... | collective-permute-start | bytes 393224 | tf_op jit(solution)/shard_map/ppermute | solution.py:519
  23.9 2.5 %prefill_second.1 = (bf16[512,2048]{1,0:T(8,128)(2,1)}, bf16[4,128,1024]{2,1,0:T(8,128)(2,1)S(1)}, f32[64,1024]{1,0:T(8,128)S(1)}) custom-call(bf16[4,128,1024]{2,1,0:T(8,128)(2,1)S(1)} %get-tuple-element.34.refs_5_.q, f32[4,128,384]{2,1,0:T(8,128)S(1)} %get-tuple-element.35.bias, ...), custom_call_target="tpu_custom_call", output_to_operand_aliasing={{2}: (5, {})} | custom-call | flops 1207959552 | bytes 2097152 | tf_op jit(solution)/shard_map/prefill_second/pallas_call | solution.py:365
  26.4 1.6 %collective-permute-done.7 = bf16[64,1024]{1,0:T(8,128)(2,1)S(1)} collective-permute-done((bf16[64,1024]{1,0:T(8,128)(2,1)S(1)}, bf16[64,1024]{1,0:T(8,128)(2,1)S(1)}, u32[]{:S(2)}, u32[]{:S(2)}) %collective-permute-start.7) | collective-permute-done | bytes 131104 | tf_op jit(solution)/shard_map/ppermute | solution.py:519
  28.0 0.1 collective-permute-start.8
  28.1 1.1 %spread_own.1 = (bf16[32,4,2048]{2,1,0:T(4,128)(2,1)}, bf16[512,2048]{1,0:T(8,128)(2,1)}) custom-call(bf16[128,64]{1,0:T(8,128)(2,1)S(1)} %get-tuple-element.33.spread, bf16[64,1024]{1,0:T(8,128)(2,1)S(1)} %add_convert_fusion.rows, bf16[4,128,1024]{2,1,0:T(8,128)(2,1)S(1)} %get-tuple-element.38.done_o, ...), custom_call_target="tpu_custom_call", output_to_operand_aliasing={{1}: (3, {})} | custom-call | tf_op jit(solution)/shard_map/spread_own/pallas_call | solution.py:479
  29.2 0.2 collective-permute-done.8.rows
  29.4 0.9 %spread_other.1 = bf16[32,4,2048]{2,1,0:T(4,128)(2,1)} custom-call(bf16[128,64]{1,0:T(8,128)(2,1)S(1)} %get-tuple-element.33.spread, bf16[64,1024]{1,0:T(8,128)(2,1)S(1)} %collective-permute-done.8.rows, bf16[32,4,2048]{2,1,0:T(4,128)(2,1)} %get-tuple-element.41.out_in), custom_call_target="tpu_custom_call", output_to_operand_aliasing={{}: (2, {})} | custom-call | tf_op jit(solution)/shard_map/spread_other/pallas_call | solution.py:505
  (2 shorter events, 0.1 us)
Async XLA Ops:
  1.6 9.0 %collective-permute-start = (bf16[2,4,2560]{2,1,0:T(4,128)(2,1)S(1)}, bf16[2,4,2560]{2,1,0:T(4,128)(2,1)S(1)}, u32[]{:S(2)}, u32[]{:S(2)}) collective-permute-start(bf16[2,4,2560]{2,1,0:T(4,128)(2,1)S(1)} %get-tuple-element.30), channel_id=1, source_target_pairs={{0,4},{4,12},{8,0},{12,8},{1,5},{5,13},{9,1},{13,9},{2,6},{6,14},{... | collective-permute-start | bytes 122888 | tf_op jit(solution)/shard_map/ppermute | solution.py:71
  4.7 6.1 %collective-permute-start.1 = (bf16[2,4,2560]{2,1,0:T(4,128)(2,1)S(1)}, bf16[2,4,2560]{2,1,0:T(4,128)(2,1)S(1)}, u32[]{:S(2)}, u32[]{:S(2)}) collective-permute-start(bf16[2,4,2560]{2,1,0:T(4,128)(2,1)S(1)} %get-tuple-element.31), channel_id=1, source_target_pairs={{0,12},{4,8},{8,4},{12,0},{1,13},{5,9},{9,5},{13,1},{2,14},{6,10},... | collective-permute-start | bytes 122888 | tf_op jit(solution)/shard_map/ppermute | solution.py:71
  7.1 4.0 %collective-permute-start.2 = (bf16[2,4,2560]{2,1,0:T(4,128)(2,1)S(1)}, bf16[2,4,2560]{2,1,0:T(4,128)(2,1)S(1)}, u32[]{:S(2)}, u32[]{:S(2)}) collective-permute-start(bf16[2,4,2560]{2,1,0:T(4,128)(2,1)S(1)} %get-tuple-element.32), channel_id=1, source_target_pairs={{0,8},{4,0},{8,12},{12,4},{1,9},{5,1},{9,13},{13,5},{2,10},{6,2},{... | collective-permute-start | bytes 122888 | tf_op jit(solution)/shard_map/ppermute | solution.py:71
  8.8 11.4 %copy-start = (bf16[2048,2048]{1,0:T(8,128)(2,1)S(1)}, bf16[2048,2048]{1,0:T(8,128)(2,1)}, u32[]{:S(2)}) copy-start(bf16[2048,2048]{1,0:T(8,128)(2,1)} %refs_4_.3) | copy-start | bytes 25165828
  12.1 7.0 %collective-permute-start.5 = (bf16[16,2048]{1,0:T(8,128)(2,1)S(1)}, bf16[16,2048]{1,0:T(8,128)(2,1)S(1)}, u32[]{:S(2)}, u32[]{:S(2)}) collective-permute-start(bf16[16,2048]{1,0:T(8,128)(2,1)S(1)} %decode_attention.1.after.refs_3_), channel_id=1, source_target_pairs={{0,12},{4,8},{8,4},{12,0},{1,13},{5,9},{9,5},{13,1},{2,14},{6,10},... | collective-permute-start | bytes 196616 | tf_op jit(solution)/shard_map/ppermute | solution.py:71
  14.3 5.9 %collective-permute-start.4 = (bf16[16,2048]{1,0:T(8,128)(2,1)S(1)}, bf16[16,2048]{1,0:T(8,128)(2,1)S(1)}, u32[]{:S(2)}, u32[]{:S(2)}) collective-permute-start(bf16[16,2048]{1,0:T(8,128)(2,1)S(1)} %decode_attention.1.after.refs_3_), channel_id=1, source_target_pairs={{0,8},{4,12},{8,0},{12,4},{1,9},{5,13},{9,1},{13,5},{2,10},{6,14},... | collective-permute-start | bytes 196616 | tf_op jit(solution)/shard_map/ppermute | solution.py:71
  14.7 5.4 %collective-permute-start.3 = (bf16[16,2048]{1,0:T(8,128)(2,1)S(1)}, bf16[16,2048]{1,0:T(8,128)(2,1)S(1)}, u32[]{:S(2)}, u32[]{:S(2)}) collective-permute-start(bf16[16,2048]{1,0:T(8,128)(2,1)S(1)} %decode_attention.1.after.refs_3_), channel_id=1, source_target_pairs={{0,4},{4,0},{8,12},{12,8},{1,5},{5,1},{9,13},{13,9},{2,6},{6,2},{1... | collective-permute-start | bytes 196616 | tf_op jit(solution)/shard_map/ppermute | solution.py:71
  20.9 1.4 %collective-permute-start.6 = (bf16[64,1024]{1,0:T(8,128)(2,1)S(1)}, bf16[64,1024]{1,0:T(8,128)(2,1)S(1)}, u32[]{:S(2)}, u32[]{:S(2)}) collective-permute-start(bf16[64,1024]{1,0:T(8,128)(2,1)S(1)} %project_half.3), channel_id=1, source_target_pairs={{0,1},{1,0},{2,3},{3,2},{4,5},{5,4},{6,7},{7,6},{8,9},{9,8},{10,11... | collective-permute-start | bytes 393224 | tf_op jit(solution)/shard_map/ppermute | solution.py:519
  22.4 5.6 %collective-permute-start.7 = (bf16[64,1024]{1,0:T(8,128)(2,1)S(1)}, bf16[64,1024]{1,0:T(8,128)(2,1)S(1)}, u32[]{:S(2)}, u32[]{:S(2)}) collective-permute-start(bf16[64,1024]{1,0:T(8,128)(2,1)S(1)} %get-tuple-element.42), channel_id=1, source_target_pairs={{0,2},{1,3},{2,0},{3,1},{4,6},{5,7},{6,4},{7,5},{8,10},{9,11},{10,... | collective-permute-start | bytes 393224 | tf_op jit(solution)/shard_map/ppermute | solution.py:519
  28.0 1.4 %collective-permute-start.8 = (bf16[64,1024]{1,0:T(8,128)(2,1)S(1)}, bf16[64,1024]{1,0:T(8,128)(2,1)S(1)}, u32[]{:S(2)}, u32[]{:S(2)}) collective-permute-start(bf16[64,1024]{1,0:T(8,128)(2,1)S(1)} %add_convert_fusion.rows), channel_id=1, source_target_pairs={{0,1},{1,0},{2,3},{3,2},{4,5},{5,4},{6,7},{7,6},{8,9},{9,8},{10,11... | collective-permute-start | bytes 393224 | tf_op jit(solution)/shard_map/ppermute | solution.py:519

commit v5 on v4

--- a/solution.py
+++ b/solution.py
@@ -37,8 +37,8 @@
     return pltpu.with_memory_space_constraint(x, pltpu.HBM)
 
 
-FIRST_ROUND = ((0, 1, 2, 3), (1, 3, 0, 2), (3, 2, 1, 0), (2, 0, 3, 1))
-SECOND_ROUND = ((0, 1, 2, 3), (3, 2, 1, 0), (2, 3, 0, 1), (1, 0, 3, 2))
+FIRST_ROUND = ((0, 1, 2, 3), (1, 2, 3, 0), (2, 3, 0, 1), (3, 0, 1, 2))
+SECOND_ROUND = ((0, 1, 2, 3), (1, 3, 0, 2), (3, 2, 1, 0), (2, 0, 3, 1))
 
 
 def routes(table, sections):
@@ -407,12 +407,17 @@
         s = (s.reshape(GROUP, ROWS, TOK_DEV) + seen[...][None]).reshape(many, TOK_DEV)
         s_new = lax.dot_general(q, new_keys, contract, preferred_element_type=jnp.float32)
         s_new = jnp.where(new_allowed, s_new, MASKED)
-        m = jnp.maximum(jnp.max(s, axis=1, keepdims=True), jnp.max(s_new, axis=1, keepdims=True))
-        p = jnp.exp2((s - m) * EXP2_SCALE)
-        p_new = jnp.exp2((s_new - m) * EXP2_SCALE)
-        o = jnp.dot(p.astype(jnp.bfloat16), values[k], preferred_element_type=jnp.float32)
-        total = o[:, HEAD_DIM:] + jnp.sum(p_new, axis=1, keepdims=True)
-        o = o[:, :HEAD_DIM] + jnp.dot(p_new.astype(jnp.bfloat16), new_values, preferred_element_type=jnp.float32)
+        m_old = jnp.max(s, axis=1, keepdims=True)
+        m_new = jnp.max(s_new, axis=1, keepdims=True)
+        m = jnp.maximum(m_old, m_new)
+        scale_old = jnp.exp2((m_old - m) * EXP2_SCALE)
+        scale_new = jnp.exp2((m_new - m) * EXP2_SCALE)
+        p = jnp.exp2((s - m_old) * EXP2_SCALE)
+        p_new = jnp.exp2((s_new - m_new) * EXP2_SCALE)
+        o = jnp.dot(p.astype(jnp.bfloat16), values[k], preferred_element_type=jnp.float32) * scale_old
+        total = o[:, HEAD_DIM:] + jnp.sum(p_new, axis=1, keepdims=True) * scale_new
+        y = jnp.dot(p_new.astype(jnp.bfloat16), new_values, preferred_element_type=jnp.float32)
+        o = o[:, :HEAD_DIM] + y * scale_new
         o = (o / total).astype(jnp.bfloat16)
         for g in range(GROUP):
             ctx_ref[:, (k * GROUP + g) * HEAD_DIM : (k * GROUP + g + 1) * HEAD_DIM] = o[g * ROWS : (g + 1) * ROWS]

time: 30.5 us -> 30.3 us (level)
  waiting for transfers between devices: 4.08 us -> 3.24 us
  starting transfers between devices: 13.3 us -> 14 us
    ppermute x6, waiting for transfers between devices: 1.7 us -> 0.86 us  [send(): return lax.ppermute(x, 'section', list(enumerate(route)))]
    ppermute x6, starting transfers between devices: 11.6 us -> 12.3 us  [send(): return lax.ppermute(x, 'section', list(enumerate(route)))]
  transfers between devices with their start and end apart: 9 -> 9, of which waited for: 6 -> 4; matrix products, arithmetic and copies ran while one was open for 0% -> 0% of each run, Pallas kernels for 28% -> 29%
where the time goes in v5:
time: 30.3 us; the launch traced here: 30.1 us
  starting transfers between devices  14 us (46%)
  Pallas kernels  12.1 us (40%)
  waiting for transfers between devices  3.24 us (11%)
  between operations  0.77 us (3%)
    ppermute x6, starting transfers between devices, send(): return lax.ppermute(x, 'section', list(enumerate(route)))  12.3 us
    pallas_call x1, Pallas kernels, prefill_first(): pl.pallas_call(functools.partial(first_kernel, sections, units, later), o...  2.52 us
    pallas_call x1, Pallas kernels, prefill_second(): pl.pallas_call(functools.partial(second_kernel, units, done), out_shape=[...  2.48 us
    ppermute x3, waiting for transfers between devices, swap(): return lax.ppermute(x, axis, [(i, i ^ k) for i in range(count)])  2.38 us
    pallas_call x1, Pallas kernels, make_tables(): pl.pallas_call(functools.partial(tables_kernel, sections, units), out_sha...  1.77 us
    ppermute x3, starting transfers between devices, swap(): return lax.ppermute(x, axis, [(i, i ^ k) for i in range(count)])  1.7 us
    pallas_call x2, Pallas kernels, project(): pl.pallas_call(functools.partial(project_kernel, sections, flip), out_sha...  1.46 us
    pallas_call x1, Pallas kernels, spread_own(): pl.pallas_call(functools.partial(spread_own_kernel, done), out_shape=[jax...  1.11 us
  transfers between devices with their start and end apart: 9, of which 4 were waited for; matrix products, arithmetic and copies ran while one was open for 0% of the time, Pallas kernels for 29%

profile of v5, /device:TPU:0, one launch (start us, length us, event | category | flops | bytes accessed | tf_op | source)
XLA Modules:
  0.0 30.1 jit_solution(10506836365857747140)
XLA Ops:
  0.6 0.9 %pack_queries.1 = (bf16[2,4,2560]{2,1,0:T(4,128)(2,1)S(1)}, bf16[2,4,2560]{2,1,0:T(4,128)(2,1)S(1)}, bf16[2,4,2560]{2,1,0:T(4,128)(2,1)S(1)}, bf16[2,4,2560]{2,1,0:T(4,128)(2,1)S(1)}) custom-call(s32[16]{0:T(128)} %bitcast.2, bf16[8,4,2048]{2,1,0:T(4,128)(2,1)} %q_hbm.3, bf16[2,8,4,256]{3,2,1,0:T(4,128)(2,1)} %kv_hbm.2), custom_call_target="tpu_custom_call" | custom-call | tf_op jit(solution)/shard_map/pack_queries/pallas_call | solution.py:128
  1.6 3.2 %collective-permute-start = (bf16[2,4,2560]{2,1,0:T(4,128)(2,1)S(1)}, bf16[2,4,2560]{2,1,0:T(4,128)(2,1)S(1)}, u32[]{:S(2)}, u32[]{:S(2)}) collective-permute-start(bf16[2,4,2560]{2,1,0:T(4,128)(2,1)S(1)} %get-tuple-element.30), channel_id=1, source_target_pairs={{0,4},{4,8},{8,12},{12,0},{1,5},{5,9},{9,13},{13,1},{2,6},{6,10},{... | collective-permute-start | bytes 122888 | tf_op jit(solution)/shard_map/ppermute | solution.py:71
  4.8 2.5 %collective-permute-start.1 = (bf16[2,4,2560]{2,1,0:T(4,128)(2,1)S(1)}, bf16[2,4,2560]{2,1,0:T(4,128)(2,1)S(1)}, u32[]{:S(2)}, u32[]{:S(2)}) collective-permute-start(bf16[2,4,2560]{2,1,0:T(4,128)(2,1)S(1)} %get-tuple-element.31), channel_id=1, source_target_pairs={{0,8},{4,12},{8,0},{12,4},{1,9},{5,13},{9,1},{13,5},{2,10},{6,14},... | collective-permute-start | bytes 122888 | tf_op jit(solution)/shard_map/ppermute | solution.py:71
  7.2 1.4 %collective-permute-start.2 = (bf16[2,4,2560]{2,1,0:T(4,128)(2,1)S(1)}, bf16[2,4,2560]{2,1,0:T(4,128)(2,1)S(1)}, u32[]{:S(2)}, u32[]{:S(2)}) collective-permute-start(bf16[2,4,2560]{2,1,0:T(4,128)(2,1)S(1)} %get-tuple-element.32), channel_id=1, source_target_pairs={{0,12},{4,0},{8,4},{12,8},{1,13},{5,1},{9,5},{13,9},{2,14},{6,2},{... | collective-permute-start | bytes 122888 | tf_op jit(solution)/shard_map/ppermute | solution.py:71
  8.6 0.0 copy-start
  8.6 1.8 %make_tables.1 = (s32[4,32]{1,0:T(4,128)S(1)}, s32[1,16]{1,0:T(1,128)S(1)}, bf16[2,128,512]{2,1,0:T(8,128)(2,1)S(1)}, bf16[2,512,256]{2,1,0:T(8,128)(2,1)S(1)}, ...) custom-call(s32[4,32]{1,0:T(4,128)} %page_hbm.1, s32[1,16]{1,0:T(1,128)} %bitcast.3, ...), custom_call_target="tpu_custom_call" | custom-call | flops 1207959552 | bytes 2097152 | tf_op jit(solution)/shard_map/make_tables/pallas_call | solution.py:322
  10.4 0.0 collective-permute-done.refs_1_
  10.4 0.0 collective-permute-done.1.refs_2_
  10.4 0.8 %collective-permute-done.2.refs_3_ = bf16[2,4,2560]{2,1,0:T(4,128)(2,1)S(1)} collective-permute-done((bf16[2,4,2560]{2,1,0:T(4,128)(2,1)S(1)}, bf16[2,4,2560]{2,1,0:T(4,128)(2,1)S(1)}, u32[]{:S(2)}, u32[]{:S(2)}) %collective-permute-start.2) | collective-permute-done | bytes 40992 | tf_op jit(solution)/shard_map/ppermute | solution.py:71
  11.2 0.8 %decode_attention.1.after.refs_3_ = bf16[16,2048]{1,0:T(8,128)(2,1)S(1)} custom-call(f32[16,512]{1,0:T(8,128)S(1)} %get-tuple-element.28.seen, bf16[16,32]{1,0:T(8,128)(2,1)S(1)} %get-tuple-element.29.pick, bf16[2,128,512]{2,1,0:T(8,128)(2,1)S(1)} %get-tuple-element.26.keys, bf16[2,512,256]{2,1,0:T(8,128)(2,1)S(1)} %get-tuple-element.27.values, ...), custom_call_target="tpu_custom_call" | custom-call | tf_op jit(solution)/shard_map/decode_attention/pallas_call | solution.py:429
  12.1 0.4 %collective-permute-start.5 = (bf16[16,2048]{1,0:T(8,128)(2,1)S(1)}, bf16[16,2048]{1,0:T(8,128)(2,1)S(1)}, u32[]{:S(2)}, u32[]{:S(2)}) collective-permute-start(bf16[16,2048]{1,0:T(8,128)(2,1)S(1)} %decode_attention.1.after.refs_3_), channel_id=1, source_target_pairs={{0,4},{4,12},{8,0},{12,8},{1,5},{5,13},{9,1},{13,9},{2,6},{6,14},{... | collective-permute-start | bytes 196616 | tf_op jit(solution)/shard_map/ppermute | solution.py:71
  12.5 2.9 %collective-permute-start.4 = (bf16[16,2048]{1,0:T(8,128)(2,1)S(1)}, bf16[16,2048]{1,0:T(8,128)(2,1)S(1)}, u32[]{:S(2)}, u32[]{:S(2)}) collective-permute-start(bf16[16,2048]{1,0:T(8,128)(2,1)S(1)} %decode_attention.1.after.refs_3_), channel_id=1, source_target_pairs={{0,12},{4,8},{8,4},{12,0},{1,13},{5,9},{9,5},{13,1},{2,14},{6,10},... | collective-permute-start | bytes 196616 | tf_op jit(solution)/shard_map/ppermute | solution.py:71
  15.4 1.9 %collective-permute-start.3 = (bf16[16,2048]{1,0:T(8,128)(2,1)S(1)}, bf16[16,2048]{1,0:T(8,128)(2,1)S(1)}, u32[]{:S(2)}, u32[]{:S(2)}) collective-permute-start(bf16[16,2048]{1,0:T(8,128)(2,1)S(1)} %decode_attention.1.after.refs_3_), channel_id=1, source_target_pairs={{0,8},{4,0},{8,12},{12,4},{1,9},{5,1},{9,13},{13,5},{2,10},{6,2},{... | collective-permute-start | bytes 196616 | tf_op jit(solution)/shard_map/ppermute | solution.py:71
  17.3 2.5 %prefill_first.1 = (bf16[4,128,1024]{2,1,0:T(8,128)(2,1)S(1)}, bf16[4,128,1024]{2,1,0:T(8,128)(2,1)S(1)}, f32[4,128,384]{2,1,0:T(8,128)S(1)}, bf16[128,64]{1,0:T(8,128)(2,1)S(1)}) custom-call(s32[4,32]{1,0:T(4,128)S(1)} %get-tuple-element.23.page, s32[1,16]{1,0:T(1,128)S(1)} %get-tuple-element.24.owner, bf16[4,128,1024]{2,1,0:T(8,128)(2,1)S(1)} %get-tuple-element.25.q, ...), custom_call_target="tpu_custom_call" | custom-call | flops 1207959552 | bytes 2097152 | tf_op jit(solution)/shard_map/prefill_first/pallas_call | solution.py:347
  19.9 0.0 collective-permute-done.5.refs_2_
  19.9 0.0 collective-permute-done.4.refs_1_
  19.9 0.0 collective-permute-done.3.refs_0_
  19.9 0.0 copy-done
  19.9 0.7 %project_half.3 = bf16[64,1024]{1,0:T(8,128)(2,1)S(1)} custom-call(bf16[16,2048]{1,0:T(8,128)(2,1)S(1)} %collective-permute-done.3.refs_0_, bf16[16,2048]{1,0:T(8,128)(2,1)S(1)} %collective-permute-done.4.refs_1_, bf16[16,2048]{1,0:T(8,128)(2,1)S(1)} %collective-permute-done.5.refs_2_, bf16[16,2048]{1,0:T(8,128)(2,1)S(1)} %decode_attention.1.after.refs_3_, ...), custom_call_target="tpu_custom_call" | custom-call | flops 268435456 | bytes 4194304 | tf_op jit(solution)/shard_map/project_half/pallas_call | solution.py:452
  20.6 0.1 collective-permute-start.6
  20.7 0.7 %project_half.2 = f32[64,1024]{1,0:T(8,128)S(1)} custom-call(bf16[16,2048]{1,0:T(8,128)(2,1)S(1)} %collective-permute-done.3.refs_0_, bf16[16,2048]{1,0:T(8,128)(2,1)S(1)} %collective-permute-done.4.refs_1_, bf16[16,2048]{1,0:T(8,128)(2,1)S(1)} %collective-permute-done.5.refs_2_, bf16[16,2048]{1,0:T(8,128)(2,1)S(1)} %decode_attention.1.after.refs_3_, ...), custom_call_target="tpu_custom_call" | custom-call | flops 268435456 | bytes 4194304 | tf_op jit(solution)/shard_map/project_half/pallas_call | solution.py:452
  21.5 0.6 %collective-permute-done.6 = bf16[64,1024]{1,0:T(8,128)(2,1)S(1)} collective-permute-done((bf16[64,1024]{1,0:T(8,128)(2,1)S(1)}, bf16[64,1024]{1,0:T(8,128)(2,1)S(1)}, u32[]{:S(2)}, u32[]{:S(2)}) %collective-permute-start.6) | collective-permute-done | bytes 131104 | tf_op jit(solution)/shard_map/ppermute | solution.py:524
  22.1 1.6 %collective-permute-start.7 = (bf16[64,1024]{1,0:T(8,128)(2,1)S(1)}, bf16[64,1024]{1,0:T(8,128)(2,1)S(1)}, u32[]{:S(2)}, u32[]{:S(2)}) collective-permute-start(bf16[64,1024]{1,0:T(8,128)(2,1)S(1)} %get-tuple-element.42), channel_id=1, source_target_pairs={{0,2},{1,3},{2,0},{3,1},{4,6},{5,7},{6,4},{7,5},{8,10},{9,11},{10,... | collective-permute-start | bytes 393224 | tf_op jit(solution)/shard_map/ppermute | solution.py:524
  23.7 2.5 %prefill_second.1 = (bf16[512,2048]{1,0:T(8,128)(2,1)}, bf16[4,128,1024]{2,1,0:T(8,128)(2,1)S(1)}, f32[64,1024]{1,0:T(8,128)S(1)}) custom-call(bf16[4,128,1024]{2,1,0:T(8,128)(2,1)S(1)} %get-tuple-element.34.refs_5_.q, f32[4,128,384]{2,1,0:T(8,128)S(1)} %get-tuple-element.35.bias, ...), custom_call_target="tpu_custom_call", output_to_operand_aliasing={{2}: (5, {})} | custom-call | flops 1207959552 | bytes 2097152 | tf_op jit(solution)/shard_map/prefill_second/pallas_call | solution.py:365
  26.2 1.6 %collective-permute-done.7 = bf16[64,1024]{1,0:T(8,128)(2,1)S(1)} collective-permute-done((bf16[64,1024]{1,0:T(8,128)(2,1)S(1)}, bf16[64,1024]{1,0:T(8,128)(2,1)S(1)}, u32[]{:S(2)}, u32[]{:S(2)}) %collective-permute-start.7) | collective-permute-done | bytes 131104 | tf_op jit(solution)/shard_map/ppermute | solution.py:524
  27.7 0.1 collective-permute-start.8
  27.8 1.1 %spread_own.1 = (bf16[32,4,2048]{2,1,0:T(4,128)(2,1)}, bf16[512,2048]{1,0:T(8,128)(2,1)}) custom-call(bf16[128,64]{1,0:T(8,128)(2,1)S(1)} %get-tuple-element.33.spread, bf16[64,1024]{1,0:T(8,128)(2,1)S(1)} %add_convert_fusion.rows, bf16[4,128,1024]{2,1,0:T(8,128)(2,1)S(1)} %get-tuple-element.38.done_o, ...), custom_call_target="tpu_custom_call", output_to_operand_aliasing={{1}: (3, {})} | custom-call | tf_op jit(solution)/shard_map/spread_own/pallas_call | solution.py:484
  28.9 0.2 collective-permute-done.8.rows
  29.2 0.9 %spread_other.1 = bf16[32,4,2048]{2,1,0:T(4,128)(2,1)} custom-call(bf16[128,64]{1,0:T(8,128)(2,1)S(1)} %get-tuple-element.33.spread, bf16[64,1024]{1,0:T(8,128)(2,1)S(1)} %collective-permute-done.8.rows, bf16[32,4,2048]{2,1,0:T(4,128)(2,1)} %get-tuple-element.41.out_in), custom_call_target="tpu_custom_call", output_to_operand_aliasing={{}: (2, {})} | custom-call | tf_op jit(solution)/shard_map/spread_other/pallas_call | solution.py:510
  (2 shorter events, 0.1 us)
Async XLA Ops:
  1.6 8.8 %collective-permute-start = (bf16[2,4,2560]{2,1,0:T(4,128)(2,1)S(1)}, bf16[2,4,2560]{2,1,0:T(4,128)(2,1)S(1)}, u32[]{:S(2)}, u32[]{:S(2)}) collective-permute-start(bf16[2,4,2560]{2,1,0:T(4,128)(2,1)S(1)} %get-tuple-element.30), channel_id=1, source_target_pairs={{0,4},{4,8},{8,12},{12,0},{1,5},{5,9},{9,13},{13,1},{2,6},{6,10},{... | collective-permute-start | bytes 122888 | tf_op jit(solution)/shard_map/ppermute | solution.py:71
  4.8 5.6 %collective-permute-start.1 = (bf16[2,4,2560]{2,1,0:T(4,128)(2,1)S(1)}, bf16[2,4,2560]{2,1,0:T(4,128)(2,1)S(1)}, u32[]{:S(2)}, u32[]{:S(2)}) collective-permute-start(bf16[2,4,2560]{2,1,0:T(4,128)(2,1)S(1)} %get-tuple-element.31), channel_id=1, source_target_pairs={{0,8},{4,12},{8,0},{12,4},{1,9},{5,13},{9,1},{13,5},{2,10},{6,14},... | collective-permute-start | bytes 122888 | tf_op jit(solution)/shard_map/ppermute | solution.py:71
  7.2 4.0 %collective-permute-start.2 = (bf16[2,4,2560]{2,1,0:T(4,128)(2,1)S(1)}, bf16[2,4,2560]{2,1,0:T(4,128)(2,1)S(1)}, u32[]{:S(2)}, u32[]{:S(2)}) collective-permute-start(bf16[2,4,2560]{2,1,0:T(4,128)(2,1)S(1)} %get-tuple-element.32), channel_id=1, source_target_pairs={{0,12},{4,0},{8,4},{12,8},{1,13},{5,1},{9,5},{13,9},{2,14},{6,2},{... | collective-permute-start | bytes 122888 | tf_op jit(solution)/shard_map/ppermute | solution.py:71
  8.6 11.3 %copy-start = (bf16[2048,2048]{1,0:T(8,128)(2,1)S(1)}, bf16[2048,2048]{1,0:T(8,128)(2,1)}, u32[]{:S(2)}) copy-start(bf16[2048,2048]{1,0:T(8,128)(2,1)} %refs_4_.3) | copy-start | bytes 25165828
  12.1 7.8 %collective-permute-start.5 = (bf16[16,2048]{1,0:T(8,128)(2,1)S(1)}, bf16[16,2048]{1,0:T(8,128)(2,1)S(1)}, u32[]{:S(2)}, u32[]{:S(2)}) collective-permute-start(bf16[16,2048]{1,0:T(8,128)(2,1)S(1)} %decode_attention.1.after.refs_3_), channel_id=1, source_target_pairs={{0,4},{4,12},{8,0},{12,8},{1,5},{5,13},{9,1},{13,9},{2,6},{6,14},{... | collective-permute-start | bytes 196616 | tf_op jit(solution)/shard_map/ppermute | solution.py:71
  12.5 7.4 %collective-permute-start.4 = (bf16[16,2048]{1,0:T(8,128)(2,1)S(1)}, bf16[16,2048]{1,0:T(8,128)(2,1)S(1)}, u32[]{:S(2)}, u32[]{:S(2)}) collective-permute-start(bf16[16,2048]{1,0:T(8,128)(2,1)S(1)} %decode_attention.1.after.refs_3_), channel_id=1, source_target_pairs={{0,12},{4,8},{8,4},{12,0},{1,13},{5,9},{9,5},{13,1},{2,14},{6,10},... | collective-permute-start | bytes 196616 | tf_op jit(solution)/shard_map/ppermute | solution.py:71
  15.4 4.5 %collective-permute-start.3 = (bf16[16,2048]{1,0:T(8,128)(2,1)S(1)}, bf16[16,2048]{1,0:T(8,128)(2,1)S(1)}, u32[]{:S(2)}, u32[]{:S(2)}) collective-permute-start(bf16[16,2048]{1,0:T(8,128)(2,1)S(1)} %decode_attention.1.after.refs_3_), channel_id=1, source_target_pairs={{0,8},{4,0},{8,12},{12,4},{1,9},{5,1},{9,13},{13,5},{2,10},{6,2},{... | collective-permute-start | bytes 196616 | tf_op jit(solution)/shard_map/ppermute | solution.py:71
  20.6 1.4 %collective-permute-start.6 = (bf16[64,1024]{1,0:T(8,128)(2,1)S(1)}, bf16[64,1024]{1,0:T(8,128)(2,1)S(1)}, u32[]{:S(2)}, u32[]{:S(2)}) collective-permute-start(bf16[64,1024]{1,0:T(8,128)(2,1)S(1)} %project_half.3), channel_id=1, source_target_pairs={{0,1},{1,0},{2,3},{3,2},{4,5},{5,4},{6,7},{7,6},{8,9},{9,8},{10,11... | collective-permute-start | bytes 393224 | tf_op jit(solution)/shard_map/ppermute | solution.py:524
  22.1 5.6 %collective-permute-start.7 = (bf16[64,1024]{1,0:T(8,128)(2,1)S(1)}, bf16[64,1024]{1,0:T(8,128)(2,1)S(1)}, u32[]{:S(2)}, u32[]{:S(2)}) collective-permute-start(bf16[64,1024]{1,0:T(8,128)(2,1)S(1)} %get-tuple-element.42), channel_id=1, source_target_pairs={{0,2},{1,3},{2,0},{3,1},{4,6},{5,7},{6,4},{7,5},{8,10},{9,11},{10,... | collective-permute-start | bytes 393224 | tf_op jit(solution)/shard_map/ppermute | solution.py:524
  27.7 1.4 %collective-permute-start.8 = (bf16[64,1024]{1,0:T(8,128)(2,1)S(1)}, bf16[64,1024]{1,0:T(8,128)(2,1)S(1)}, u32[]{:S(2)}, u32[]{:S(2)}) collective-permute-start(bf16[64,1024]{1,0:T(8,128)(2,1)S(1)} %add_convert_fusion.rows), channel_id=1, source_target_pairs={{0,1},{1,0},{2,3},{3,2},{4,5},{5,4},{6,7},{7,6},{8,9},{9,8},{10,11... | collective-permute-start | bytes 393224 | tf_op jit(solution)/shard_map/ppermute | solution.py:524
